TPU v7x, 128 devices: a whole 4x4x4 slice. The times are simulated.
128 devices in a mesh: rows: 8 (over y, z_lo), cols: 16 (over x, z_hi, core).
Axes of the slice: x: 4, y: 4, z: 4 (z_hi: 2, z_lo: 2; z = z_hi * 2 + z_lo), core: 2. Of those that a mesh axis runs over, the one named last changes fastest.
Arguments:
- coarse: bfloat16 [16, 32, 128, 512], P('cols', 'rows'), may hold values from -35 to 35
- broad_entry_scale: float32 [512], replicated, may hold values from 0.1 to 1.9
- broad_entry_bias: float32 [512], replicated, may hold values from -2.5 to 2.5
- broad_entry_kernel: bfloat16 [3, 3, 512, 256], replicated, may hold values from -0.09375 to 0.09375
- broad_inner_scale: float32 [256], replicated, may hold values from 0.1 to 1.9
- broad_inner_bias: float32 [256], replicated, may hold values from -2.5 to 2.5
- broad_inner_kernel: bfloat16 [3, 3, 256, 256], replicated, may hold values from -0.125 to 0.125
- broad_skip_projection: bfloat16 [512, 256], replicated, may hold values from -0.25 to 0.25
- detail_entry_scale: float32 [256], replicated, may hold values from 0.1 to 1.9
- detail_entry_bias: float32 [256], replicated, may hold values from -2.5 to 2.5
- detail_entry_kernel: bfloat16 [3, 3, 256, 128], replicated, may hold values from -0.125 to 0.125
- detail_inner_scale: float32 [128], replicated, may hold values from 0.1 to 1.9
- detail_inner_bias: float32 [128], replicated, may hold values from -2.5 to 2.5
- detail_inner_kernel: bfloat16 [3, 3, 128, 128], replicated, may hold values from -0.1875 to 0.1875
- detail_skip_projection: bfloat16 [256, 128], replicated, may hold values from -0.375 to 0.375
Outputs:
- decoded: bfloat16 [16, 128, 512, 128], P(None, 'rows', 'cols')
All inputs are finite; a program needn't handle non-finite values.
Results may differ from a plain program's by a relative error of at most 0.007.
Values may be sent and summed in bfloat16 or wider, within the bound.
No kernel may reach another device: no remote copies, remote signals or barrier semaphores. Data moves between devices by JAX's collectives and lax.ppermute only.
A program may use at most 64 MiB of HBM per device.

v0:
```python
import jax
import jax.numpy as jnp
from jax import lax
from jax.sharding import PartitionSpec as P

GROUPS = 32


EPSILON = 1e-06


def with_halo(cells, sides, width):
    for axis, dim in sides:
        count = lax.axis_size(axis)
        ends = count - 1
        head = lax.slice_in_dim(cells, 0, width, axis=dim)
        tail = lax.slice_in_dim(cells, cells.shape[dim] - width, cells.shape[dim], axis=dim)
        cells = jnp.concatenate(
            [
                lax.ppermute(tail, axis, [(i, (i + 1) % count) for i in range(ends)]),
                cells,
                lax.ppermute(head, axis, [((i + 1) % count, i) for i in range(ends)]),
            ],
            axis=dim,
        )
    return cells


def enlarge_grid(value):
    return jnp.repeat(jnp.repeat(value, 2, axis=1), 2, axis=2)


def normalize(value, gain, shift):
    whole = value.astype(jnp.float32)
    count, height, width, chans = whole.shape
    grouped = whole.reshape(count, height, width, GROUPS, chans // GROUPS)
    entries = height * width * lax.axis_size("rows") * lax.axis_size("cols") * (chans // GROUPS)
    total = lax.psum(jnp.sum(grouped, axis=(1, 2, 4)), ("rows", "cols"))
    center = (total / entries).reshape(count, 1, 1, GROUPS, 1)
    square = lax.psum(jnp.sum((grouped - center) ** 2, axis=(1, 2, 4)), ("rows", "cols"))
    spread = (square / entries).reshape(count, 1, 1, GROUPS, 1)
    scaled = ((grouped - center) * lax.rsqrt(spread + EPSILON)).reshape(count, height, width, chans)
    scaled = scaled * gain + shift
    return jax.nn.silu(scaled).astype(jnp.bfloat16)


def convolve(padded, kernel):
    return lax.conv_general_dilated(
        padded,
        kernel,
        (1, 1),
        "VALID",
        dimension_numbers=("NHWC", "HWIO", "NHWC"),
        preferred_element_type=jnp.float32,
    )


def residual_unit(
    reduced_grid,
    entry_scale,
    entry_bias,
    entry_kernel,
    inner_scale,
    inner_bias,
    inner_kernel,
    skip_projection,
):
    input_pixels = enlarge_grid(reduced_grid)
    active = normalize(input_pixels, entry_scale, entry_bias)
    padded = with_halo(active, (("rows", 1), ("cols", 2)), 1)
    middle = convolve(padded, entry_kernel).astype(jnp.bfloat16)
    active_mid = normalize(middle, inner_scale, inner_bias)
    padded_mid = with_halo(active_mid, (("rows", 1), ("cols", 2)), 1)
    branch = convolve(padded_mid, inner_kernel)
    count, height, width, chans = input_pixels.shape
    direct = jnp.dot(
        input_pixels.reshape(-1, chans), skip_projection, preferred_element_type=jnp.float32
    )
    return (direct.reshape(count, height, width, -1) + branch).astype(jnp.bfloat16)


def body(
    coarse,
    broad_entry_scale,
    broad_entry_bias,
    broad_entry_kernel,
    broad_inner_scale,
    broad_inner_bias,
    broad_inner_kernel,
    broad_skip_projection,
    detail_entry_scale,
    detail_entry_bias,
    detail_entry_kernel,
    detail_inner_scale,
    detail_inner_bias,
    detail_inner_kernel,
    detail_skip_projection,
):
    blocks = lax.all_to_all(coarse, "cols", split_axis=2, concat_axis=0, tiled=True)
    broad_output = residual_unit(
        blocks,
        broad_entry_scale,
        broad_entry_bias,
        broad_entry_kernel,
        broad_inner_scale,
        broad_inner_bias,
        broad_inner_kernel,
        broad_skip_projection,
    )
    return residual_unit(
        broad_output,
        detail_entry_scale,
        detail_entry_bias,
        detail_entry_kernel,
        detail_inner_scale,
        detail_inner_bias,
        detail_inner_kernel,
        detail_skip_projection,
    )


def solution(mesh):
    return jax.shard_map(
        body,
        mesh=mesh,
        in_specs=(
            P("cols", "rows", None, None),
            P(),
            P(),
            P(),
            P(),
            P(),
            P(),
            P(),
            P(),
            P(),
            P(),
            P(),
            P(),
            P(),
            P(),
        ),
        out_specs=P(None, "rows", "cols", None),
        check_vma=False,
    )
```

profile of v0, /device:TPU:1, one launch (start us, length us, event | category | flops | bytes accessed | tf_op | source)
XLA Modules:
  0.0 705.6 jit_solution(464197705344058362)
XLA Ops:
  1.6 20.1 %all_to_all.18 = bf16[1,4,128,512]{3,1,0,2:T(4,128)(2,1)S(1)} all-to-all(bf16[1,4,128,512]{3,1,0,2:T(4,128)(2,1)S(1)} %copy.99), channel_id=1, replica_groups=mesh['rows'=8,'cols'=16] {'cols'}, dimensions={2} | all-to-all | bytes 1048576 | tf_op jit(solution)/shard_map/all_to_all | solution.py:99
  26.4 64.9 %psum.56 = f32[16,32]{1,0:T(8,128)S(1)} all-reduce(f32[16,32]{1,0:T(8,128)S(1)} %reduce_sum.97), channel_id=1, replica_groups=mesh['rows'=8,'cols'=16] {'rows','cols'}, use_global_device_ids=true, to_apply=%region_2.0 | all-reduce | flops 512 | bytes 4096 | tf_op jit(solution)/shard_map/psum | solution.py:38
  97.2 62.9 %psum.57 = f32[16,32]{1,0:T(8,128)S(1)} all-reduce(f32[16,32]{1,0:T(8,128)S(1)} %reduce_sum.100), channel_id=1, replica_groups=mesh['rows'=8,'cols'=16] {'rows','cols'}, use_global_device_ids=true, to_apply=%region_5.6 | all-reduce | flops 512 | bytes 4096 | tf_op jit(solution)/shard_map/psum | solution.py:40
  167.5 3.2 collective-permute-done
  170.8 4.0 collective-permute-done.1
  174.8 7.8 %collective-permute-start.2 = (bf16[16,10,1,512]{3,0,2,1:T(8,128)(2,1)S(1)}, bf16[16,10,1,512]{3,0,2,1:T(8,128)(2,1)S(1)}, u32[]{:S(2)}, u32[]{:S(2)}) collective-permute-start(bf16[16,10,1,512]{3,0,2,1:T(8,128)(2,1)S(1)} %get-tuple-element.9), channel_id=1, source_target_pairs={{0,1},{1,2},{2,3},{3,4},{4,5},{5,6},{6,7},{7,8},{8,9},{9,10},{10,1... | collective-permute-start | bytes 491528 | tf_op jit(solution)/shard_map/ppermute | solution.py:20
  184.8 5.9 collective-permute-done.3
  190.7 5.2 convert_reduce_fusion.1
  196.2 64.6 %psum.58 = f32[16,32]{1,0:T(8,128)S(1)} all-reduce(f32[16,32]{1,0:T(8,128)S(1)} %copy.104), channel_id=1, replica_groups=mesh['rows'=8,'cols'=16] {'rows','cols'}, use_global_device_ids=true, to_apply=%region_8.9 | all-reduce | flops 512 | bytes 4096 | tf_op jit(solution)/shard_map/psum | solution.py:38
  264.1 62.7 %psum.59 = f32[16,32]{1,0:T(8,128)S(1)} all-reduce(f32[16,32]{1,0:T(8,128)S(1)} %copy.108), channel_id=1, replica_groups=mesh['rows'=8,'cols'=16] {'rows','cols'}, use_global_device_ids=true, to_apply=%region_11.12 | all-reduce | flops 512 | bytes 4096 | tf_op jit(solution)/shard_map/psum | solution.py:40
  335.1 3.8 collective-permute-done.5
  339.0 6.4 collective-permute-start.6
  347.7 5.1 collective-permute-done.7
  355.6 3.4 fusion.55
  365.2 64.1 %psum.60 = f32[16,32]{1,0:T(8,128)S(1)} all-reduce(f32[16,32]{1,0:T(8,128)S(1)} %copy.115), channel_id=1, replica_groups=mesh['rows'=8,'cols'=16] {'rows','cols'}, use_global_device_ids=true, to_apply=%region_14.15 | all-reduce | flops 512 | bytes 4096 | tf_op jit(solution)/shard_map/psum | solution.py:38
  429.5 3.0 multiply_reduce_fusion
  432.7 63.2 %psum.61 = f32[16,32]{1,0:T(8,128)S(1)} all-reduce(f32[16,32]{1,0:T(8,128)S(1)} %copy.120), channel_id=1, replica_groups=mesh['rows'=8,'cols'=16] {'rows','cols'}, use_global_device_ids=true, to_apply=%region_17.18 | all-reduce | flops 512 | bytes 4096 | tf_op jit(solution)/shard_map/psum | solution.py:40
  498.1 3.0 multiply_convert_fusion
  505.3 3.4 collective-permute-done.8
  508.7 3.9 collective-permute-done.9
  512.6 7.6 %collective-permute-start.10 = (bf16[16,18,1,256]{3,0,2,1:T(8,128)(2,1)S(1)}, bf16[16,18,1,256]{3,0,2,1:T(8,128)(2,1)S(1)}, u32[]{:S(2)}, u32[]{:S(2)}) collective-permute-start(bf16[16,18,1,256]{3,0,2,1:T(8,128)(2,1)S(1)} %get-tuple-element.5), channel_id=1, source_target_pairs={{0,1},{1,2},{2,3},{3,4},{4,5},{5,6},{6,7},{7,8},{8,9},{9,10},{10,1... | collective-permute-start | bytes 442376 | tf_op jit(solution)/shard_map/ppermute | solution.py:20
  522.4 5.9 collective-permute-done.11
  528.3 11.2 %convert_reduce_fusion = (f32[16,128]{1,0:T(8,128)S(1)}, bf16[16,16,32,128]{3,0,2,1:T(8,128)(2,1)}) fusion(bf16[3,3,256,128]{3,2,1,0:T(8,128)(2,1)S(1)} %copy-done.16, bf16[16,18,1,256]{3,0,2,1:T(8,128)(2,1)S(1)} %collective-permute-done.11, bf16[16,1,32,256]{3,0,2,1:T(8,128)(2,1)S(1)} %collective-permute-done.9, ...), kind=kOutput, calls=%fused_computation.3 | convolution fusion | flops 4845008896 | bytes 7708672 | tf_op jit(solution)/shard_map/conv_general_dilated | solution.py:48
  539.7 64.6 %psum.62 = f32[16,32]{1,0:T(8,128)S(1)} all-reduce(f32[16,32]{1,0:T(8,128)S(1)} %copy.124), channel_id=1, replica_groups=mesh['rows'=8,'cols'=16] {'rows','cols'}, use_global_device_ids=true, to_apply=%region_20.21 | all-reduce | flops 512 | bytes 4096 | tf_op jit(solution)/shard_map/psum | solution.py:38
  606.9 62.9 %psum.63 = f32[16,32]{1,0:T(8,128)S(1)} all-reduce(f32[16,32]{1,0:T(8,128)S(1)} %copy.128), channel_id=1, replica_groups=mesh['rows'=8,'cols'=16] {'rows','cols'}, use_global_device_ids=true, to_apply=%region_23.24 | all-reduce | flops 512 | bytes 4096 | tf_op jit(solution)/shard_map/psum | solution.py:40
  669.9 3.1 fusion.20
  673.1 2.8 collective-permute-start.12
  677.8 3.8 collective-permute-done.13
  681.6 6.4 collective-permute-start.14
  690.1 5.2 collective-permute-done.15
  695.4 5.1 fusion.34
  700.5 5.0 fusion.21
  (131 shorter events, 60.5 us)
Async XLA Ops:
  0.0 190.7 %copy-start = (bf16[3,3,512,256]{3,2,1,0:T(8,128)(2,1)S(1)}, bf16[3,3,512,256]{3,2,1,0:T(8,128)(2,1)}, u32[]{:S(2)}) copy-start(bf16[3,3,512,256]{3,2,1,0:T(8,128)(2,1)} %param.18) | copy-start | bytes 7077892
  93.2 69.1 %copy-start.9 = (f32[512]{0:T(512)S(1)}, f32[512]{0:T(512)}, u32[]{:S(2)}) copy-start(f32[512]{0:T(512)} %param.17) | copy-start | bytes 6148
  93.2 69.1 %copy-start.10 = (f32[512]{0:T(512)S(1)}, f32[512]{0:T(512)}, u32[]{:S(2)}) copy-start(f32[512]{0:T(512)} %param.16) | copy-start | bytes 6148
  162.3 12.5 %copy-start.4 = (bf16[16,8,8,2,512]{4,0,3,2,1:T(8,128)(2,1)}, bf16[16,8,8,2,512]{4,0,3,2,1:T(8,128)(2,1)S(1)}, u32[]{:S(2)}) copy-start(bf16[16,8,8,2,512]{4,0,3,2,1:T(8,128)(2,1)S(1)} %broadcast_in_dim.25) | copy-start | bytes 6291460
  163.8 7.0 collective-permute-start
  166.2 8.5 %collective-permute-start.1 = (bf16[16,1,16,512]{3,0,2,1:T(8,128)(2,1)S(1)}, bf16[16,1,16,512]{3,0,2,1:T(8,128)(2,1)S(1)}, u32[]{:S(2)}, u32[]{:S(2)}) collective-permute-start(bf16[16,1,16,512]{3,0,2,1:T(8,128)(2,1)S(1)} %get-tuple-element.16), channel_id=1, source_target_pairs={{16,0},{32,16},{48,32},{64,48},{80,64},{96,80},{112,96},{17,1},{33... | collective-permute-start | bytes 786440 | tf_op jit(solution)/shard_map/ppermute | solution.py:22
  174.8 10.0 %collective-permute-start.2 = (bf16[16,10,1,512]{3,0,2,1:T(8,128)(2,1)S(1)}, bf16[16,10,1,512]{3,0,2,1:T(8,128)(2,1)S(1)}, u32[]{:S(2)}, u32[]{:S(2)}) collective-permute-start(bf16[16,10,1,512]{3,0,2,1:T(8,128)(2,1)S(1)} %get-tuple-element.9), channel_id=1, source_target_pairs={{0,1},{1,2},{2,3},{3,4},{4,5},{5,6},{6,7},{7,8},{8,9},{9,10},{10,1... | collective-permute-start | bytes 491528 | tf_op jit(solution)/shard_map/ppermute | solution.py:20
  182.6 8.1 %collective-permute-start.3 = (bf16[16,10,1,512]{3,0,2,1:T(8,128)(2,1)S(1)}, bf16[16,10,1,512]{3,0,2,1:T(8,128)(2,1)S(1)}, u32[]{:S(2)}, u32[]{:S(2)}) collective-permute-start(bf16[16,10,1,512]{3,0,2,1:T(8,128)(2,1)S(1)} %get-tuple-element.10), channel_id=1, source_target_pairs={{1,0},{2,1},{3,2},{4,3},{5,4},{6,5},{7,6},{8,7},{9,8},{10,9},{11,1... | collective-permute-start | bytes 491528 | tf_op jit(solution)/shard_map/ppermute | solution.py:22
  328.8 24.0 %copy-start.15 = (bf16[3,3,256,256]{3,2,1,0:T(8,128)(2,1)S(1)}, bf16[3,3,256,256]{3,2,1,0:T(8,128)(2,1)}, u32[]{:S(2)}) copy-start(bf16[3,3,256,256]{3,2,1,0:T(8,128)(2,1)} %param.21) | copy-start | bytes 3538948
  330.4 4.7 collective-permute-start.4
  333.2 5.7 collective-permute-start.5
  339.0 8.7 %collective-permute-start.6 = (bf16[16,10,1,256]{3,0,2,1:T(8,128)(2,1)S(1)}, bf16[16,10,1,256]{3,0,2,1:T(8,128)(2,1)S(1)}, u32[]{:S(2)}, u32[]{:S(2)}) collective-permute-start(bf16[16,10,1,256]{3,0,2,1:T(8,128)(2,1)S(1)} %get-tuple-element.17), channel_id=1, source_target_pairs={{0,1},{1,2},{2,3},{3,4},{4,5},{5,6},{6,7},{7,8},{8,9},{9,10},{10,1... | collective-permute-start | bytes 245768 | tf_op jit(solution)/shard_map/ppermute | solution.py:20
  345.4 10.1 %copy-start.5 = (bf16[16,8,8,2,512]{4,0,3,2,1:T(8,128)(2,1)S(1)}, bf16[16,8,8,2,512]{4,0,3,2,1:T(8,128)(2,1)}, u32[]{:S(2)}) copy-start(bf16[16,8,8,2,512]{4,0,3,2,1:T(8,128)(2,1)} %copy-done.4) | copy-start | bytes 6291460
  345.4 10.1 %copy-start.7 = (bf16[512,256]{1,0:T(8,128)(2,1)S(1)}, bf16[512,256]{1,0:T(8,128)(2,1)}, u32[]{:S(2)}) copy-start(bf16[512,256]{1,0:T(8,128)(2,1)} %param.22) | copy-start | bytes 786436
  345.4 7.4 %collective-permute-start.7 = (bf16[16,10,1,256]{3,0,2,1:T(8,128)(2,1)S(1)}, bf16[16,10,1,256]{3,0,2,1:T(8,128)(2,1)S(1)}, u32[]{:S(2)}, u32[]{:S(2)}) collective-permute-start(bf16[16,10,1,256]{3,0,2,1:T(8,128)(2,1)S(1)} %get-tuple-element.18), channel_id=1, source_target_pairs={{1,0},{2,1},{3,2},{4,3},{5,4},{6,5},{7,6},{8,7},{9,8},{10,9},{11,1... | collective-permute-start | bytes 245768 | tf_op jit(solution)/shard_map/ppermute | solution.py:22
  496.0 2.0 copy-start.11
  496.0 2.0 copy-start.12
  498.0 3.1 copy-start.1
  501.1 27.1 %copy-start.16 = (bf16[3,3,256,128]{3,2,1,0:T(8,128)(2,1)S(1)}, bf16[3,3,256,128]{3,2,1,0:T(8,128)(2,1)}, u32[]{:S(2)}) copy-start(bf16[3,3,256,128]{3,2,1,0:T(8,128)(2,1)} %param.25) | copy-start | bytes 1769476
  501.2 7.5 %collective-permute-start.8 = (bf16[16,1,32,256]{3,0,2,1:T(8,128)(2,1)S(1)}, bf16[16,1,32,256]{3,0,2,1:T(8,128)(2,1)S(1)}, u32[]{:S(2)}, u32[]{:S(2)}) collective-permute-start(bf16[16,1,32,256]{3,0,2,1:T(8,128)(2,1)S(1)} %get-tuple-element.7), channel_id=1, source_target_pairs={{0,16},{16,32},{32,48},{48,64},{64,80},{80,96},{96,112},{1,17},{17... | collective-permute-start | bytes 786440 | tf_op jit(solution)/shard_map/ppermute | solution.py:20
  504.0 8.7 %collective-permute-start.9 = (bf16[16,1,32,256]{3,0,2,1:T(8,128)(2,1)S(1)}, bf16[16,1,32,256]{3,0,2,1:T(8,128)(2,1)S(1)}, u32[]{:S(2)}, u32[]{:S(2)}) collective-permute-start(bf16[16,1,32,256]{3,0,2,1:T(8,128)(2,1)S(1)} %get-tuple-element.8), channel_id=1, source_target_pairs={{16,0},{32,16},{48,32},{64,48},{80,64},{96,80},{112,96},{17,1},{33... | collective-permute-start | bytes 786440 | tf_op jit(solution)/shard_map/ppermute | solution.py:22
  512.6 9.7 %collective-permute-start.10 = (bf16[16,18,1,256]{3,0,2,1:T(8,128)(2,1)S(1)}, bf16[16,18,1,256]{3,0,2,1:T(8,128)(2,1)S(1)}, u32[]{:S(2)}, u32[]{:S(2)}) collective-permute-start(bf16[16,18,1,256]{3,0,2,1:T(8,128)(2,1)S(1)} %get-tuple-element.5), channel_id=1, source_target_pairs={{0,1},{1,2},{2,3},{3,4},{4,5},{5,6},{6,7},{7,8},{8,9},{9,10},{10,1... | collective-permute-start | bytes 442376 | tf_op jit(solution)/shard_map/ppermute | solution.py:20
  520.3 149.6 %copy-start.13 = (f32[128]{0:T(128)S(1)}, f32[128]{0:T(128)}, u32[]{:S(2)}) copy-start(f32[128]{0:T(128)} %param.27) | copy-start | bytes 1540
  520.3 149.6 %copy-start.14 = (f32[128]{0:T(128)S(1)}, f32[128]{0:T(128)}, u32[]{:S(2)}) copy-start(f32[128]{0:T(128)} %param.26) | copy-start | bytes 1540
  520.3 8.0 %collective-permute-start.11 = (bf16[16,18,1,256]{3,0,2,1:T(8,128)(2,1)S(1)}, bf16[16,18,1,256]{3,0,2,1:T(8,128)(2,1)S(1)}, u32[]{:S(2)}, u32[]{:S(2)}) collective-permute-start(bf16[16,18,1,256]{3,0,2,1:T(8,128)(2,1)S(1)} %get-tuple-element.6), channel_id=1, source_target_pairs={{1,0},{2,1},{3,2},{4,3},{5,4},{6,5},{7,6},{8,7},{9,8},{10,9},{11,1... | collective-permute-start | bytes 442376 | tf_op jit(solution)/shard_map/ppermute | solution.py:22
  669.9 25.5 %copy-start.17 = (bf16[3,3,128,128]{3,2,1,0:T(8,128)(2,1)S(1)}, bf16[3,3,128,128]{3,2,1,0:T(8,128)(2,1)}, u32[]{:S(2)}) copy-start(bf16[3,3,128,128]{3,2,1,0:T(8,128)(2,1)} %param.28) | copy-start | bytes 884740
  673.1 4.7 collective-permute-start.12
  675.9 5.7 collective-permute-start.13
  681.6 8.5 %collective-permute-start.14 = (bf16[16,18,1,128]{3,0,2,1:T(8,128)(2,1)S(1)}, bf16[16,18,1,128]{3,0,2,1:T(8,128)(2,1)S(1)}, u32[]{:S(2)}, u32[]{:S(2)}) collective-permute-start(bf16[16,18,1,128]{3,0,2,1:T(8,128)(2,1)S(1)} %get-tuple-element.11), channel_id=1, source_target_pairs={{0,1},{1,2},{2,3},{3,4},{4,5},{5,6},{6,7},{7,8},{8,9},{9,10},{10,1... | collective-permute-start | bytes 221192 | tf_op jit(solution)/shard_map/ppermute | solution.py:20
  688.0 12.4 %copy-start.8 = (bf16[256,128]{1,0:T(8,128)(2,1)S(1)}, bf16[256,128]{1,0:T(8,128)(2,1)}, u32[]{:S(2)}) copy-start(bf16[256,128]{1,0:T(8,128)(2,1)} %param.29) | copy-start | bytes 196612
  688.0 7.3 %collective-permute-start.15 = (bf16[16,18,1,128]{3,0,2,1:T(8,128)(2,1)S(1)}, bf16[16,18,1,128]{3,0,2,1:T(8,128)(2,1)S(1)}, u32[]{:S(2)}, u32[]{:S(2)}) collective-permute-start(bf16[16,18,1,128]{3,0,2,1:T(8,128)(2,1)S(1)} %get-tuple-element.12), channel_id=1, source_target_pairs={{1,0},{2,1},{3,2},{4,3},{5,4},{6,5},{7,6},{8,7},{9,8},{10,9},{11,1... | collective-permute-start | bytes 221192 | tf_op jit(solution)/shard_map/ppermute | solution.py:22
  695.4 5.1 copy-start.2
  (2 other events, 3.3 us)
where the time goes:
time: 714 us; the launch traced here: 706 us
  blocking collectives  530 us (74%)
  starting transfers between devices  52.5 us (7%)
  waiting for transfers between devices  45.8 us (6%)
  matrix products  32.7 us (5%)
  other arithmetic  22.5 us (3%)
  local copies, waits for them, and re-layouts  21.5 us (3%)
    psum x4, blocking collectives, normalize(): total = lax.psum(jnp.sum(grouped, axis=(1, 2, 4)), ('rows', 'cols'))  258 us
    psum x4, blocking collectives, normalize(): lax.psum(jnp.sum((grouped - center) ** 2, axis=(1, 2, 4)), ('rows', 'cols'))  252 us
    ppermute x8, starting transfers between devices, with_halo(): lax.ppermute(tail, axis, [(i, (i + 1) % count) for i in range(ends)])  39 us
    ppermute x8, waiting for transfers between devices, with_halo(): lax.ppermute(head, axis, [((i + 1) % count, i) for i in range(ends)])  37.6 us
    conv_general_dilated x4, matrix products, convolve(): lax.conv_general_dilated(padded, kernel, (1, 1), 'VALID', dimension_numbe...  24.2 us
    all_to_all x1, blocking collectives, body(): lax.all_to_all(coarse, 'cols', split_axis=2, concat_axis=0, tiled=True)  20.1 us
  transfers between devices with their start and end apart: 16, of which 14 were waited for; matrix products, arithmetic and copies ran while one was open for 0% of the time, Pallas kernels for 0%

commit v1 on v0

v1 whole, which is shorter than its diff:
```python
import functools

import jax
import jax.numpy as jnp
from jax import lax
from jax.experimental import pallas as pl
from jax.experimental.pallas import tpu as pltpu
from jax.sharding import PartitionSpec as P

GROUPS = 32
EPSILON = 1e-06
F32 = jnp.float32
BF16 = jnp.bfloat16
ROWS = 8
COLS = 16
W = 128
VMEM_LIMIT = 48 * 1024 * 1024


def call(kernel, out_shape, scratch=(), flops=0, name=None):
    return pl.pallas_call(
        kernel,
        out_shape=out_shape,
        scratch_shapes=list(scratch),
        name=name,
        cost_estimate=pl.CostEstimate(flops=flops, bytes_accessed=0, transcendentals=0),
        compiler_params=pltpu.CompilerParams(vmem_limit_bytes=VMEM_LIMIT),
    )


def group_sum(v, size):
    count = v.shape[-1]
    lane = lax.broadcasted_iota(jnp.int32, v.shape, 1)
    step = 1
    while step < size:
        before = pltpu.roll(v, step, 1)
        after = pltpu.roll(v, count - step, 1)
        v = v + jnp.where((lane & step) != 0, before, after)
        step *= 2
    return v


def moments(parts, held):
    both = jnp.concatenate([parts[d] for d in range(ROWS)], axis=0)
    chans = both.shape[1] // 2
    size = chans // GROUPS
    sums, squares = both[:, :chans], both[:, chans:]
    entries = float(ROWS * held * size)
    total = jnp.broadcast_to(jnp.sum(sums, axis=0, keepdims=True), sums.shape)
    mean = group_sum(total, size) / entries
    off = sums / float(held) - mean
    spread = jnp.sum(squares + float(held) * off * off, axis=0, keepdims=True)
    spread = group_sum(jnp.broadcast_to(spread, sums.shape), size) / entries
    return mean, lax.rsqrt(spread + EPSILON)


def tile_lanes(v, times):
    return jnp.concatenate([v] * times, axis=1) if times > 1 else v


def active(value, mean, gain, shift):
    y = (value.astype(F32) - mean) * gain + shift
    half = 0.5 * y
    return half + half * jnp.tanh(half)


def block_moments(blocks):
    n = blocks[0].shape[0]
    sums, squares = [], []
    for block in blocks:
        s = jnp.sum(block, axis=0, keepdims=True)
        d = block - s / float(n)
        sums.append(s)
        squares.append(jnp.sum(d * d, axis=0, keepdims=True))
    return merge_moments(sums, squares, n)


def merge_moments(sums, squares, n):
    total = functools.reduce(jnp.add, sums)
    mean = total / float(n * len(sums))
    out = functools.reduce(jnp.add, squares)
    for s in sums:
        off = s / float(n) - mean
        out = out + float(n) * off * off
    return jnp.concatenate([total, out], axis=1)


def publish(ref, vector):
    for d in range(ROWS):
        ref[d] = vector


def next_col(v):
    col = lax.broadcasted_iota(jnp.int32, v.shape, 0) % W
    return jnp.where(col == W - 1, 0.0, pltpu.roll(v, v.shape[0] - 1, 0))


def last_col(v):
    col = lax.broadcasted_iota(jnp.int32, v.shape, 0) % W
    return jnp.where(col == 0, 0.0, pltpu.roll(v, 1, 0))


def edge_flags():
    row = lax.axis_index("rows")
    return row == 0, row == ROWS - 1


def mm(a, b):
    return jnp.dot(a, b, preferred_element_type=F32)


def coarse_stats_kernel(x_ref, out_ref):
    x = x_ref[...].astype(F32).reshape(4 * W, 512)
    publish(out_ref, block_moments([x]))


def pack_broad_kernel(k_ref, out_ref):
    rows = (((0,), (1, 2)), ((0, 1), (2,)))
    step = 128
    for a in range(2):
        for t in range(2):
            for c in range(0, 512, step):
                col = [
                    functools.reduce(
                        jnp.add, [k_ref[ky, kx, c : c + step, :].astype(F32) for ky in rows[a][t]]
                    )
                    for kx in range(3)
                ]
                for n, v in enumerate((col[0], col[1] + col[2], col[0] + col[1], col[2])):
                    out_ref[a, t * 512 + c : t * 512 + c + step, n * 256 : (n + 1) * 256] = v.astype(BF16)


def pack_detail_kernel(k_ref, x_ref, z_ref):
    rows = (((0,), (1, 2)), ((0, 1), (2,)))
    for a in range(2):
        for t in range(2):
            col = [
                functools.reduce(jnp.add, [k_ref[ky, kx].astype(F32) for ky in rows[a][t]])
                for kx in range(3)
            ]
            x_ref[a, t] = jnp.concatenate([col[0] + col[1], col[0]], axis=1).astype(BF16)
            z_ref[a, t] = jnp.concatenate([col[2], col[1] + col[2]], axis=1).astype(BF16)


def pack_inner_kernel(k_ref, main_ref, side_ref):
    zero = jnp.zeros((128, 128), BF16)
    for ky in range(3):
        k = [k_ref[ky, kx] for kx in range(3)]
        table = (
            (zero, zero, k[2], k[1]),
            (k[1], k[0], zero, zero),
            (k[2], k[1], k[0], zero),
            (zero, k[2], k[1], k[0]),
        )
        for i, line in enumerate(table):
            for o, v in enumerate(line):
                main_ref[ky * 512 + i * 128 : ky * 512 + (i + 1) * 128, o * 128 : (o + 1) * 128] = v
        base = ky * 256
        side_ref[base : base + 128, 0:128] = k[0]
        side_ref[base : base + 128, 128:256] = zero
        side_ref[base + 128 : base + 256, 0:128] = zero
        side_ref[base + 128 : base + 256, 128:256] = k[2]


def broad_entry_kernel_body(x_ref, up_ref, down_ref, parts_ref, gain_ref, shift_ref, w_ref, out_ref, stat_ref, an):
    first, last = edge_flags()
    mean, rate = moments(parts_ref, 4 * W)
    mean, gain, shift = mean[:1], rate[:1] * gain_ref[...], shift_ref[...]
    keep_up = jnp.where(first, 0.0, 1.0)
    keep_down = jnp.where(last, 0.0, 1.0)
    for h in range(2):
        an[h] = (active(up_ref[h], mean, gain, shift) * keep_up).astype(BF16)
        an[6 + h] = (active(down_ref[h], mean, gain, shift) * keep_down).astype(BF16)
    for h in range(4):
        an[2 + h] = active(x_ref[h], mean, gain, shift).astype(BF16)
    blocks = []
    for a in range(2):
        near = an[a : a + 6].reshape(6 * W, 512)
        far = an[a + 1 : a + 7].reshape(6 * W, 512)
        both = jnp.concatenate([near, far], axis=1)
        for b in range(2):
            z = [mm(both, w_ref[a, :, n * 256 : (n + 1) * 256]) for n in (2 * b, 2 * b + 1)]
            v = last_col(z[0]) + z[1] if b == 0 else z[0] + next_col(z[1])
            v = v.astype(BF16)
            for h in range(6):
                out_ref[2 * h + a, :, b * 256 : (b + 1) * 256] = v[h * W : (h + 1) * W]
            blocks.append(v[W : 5 * W].astype(F32))
    publish(stat_ref, block_moments(blocks))


def broad_inner_kernel_body(
    h_ref, x_ref, up_ref, down_ref, parts_ref, gain_ref, shift_ref, w_ref, p_ref, out_ref, stat_ref, an
):
    first, last = edge_flags()
    mean, rate = moments(parts_ref, 8 * 2 * W)
    mean, gain, shift = mean[:1], rate[:1] * gain_ref[...], shift_ref[...]
    mean, gain, shift = (tile_lanes(v, 2) for v in (mean, gain, shift))
    keep_up = jnp.where(first, 0.0, 1.0)
    keep_down = jnp.where(last, 0.0, 1.0)
    for i in range(12):
        v = active(h_ref[i], mean, gain, shift)
        if i < 2:
            v = v * keep_up
        elif i >= 10:
            v = v * keep_down
        an[i] = v.astype(BF16)
    skip_in = jnp.concatenate([up_ref[1]] + [x_ref[h] for h in range(4)] + [down_ref[0]], axis=0)
    skip = mm(skip_in, p_ref[...])
    w = w_ref
    even_w = jnp.concatenate([w[ky * 768 + 256 : ky * 768 + 768] for ky in range(3)], axis=0)
    odd_w = jnp.concatenate([w[ky * 768 : ky * 768 + 512] for ky in range(3)], axis=0)
    even_side = jnp.concatenate([w[ky * 768 : ky * 768 + 256] for ky in range(3)], axis=0)
    odd_side = jnp.concatenate([w[ky * 768 + 512 : ky * 768 + 768] for ky in range(3)], axis=0)
    evens, odds = [], []
    count = 5
    for j in range(0, 10, count):
        main = jnp.concatenate([an[j + ky : j + ky + count].reshape(count * W, 512) for ky in range(3)], axis=1)
        even_in = jnp.concatenate(
            [an[j + ky : j + ky + count, :, 0:256].reshape(count * W, 256) for ky in range(3)], axis=1
        )
        odd_in = jnp.concatenate(
            [an[j + ky : j + ky + count, :, 256:512].reshape(count * W, 256) for ky in range(3)], axis=1
        )
        extra = jnp.concatenate([skip[(i + 1) // 2 * W : ((i + 1) // 2 + 1) * W] for i in range(j, j + count)], axis=0)
        even = (mm(main, even_w) + last_col(mm(odd_in, even_side)) + extra).astype(BF16)
        odd = (mm(main, odd_w) + next_col(mm(even_in, odd_side)) + extra).astype(BF16)
        for i in range(count):
            out_ref[j + i, :, 0:256] = even[i * W : (i + 1) * W]
            out_ref[j + i, :, 256:512] = odd[i * W : (i + 1) * W]
        lo, hi = (W, count * W) if j == 0 else (0, (count - 1) * W)
        evens.append(even[lo:hi].astype(F32))
        odds.append(odd[lo:hi].astype(F32))
    publish(stat_ref, block_moments(evens + odds))


def detail_entry_kernel_body(x_ref, parts_ref, gain_ref, shift_ref, wx_ref, wz_ref, out_ref, stat_ref, an):
    first, last = edge_flags()
    mean, rate = moments(parts_ref, 8 * 2 * W)
    mean, gain, shift = mean[:1], rate[:1] * gain_ref[...], shift_ref[...]
    mean, gain, shift = (tile_lanes(v, 2) for v in (mean, gain, shift))
    keep_up = jnp.where(first, 0.0, 1.0)
    keep_down = jnp.where(last, 0.0, 1.0)
    for i in range(10):
        v = active(x_ref[i], mean, gain, shift)
        if i < 1:
            v = v * keep_up
        elif i >= 9:
            v = v * keep_down
        an[i] = v.astype(BF16)
    blocks = []
    for a in range(2):
        lhs = [an[t : t + 9].reshape(9 * W, 512) for t in range(2)]
        main = jnp.concatenate(lhs, axis=1)
        odd = jnp.concatenate([v[:, 256:512] for v in lhs], axis=1)
        even = jnp.concatenate([v[:, 0:256] for v in lhs], axis=1)
        wx = [wx_ref[a, t] for t in range(2)]
        wz = [wz_ref[a, t] for t in range(2)]
        middle = mm(main, jnp.concatenate([wx[0], wz[0], wx[1], wz[1]], axis=0))
        right = mm(odd, jnp.concatenate(wx, axis=0))
        left = mm(even, jnp.concatenate(wz, axis=0))
        q3 = (right[:, 0:128] + next_col(left[:, 0:128])).astype(BF16)
        q0 = (last_col(right[:, 128:256]) + left[:, 128:256]).astype(BF16)
        middle = middle.astype(BF16)
        for i in range(9):
            f = 2 * i + 1 - a
            out_ref[f, :, 0:128] = q3[i * W : (i + 1) * W]
            out_ref[f, :, 128:256] = q0[i * W : (i + 1) * W]
            out_ref[f, :, 256:512] = middle[i * W : (i + 1) * W]
        lo, hi = (W, 9 * W) if a == 1 else (0, 8 * W)
        for v in (q3, q0, middle[:, 0:128], middle[:, 128:256]):
            blocks.append(v[lo:hi].astype(F32))
    publish(stat_ref, block_moments(blocks))


def detail_inner_kernel_body(
    h_ref, x_ref, parts_ref, gain_ref, shift_ref, w_ref, side_ref, p_ref, out_ref, an, tmp
):
    first, last = edge_flags()
    mean, rate = moments(parts_ref, 16 * 4 * W)
    mean, gain, shift = mean[:1], rate[:1] * gain_ref[...], shift_ref[...]
    mean, gain, shift = (tile_lanes(v, 4) for v in (mean, gain, shift))
    keep_up = jnp.where(first, 0.0, 1.0)
    keep_down = jnp.where(last, 0.0, 1.0)
    for i in range(18):
        v = active(h_ref[i], mean, gain, shift)
        if i < 1:
            v = v * keep_up
        elif i >= 17:
            v = v * keep_down
        an[i] = v.astype(BF16)
    count = 4
    for f in range(0, 16, count):
        rows = [an[f + ky : f + ky + count].reshape(count * W, 512) for ky in range(3)]
        main = mm(jnp.concatenate(rows, axis=1), w_ref[...])
        side = mm(jnp.concatenate([v[:, 0:256] for v in rows], axis=1), side_ref[...])
        raw = x_ref[1 + f // 2 : 1 + f // 2 + count // 2].reshape(count // 2 * W, 512)
        skips = [mm(raw[:, 0:256], p_ref[...]), mm(raw[:, 256:512], p_ref[...])]
        skips = [
            jnp.concatenate([s[i // 2 * W : (i // 2 + 1) * W] for i in range(count)], axis=0) for s in skips
        ]
        cols = [main[:, o * 128 : (o + 1) * 128] + skips[o // 2] for o in range(4)]
        cols[0] = cols[0] + last_col(side[:, 0:128])
        cols[3] = cols[3] + next_col(side[:, 128:256])
        for i in range(count):
            for o in range(4):
                tmp[i, pl.ds(o, W, stride=4), :] = cols[o][i * W : (i + 1) * W]
            out_ref[:, f + i] = tmp[i].reshape(COLS, 32, 128).astype(BF16)


def swap(parts):
    return lax.all_to_all(parts, "rows", 0, 0, tiled=True)


def shape(*dims, dtype=BF16):
    return jax.ShapeDtypeStruct(dims, dtype)


def line(v):
    return v.reshape(1, -1)


def body(
    coarse,
    broad_entry_scale,
    broad_entry_bias,
    broad_entry_kernel,
    broad_inner_scale,
    broad_inner_bias,
    broad_inner_kernel,
    broad_skip_projection,
    detail_entry_scale,
    detail_entry_bias,
    detail_entry_kernel,
    detail_inner_scale,
    detail_inner_bias,
    detail_inner_kernel,
    detail_skip_projection,
):
    x = coarse.reshape(4, W, 512)
    up = lax.ppermute(x[2:], "rows", [(i, i + 1) for i in range(ROWS - 1)])
    down = lax.ppermute(x[:2], "rows", [(i + 1, i) for i in range(ROWS - 1)])
    stat = lambda c: shape(ROWS, 1, 2 * c, dtype=F32)
    parts = swap(call(coarse_stats_kernel, stat(512), name="coarse_stats")(x))
    packed = call(pack_broad_kernel, shape(2, 1024, 1024), name="pack_broad", flops=1 << 24)(broad_entry_kernel)
    wide_h, parts = call(
        broad_entry_kernel_body,
        (shape(12, W, 512), stat(256)),
        [pltpu.VMEM((8, W, 512), BF16)],
        name="broad_entry",
        flops=1 << 32,
    )(x, up, down, parts, line(broad_entry_scale), line(broad_entry_bias), packed)
    parts = swap(parts)
    wide_out, parts = call(
        broad_inner_kernel_body,
        (shape(10, W, 512), stat(256)),
        [pltpu.VMEM((12, W, 512), BF16)],
        name="broad_inner",
        flops=1 << 32,
    )(
        wide_h,
        x,
        up,
        down,
        parts,
        line(broad_inner_scale),
        line(broad_inner_bias),
        broad_inner_kernel.reshape(9 * 256, 256),
        broad_skip_projection,
    )
    parts = swap(parts)
    wx, wz = call(
        pack_detail_kernel, (shape(2, 2, 256, 256), shape(2, 2, 256, 256)), name="pack_detail", flops=1 << 22
    )(detail_entry_kernel)
    fine_h, parts = call(
        detail_entry_kernel_body,
        (shape(18, W, 512), stat(128)),
        [pltpu.VMEM((10, W, 512), BF16)],
        name="detail_entry",
        flops=1 << 32,
    )(wide_out, parts, line(detail_entry_scale), line(detail_entry_bias), wx, wz)
    parts = swap(parts)
    main, side = call(
        pack_inner_kernel, (shape(1536, 512), shape(768, 256)), name="pack_inner", flops=1 << 22
    )(detail_inner_kernel)
    decoded = call(
        detail_inner_kernel_body,
        shape(COLS, 16, 32, 128),
        [pltpu.VMEM((18, W, 512), BF16), pltpu.VMEM((4, 4 * W, 128), F32)],
        name="detail_inner",
        flops=1 << 32,
    )(
        fine_h,
        wide_out,
        parts,
        line(detail_inner_scale),
        line(detail_inner_bias),
        main,
        side,
        detail_skip_projection,
    )
    return lax.all_to_all(decoded, "cols", 0, 0, tiled=True)


def solution(mesh):
    return jax.shard_map(
        body,
        mesh=mesh,
        in_specs=(P("cols", "rows", None, None),) + (P(),) * 14,
        out_specs=P(None, "rows", "cols", None),
        check_vma=False,
    )
```

time: 714 us -> 117 us (0.16); the launches traced: 706 us -> 116 us
  blocking collectives: 530 us -> 50 us
  waiting for transfers between devices: 45.8 us -> 9.94 us
  starting transfers between devices: 52.5 us -> 18.5 us
  matrix products: 32.7 us -> 0 us
  Pallas kernels: 0 us -> 27.5 us
  other arithmetic: 22.5 us -> 0 us
  local copies, waits for them, and re-layouts: 21.5 us -> 10.2 us
    psum x8 -> x0, blocking collectives: 510 us -> none  [the longest x4 258 us: normalize(): total = lax.psum(jnp.sum(grouped, axis=(1, 2, 4)), ('rows', 'cols'))]
    ppermute x16 -> x2, starting transfers between devices: 52.5 us -> 5.68 us  [the longest x1 4.39 us: body(): up = lax.ppermute(x[2:], 'rows', [(i, i + 1) for i in range(ROWS - 1)])]
    ppermute x16 -> x2, waiting for transfers between devices: 45.8 us -> 0.01 us  [the longest x1 0.01 us: body(): down = lax.ppermute(x[:2], 'rows', [(i + 1, i) for i in range(ROWS - 1)])]
    all_to_all x1 -> x2, blocking collectives: 20.1 us -> 50 us  [the longest x1 40.6 us: body(): return lax.all_to_all(decoded, 'cols', 0, 0, tiled=True)]
    pallas_call x0 -> x8, Pallas kernels: none -> 27.5 us  [the longest x1 6.9 us: body(): call(detail_inner_kernel_body, shape(COLS, 16, 32, 128), [pltpu.VMEM((18,...]
    conv_general_dilated x4 -> x0, matrix products: 24.2 us -> none  [convolve(): lax.conv_general_dilated(padded, kernel, (1, 1), 'VALID', dimension_numbe...]
    all_to_all x0 -> x3, starting transfers between devices: none -> 12.8 us  [swap(): return lax.all_to_all(parts, 'rows', 0, 0, tiled=True)]
    reduce_sum x14 -> x0, other arithmetic: 12.3 us -> none  [the longest x8 9.94 us: normalize(): jnp.sum((grouped - center) ** 2, axis=(1, 2, 4))]
  transfers between devices with their start and end apart: 16 -> 5, of which waited for: 14 -> 3; matrix products, arithmetic and copies ran while one was open for 0% -> 0% of each run, Pallas kernels for 0% -> 3%
where the time goes in v1:
time: 117 us; the launch traced here: 116 us
  blocking collectives  50 us (43%)
  Pallas kernels  27.5 us (24%)
  starting transfers between devices  18.5 us (16%)
  local copies, waits for them, and re-layouts  10.2 us (9%)
  waiting for transfers between devices  9.94 us (8%)
    all_to_all x1, blocking collectives, body(): return lax.all_to_all(decoded, 'cols', 0, 0, tiled=True)  40.6 us
    all_to_all x3, starting transfers between devices, swap(): return lax.all_to_all(parts, 'rows', 0, 0, tiled=True)  12.8 us
    all_to_all x3, waiting for transfers between devices, swap(): return lax.all_to_all(parts, 'rows', 0, 0, tiled=True)  9.93 us
    all_to_all x1, blocking collectives, swap(): return lax.all_to_all(parts, 'rows', 0, 0, tiled=True)  9.32 us
    unnamed x41, local copies, waits for them, and re-layouts  9.18 us
    pallas_call x1, Pallas kernels, body(): call(detail_inner_kernel_body, shape(COLS, 16, 32, 128), [pltpu.VMEM((18,...  6.9 us
    pallas_call x1, Pallas kernels, body(): call(broad_entry_kernel_body, (shape(12, W, 512), stat(256)), [pltpu.VMEM...  6.67 us
    pallas_call x1, Pallas kernels, body(): call(broad_inner_kernel_body, (shape(10, W, 512), stat(256)), [pltpu.VMEM...  4.98 us
  transfers between devices with their start and end apart: 5, of which 3 were waited for; matrix products, arithmetic and copies ran while one was open for 0% of the time, Pallas kernels for 3%

profile of v1, /device:TPU:1, one launch (start us, length us, event | category | flops | bytes accessed | tf_op | source)
XLA Modules:
  0.0 116.3 jit_solution(11626727196467165106)
XLA Ops:
  0.0 1.1 slice_bitcast_fusion
  1.1 4.4 %collective-permute-start = (bf16[2,128,512]{2,1,0:T(8,128)(2,1)S(1)}, bf16[2,128,512]{2,1,0:T(8,128)(2,1)S(1)}, u32[]{:S(2)}, u32[]{:S(2)}) collective-permute-start(bf16[2,128,512]{2,1,0:T(8,128)(2,1)S(1)} %get-tuple-element.26), channel_id=1, source_target_pairs={{0,16},{16,32},{32,48},{48,64},{64,80},{80,96},{96,112},{1,17},{17... | collective-permute-start | bytes 786440 | tf_op jit(solution)/shard_map/ppermute | solution.py:340
  5.5 1.3 %collective-permute-start.1 = (bf16[2,128,512]{2,1,0:T(8,128)(2,1)S(1)}, bf16[2,128,512]{2,1,0:T(8,128)(2,1)S(1)}, u32[]{:S(2)}, u32[]{:S(2)}) collective-permute-start(bf16[2,128,512]{2,1,0:T(8,128)(2,1)S(1)} %get-tuple-element.25), channel_id=1, source_target_pairs={{16,0},{32,16},{48,32},{64,48},{80,64},{96,80},{112,96},{17,1},{33... | collective-permute-start | bytes 786440 | tf_op jit(solution)/shard_map/ppermute | solution.py:341
  6.8 0.0 copy-start.1
  6.8 1.0 copy-done.1
  7.8 0.9 coarse_stats.1
  8.7 6.0 %all-to-all-start = ((f32[8,1,1024]{2,1,0:T(1,128)}), f32[8,1,1024]{2,1,0:T(1,128)S(1)}, u32[]{:S(2)}, u32[]{:S(2)}) async-start(f32[8,1,1024]{2,1,0:T(1,128)} %coarse_stats.1), calls=%async_computation | async-start | bytes 65536 | tf_op jit(solution)/shard_map/all_to_all | solution.py:311
  14.7 1.7 %copy-done = bf16[3,3,512,256]{3,2,1,0:T(8,128)(2,1)S(1)} copy-done((bf16[3,3,512,256]{3,2,1,0:T(8,128)(2,1)S(1)}, bf16[3,3,512,256]{3,2,1,0:T(8,128)(2,1)}, u32[]{:S(2)}) %copy-start) | copy-done | bytes 2359320
  16.3 2.7 %pack_broad.1.w_ref = bf16[2,1024,1024]{2,1,0:T(8,128)(2,1)} custom-call(bf16[3,3,512,256]{3,2,1,0:T(8,128)(2,1)S(1)} %copy-done), custom_call_target="tpu_custom_call" | custom-call | flops 16777216 | tf_op jit(solution)/shard_map/pack_broad/pallas_call | solution.py:344
  19.1 0.7 all-to-all-done.parts_ref
  19.8 0.0 copy-start.6
  19.8 0.0 copy-start.10
  19.8 6.7 %broad_entry.1 = (bf16[12,128,512]{2,1,0:T(8,128)(2,1)S(1)}, f32[8,1,512]{2,1,0:T(1,128)S(1)}) custom-call(bf16[4,128,512]{2,1,0:T(8,128)(2,1)S(1)} %bitcast.15, bf16[2,128,512]{2,1,0:T(8,128)(2,1)S(1)} %collective-permute-done.up_ref, bf16[2,128,512]{2,1,0:T(8,128)(2,1)S(1)} %collective-permute-done.1.down_ref, f32[8,1,1024]{2,1,0:T(1,128)S(1)} %all-to-all-done.parts_ref, ...), custom_call_target="tpu_custom_call" | custom-call | flops 4294967296 | tf_op jit(solution)/shard_map/broad_entry/pallas_call | solution.py:345
  26.5 9.3 %all_to_all.25.parts_ref = f32[8,1,512]{2,1,0:T(1,128)S(1)} all-to-all(f32[8,1,512]{2,1,0:T(1,128)S(1)} %get-tuple-element.16), channel_id=1, replica_groups=mesh['rows'=8,'cols'=16] {'rows'}, dimensions={0} | all-to-all | bytes 32768 | tf_op jit(solution)/shard_map/all_to_all | solution.py:311
  35.8 0.0 copy-start.3
  35.9 0.0 copy-start.12
  35.9 5.0 %broad_inner.1 = (bf16[10,128,512]{2,1,0:T(8,128)(2,1)S(1)}, f32[8,1,512]{2,1,0:T(1,128)}) custom-call(bf16[12,128,512]{2,1,0:T(8,128)(2,1)S(1)} %get-tuple-element.15.h_ref, bf16[4,128,512]{2,1,0:T(8,128)(2,1)S(1)} %bitcast.16, bf16[2,128,512]{2,1,0:T(8,128)(2,1)S(1)} %collective-permute-done.up_ref, ...), custom_call_target="tpu_custom_call" | custom-call | flops 4294967296 | tf_op jit(solution)/shard_map/broad_inner/pallas_call | solution.py:353
  40.9 1.1 copy-done.17
  41.9 3.5 %all-to-all-start.2 = ((f32[8,1,512]{2,1,0:T(1,128)}), f32[8,1,512]{2,1,0:T(1,128)S(1)}, u32[]{:S(2)}, u32[]{:S(2)}) async-start(f32[8,1,512]{2,1,0:T(1,128)} %get-tuple-element.18), calls=%async_computation.2 | async-start | bytes 32768 | tf_op jit(solution)/shard_map/all_to_all | solution.py:311
  45.4 0.2 pack_detail.1
  45.6 4.6 %all-to-all-done.2.parts_ref = f32[8,1,512]{2,1,0:T(1,128)S(1)} async-done(((f32[8,1,512]{2,1,0:T(1,128)}), f32[8,1,512]{2,1,0:T(1,128)S(1)}, u32[]{:S(2)}, u32[]{:S(2)}) %all-to-all-start.2) | async-done | bytes 16416 | tf_op jit(solution)/shard_map/all_to_all | solution.py:311
  50.2 1.3 %copy-done.18 = bf16[10,128,512]{2,1,0:T(8,128)(2,1)S(1)} copy-done((bf16[10,128,512]{2,1,0:T(8,128)(2,1)S(1)}, bf16[10,128,512]{2,1,0:T(8,128)(2,1)}, u32[]{:S(2)}) %copy-start.18) | copy-done | bytes 1310744
  51.5 4.9 %detail_entry.1 = (bf16[18,128,512]{2,1,0:T(8,128)(2,1)S(1)}, f32[8,1,256]{2,1,0:T(1,128)}) custom-call(bf16[10,128,512]{2,1,0:T(8,128)(2,1)S(1)} %copy-done.18, f32[8,1,512]{2,1,0:T(1,128)S(1)} %all-to-all-done.2.parts_ref, f32[1,256]{1,0:T(1,128)S(1)} %bitcast.22, f32[1,256]{1,0:T(1,128)S(1)} %bitcast.23, ...), custom_call_target="tpu_custom_call" | custom-call | flops 4294967296 | tf_op jit(solution)/shard_map/detail_entry/pallas_call | solution.py:374
  56.4 1.4 %copy-done.16 = bf16[18,128,512]{2,1,0:T(8,128)(2,1)} copy-done((bf16[18,128,512]{2,1,0:T(8,128)(2,1)}, bf16[18,128,512]{2,1,0:T(8,128)(2,1)S(1)}, u32[]{:S(2)}) %copy-start.16) | copy-done | bytes 2359320
  57.8 3.3 %all-to-all-start.3 = ((f32[8,1,256]{2,1,0:T(1,128)}), f32[8,1,256]{2,1,0:T(1,128)S(1)}, u32[]{:S(2)}, u32[]{:S(2)}) async-start(f32[8,1,256]{2,1,0:T(1,128)} %get-tuple-element.22), calls=%async_computation.3 | async-start | bytes 16384 | tf_op jit(solution)/shard_map/all_to_all | solution.py:311
  61.2 0.3 pack_inner.1
  61.4 4.7 %all-to-all-done.3.parts_ref = f32[8,1,256]{2,1,0:T(1,128)S(1)} async-done(((f32[8,1,256]{2,1,0:T(1,128)}), f32[8,1,256]{2,1,0:T(1,128)S(1)}, u32[]{:S(2)}, u32[]{:S(2)}) %all-to-all-start.3) | async-done | bytes 8224 | tf_op jit(solution)/shard_map/all_to_all | solution.py:311
  66.1 0.0 copy-start.19
  66.1 1.3 %copy-done.19 = bf16[10,128,512]{2,1,0:T(8,128)(2,1)S(1)} copy-done((bf16[10,128,512]{2,1,0:T(8,128)(2,1)S(1)}, bf16[10,128,512]{2,1,0:T(8,128)(2,1)}, u32[]{:S(2)}) %copy-start.19) | copy-done | bytes 1310744
  67.4 6.9 %detail_inner.1 = bf16[16,16,32,128]{3,2,1,0:T(8,128)(2,1)S(1)} custom-call(bf16[18,128,512]{2,1,0:T(8,128)(2,1)} %copy-done.16, bf16[10,128,512]{2,1,0:T(8,128)(2,1)S(1)} %copy-done.19, f32[8,1,256]{2,1,0:T(1,128)S(1)} %all-to-all-done.3.parts_ref, f32[1,128]{1,0:T(1,128)S(1)} %bitcast.24, f32[1,128]{1,0:T(1,128)S(1)} %bitcast.25, ...), custom_call_target="tpu_custom_call" | custom-call | flops 4294967296 | tf_op jit(solution)/shard_map/detail_inner/pallas_call | solution.py:385
  74.3 40.6 %all_to_all.26 = bf16[16,16,32,128]{3,2,1,0:T(8,128)(2,1)S(1)} all-to-all(bf16[16,16,32,128]{3,2,1,0:T(8,128)(2,1)S(1)} %detail_inner.1), channel_id=1, replica_groups=mesh['rows'=8,'cols'=16] {'cols'}, dimensions={0} | all-to-all | bytes 4194304 | tf_op jit(solution)/shard_map/all_to_all | solution.py:401
  115.0 1.3 %copy.17 = bf16[16,16,32,128]{3,2,1,0:T(8,128)(2,1)} copy(bf16[16,16,32,128]{3,2,1,0:T(8,128)(2,1)S(1)} %all_to_all.26) | data formatting | bytes 4194304
  (30 shorter events, 0.1 us)
Async XLA Ops:
  1.1 18.7 %collective-permute-start = (bf16[2,128,512]{2,1,0:T(8,128)(2,1)S(1)}, bf16[2,128,512]{2,1,0:T(8,128)(2,1)S(1)}, u32[]{:S(2)}, u32[]{:S(2)}) collective-permute-start(bf16[2,128,512]{2,1,0:T(8,128)(2,1)S(1)} %get-tuple-element.26), channel_id=1, source_target_pairs={{0,16},{16,32},{32,48},{48,64},{64,80},{80,96},{96,112},{1,17},{17... | collective-permute-start | bytes 786440 | tf_op jit(solution)/shard_map/ppermute | solution.py:340
  5.5 14.3 %collective-permute-start.1 = (bf16[2,128,512]{2,1,0:T(8,128)(2,1)S(1)}, bf16[2,128,512]{2,1,0:T(8,128)(2,1)S(1)}, u32[]{:S(2)}, u32[]{:S(2)}) collective-permute-start(bf16[2,128,512]{2,1,0:T(8,128)(2,1)S(1)} %get-tuple-element.25), channel_id=1, source_target_pairs={{16,0},{32,16},{48,32},{64,48},{80,64},{96,80},{112,96},{17,1},{33... | collective-permute-start | bytes 786440 | tf_op jit(solution)/shard_map/ppermute | solution.py:341
  6.8 1.0 copy-start.1
  8.7 11.0 %all-to-all-start = ((f32[8,1,1024]{2,1,0:T(1,128)}), f32[8,1,1024]{2,1,0:T(1,128)S(1)}, u32[]{:S(2)}, u32[]{:S(2)}) async-start(f32[8,1,1024]{2,1,0:T(1,128)} %coarse_stats.1), calls=%async_computation | async-start | bytes 65536 | tf_op jit(solution)/shard_map/all_to_all | solution.py:311
  14.7 1.7 %copy-start = (bf16[3,3,512,256]{3,2,1,0:T(8,128)(2,1)S(1)}, bf16[3,3,512,256]{3,2,1,0:T(8,128)(2,1)}, u32[]{:S(2)}) copy-start(bf16[3,3,512,256]{3,2,1,0:T(8,128)(2,1)} %k_ref.3) | copy-start | bytes 7077892
  16.3 3.4 %copy-start.2 = (bf16[1,4,128,512]{3,2,1,0:T(8,128)(2,1)S(1)}, bf16[1,4,128,512]{3,2,1,0:T(8,128)(2,1)}, u32[]{:S(2)}) copy-start(bf16[1,4,128,512]{3,2,1,0:T(8,128)(2,1)} %param.15) | copy-start | bytes 1572868
  16.3 3.4 %copy-start.8 = (f32[512]{0:T(512)S(1)}, f32[512]{0:T(512)}, u32[]{:S(2)}) copy-start(f32[512]{0:T(512)} %param.16) | copy-start | bytes 6148
  16.3 3.4 %copy-start.9 = (f32[512]{0:T(512)S(1)}, f32[512]{0:T(512)}, u32[]{:S(2)}) copy-start(f32[512]{0:T(512)} %param.17) | copy-start | bytes 6148
  19.8 16.0 %copy-start.5 = (bf16[3,3,256,256]{3,2,1,0:T(8,128)(2,1)S(1)}, bf16[3,3,256,256]{3,2,1,0:T(8,128)(2,1)}, u32[]{:S(2)}) copy-start(bf16[3,3,256,256]{3,2,1,0:T(8,128)(2,1)} %param.21) | copy-start | bytes 3538948
  19.8 16.0 %copy-start.6 = (bf16[512,256]{1,0:T(8,128)(2,1)S(1)}, bf16[512,256]{1,0:T(8,128)(2,1)}, u32[]{:S(2)}) copy-start(bf16[512,256]{1,0:T(8,128)(2,1)} %p_ref.2) | copy-start | bytes 786436
  19.8 16.0 %copy-start.10 = (f32[256]{0:T(256)S(1)}, f32[256]{0:T(256)}, u32[]{:S(2)}) copy-start(f32[256]{0:T(256)} %param.19) | copy-start | bytes 3076
  19.8 16.0 %copy-start.11 = (f32[256]{0:T(256)S(1)}, f32[256]{0:T(256)}, u32[]{:S(2)}) copy-start(f32[256]{0:T(256)} %param.20) | copy-start | bytes 3076
  35.8 9.6 %copy-start.3 = (bf16[3,3,256,128]{3,2,1,0:T(8,128)(2,1)S(1)}, bf16[3,3,256,128]{3,2,1,0:T(8,128)(2,1)}, u32[]{:S(2)}) copy-start(bf16[3,3,256,128]{3,2,1,0:T(8,128)(2,1)} %k_ref.4) | copy-start | bytes 1769476
  35.9 14.4 %copy-start.12 = (f32[256]{0:T(256)S(1)}, f32[256]{0:T(256)}, u32[]{:S(2)}) copy-start(f32[256]{0:T(256)} %param.23) | copy-start | bytes 3076
  35.9 14.3 %copy-start.13 = (f32[256]{0:T(256)S(1)}, f32[256]{0:T(256)}, u32[]{:S(2)}) copy-start(f32[256]{0:T(256)} %param.24) | copy-start | bytes 3076
  40.9 1.1 copy-start.17
  41.9 8.3 %all-to-all-start.2 = ((f32[8,1,512]{2,1,0:T(1,128)}), f32[8,1,512]{2,1,0:T(1,128)S(1)}, u32[]{:S(2)}, u32[]{:S(2)}) async-start(f32[8,1,512]{2,1,0:T(1,128)} %get-tuple-element.18), calls=%async_computation.2 | async-start | bytes 32768 | tf_op jit(solution)/shard_map/all_to_all | solution.py:311
  50.2 1.3 %copy-start.18 = (bf16[10,128,512]{2,1,0:T(8,128)(2,1)S(1)}, bf16[10,128,512]{2,1,0:T(8,128)(2,1)}, u32[]{:S(2)}) copy-start(bf16[10,128,512]{2,1,0:T(8,128)(2,1)} %copy-done.17) | copy-start | bytes 3932164
  51.5 9.6 %copy-start.4 = (bf16[3,3,128,128]{3,2,1,0:T(8,128)(2,1)S(1)}, bf16[3,3,128,128]{3,2,1,0:T(8,128)(2,1)}, u32[]{:S(2)}) copy-start(bf16[3,3,128,128]{3,2,1,0:T(8,128)(2,1)} %k_ref.5) | copy-start | bytes 884740
  51.5 14.6 %copy-start.7 = (bf16[256,128]{1,0:T(8,128)(2,1)S(1)}, bf16[256,128]{1,0:T(8,128)(2,1)}, u32[]{:S(2)}) copy-start(bf16[256,128]{1,0:T(8,128)(2,1)} %p_ref.3) | copy-start | bytes 196612
  51.5 14.6 %copy-start.14 = (f32[128]{0:T(128)S(1)}, f32[128]{0:T(128)}, u32[]{:S(2)}) copy-start(f32[128]{0:T(128)} %param.26) | copy-start | bytes 1540
  51.5 14.6 %copy-start.15 = (f32[128]{0:T(128)S(1)}, f32[128]{0:T(128)}, u32[]{:S(2)}) copy-start(f32[128]{0:T(128)} %param.27) | copy-start | bytes 1540
  56.4 1.4 %copy-start.16 = (bf16[18,128,512]{2,1,0:T(8,128)(2,1)}, bf16[18,128,512]{2,1,0:T(8,128)(2,1)S(1)}, u32[]{:S(2)}) copy-start(bf16[18,128,512]{2,1,0:T(8,128)(2,1)S(1)} %get-tuple-element.21.h_ref) | copy-start | bytes 7077892
  57.8 8.3 %all-to-all-start.3 = ((f32[8,1,256]{2,1,0:T(1,128)}), f32[8,1,256]{2,1,0:T(1,128)S(1)}, u32[]{:S(2)}, u32[]{:S(2)}) async-start(f32[8,1,256]{2,1,0:T(1,128)} %get-tuple-element.22), calls=%async_computation.3 | async-start | bytes 16384 | tf_op jit(solution)/shard_map/all_to_all | solution.py:311
  66.1 1.3 %copy-start.19 = (bf16[10,128,512]{2,1,0:T(8,128)(2,1)S(1)}, bf16[10,128,512]{2,1,0:T(8,128)(2,1)}, u32[]{:S(2)}) copy-start(bf16[10,128,512]{2,1,0:T(8,128)(2,1)} %copy-done.17) | copy-start | bytes 3932164

commit v2 on v1

--- a/solution.py
+++ b/solution.py
@@ -14,7 +14,7 @@
 ROWS = 8
 COLS = 16
 W = 128
-VMEM_LIMIT = 48 * 1024 * 1024
+VMEM_LIMIT = 24 * 1024 * 1024
 
 
 def call(kernel, out_shape, scratch=(), flops=0, name=None):
@@ -109,12 +109,14 @@
     return jnp.dot(a, b, preferred_element_type=F32)
 
 
-def coarse_stats_kernel(x_ref, out_ref):
+def coarse_stats_kernel(x_ref, out_ref, head_ref, tail_ref):
     x = x_ref[...].astype(F32).reshape(4 * W, 512)
+    head_ref[...] = x_ref[0:2]
+    tail_ref[...] = x_ref[2:4]
     publish(out_ref, block_moments([x]))
 
 
-def pack_broad_kernel(k_ref, out_ref):
+def pack_broad(k_ref, out_ref):
     rows = (((0,), (1, 2)), ((0, 1), (2,)))
     step = 128
     for a in range(2):
@@ -130,7 +132,7 @@
                     out_ref[a, t * 512 + c : t * 512 + c + step, n * 256 : (n + 1) * 256] = v.astype(BF16)
 
 
-def pack_detail_kernel(k_ref, x_ref, z_ref):
+def pack_detail(k_ref, x_ref, z_ref):
     rows = (((0,), (1, 2)), ((0, 1), (2,)))
     for a in range(2):
         for t in range(2):
@@ -142,7 +144,7 @@
             z_ref[a, t] = jnp.concatenate([col[2], col[1] + col[2]], axis=1).astype(BF16)
 
 
-def pack_inner_kernel(k_ref, main_ref, side_ref):
+def pack_inner(k_ref, main_ref, side_ref):
     zero = jnp.zeros((128, 128), BF16)
     for ky in range(3):
         k = [k_ref[ky, kx] for kx in range(3)]
@@ -162,7 +164,8 @@
         side_ref[base + 128 : base + 256, 128:256] = k[2]
 
 
-def broad_entry_kernel_body(x_ref, up_ref, down_ref, parts_ref, gain_ref, shift_ref, w_ref, out_ref, stat_ref, an):
+def broad_entry_kernel_body(x_ref, up_ref, down_ref, parts_ref, gain_ref, shift_ref, k_ref, out_ref, stat_ref, an, w_ref):
+    pack_broad(k_ref, w_ref)
     first, last = edge_flags()
     mean, rate = moments(parts_ref, 4 * W)
     mean, gain, shift = mean[:1], rate[:1] * gain_ref[...], shift_ref[...]
@@ -233,7 +236,8 @@
     publish(stat_ref, block_moments(evens + odds))
 
 
-def detail_entry_kernel_body(x_ref, parts_ref, gain_ref, shift_ref, wx_ref, wz_ref, out_ref, stat_ref, an):
+def detail_entry_kernel_body(x_ref, parts_ref, gain_ref, shift_ref, k_ref, out_ref, stat_ref, an, wx_ref, wz_ref):
+    pack_detail(k_ref, wx_ref, wz_ref)
     first, last = edge_flags()
     mean, rate = moments(parts_ref, 8 * 2 * W)
     mean, gain, shift = mean[:1], rate[:1] * gain_ref[...], shift_ref[...]
@@ -273,8 +277,9 @@
 
 
 def detail_inner_kernel_body(
-    h_ref, x_ref, parts_ref, gain_ref, shift_ref, w_ref, side_ref, p_ref, out_ref, an, tmp
+    h_ref, x_ref, parts_ref, gain_ref, shift_ref, k_ref, p_ref, out_ref, an, tmp, w_ref, side_ref
 ):
+    pack_inner(k_ref, w_ref, side_ref)
     first, last = edge_flags()
     mean, rate = moments(parts_ref, 16 * 4 * W)
     mean, gain, shift = mean[:1], rate[:1] * gain_ref[...], shift_ref[...]
@@ -337,18 +342,20 @@
     detail_skip_projection,
 ):
     x = coarse.reshape(4, W, 512)
-    up = lax.ppermute(x[2:], "rows", [(i, i + 1) for i in range(ROWS - 1)])
-    down = lax.ppermute(x[:2], "rows", [(i + 1, i) for i in range(ROWS - 1)])
     stat = lambda c: shape(ROWS, 1, 2 * c, dtype=F32)
-    parts = swap(call(coarse_stats_kernel, stat(512), name="coarse_stats")(x))
-    packed = call(pack_broad_kernel, shape(2, 1024, 1024), name="pack_broad", flops=1 << 24)(broad_entry_kernel)
+    parts, head, tail = call(
+        coarse_stats_kernel, (stat(512), shape(2, W, 512), shape(2, W, 512)), name="coarse_stats"
+    )(x)
+    parts = swap(parts)
+    up = lax.ppermute(tail, "rows", [(i, i + 1) for i in range(ROWS - 1)])
+    down = lax.ppermute(head, "rows", [(i + 1, i) for i in range(ROWS - 1)])
     wide_h, parts = call(
         broad_entry_kernel_body,
         (shape(12, W, 512), stat(256)),
-        [pltpu.VMEM((8, W, 512), BF16)],
+        [pltpu.VMEM((8, W, 512), BF16), pltpu.VMEM((2, 1024, 1024), BF16)],
         name="broad_entry",
         flops=1 << 32,
-    )(x, up, down, parts, line(broad_entry_scale), line(broad_entry_bias), packed)
+    )(x, up, down, parts, line(broad_entry_scale), line(broad_entry_bias), broad_entry_kernel)
     parts = swap(parts)
     wide_out, parts = call(
         broad_inner_kernel_body,
@@ -368,24 +375,23 @@
         broad_skip_projection,
     )
     parts = swap(parts)
-    wx, wz = call(
-        pack_detail_kernel, (shape(2, 2, 256, 256), shape(2, 2, 256, 256)), name="pack_detail", flops=1 << 22
-    )(detail_entry_kernel)
     fine_h, parts = call(
         detail_entry_kernel_body,
         (shape(18, W, 512), stat(128)),
-        [pltpu.VMEM((10, W, 512), BF16)],
+        [pltpu.VMEM((10, W, 512), BF16)] + [pltpu.VMEM((2, 2, 256, 256), BF16)] * 2,
         name="detail_entry",
         flops=1 << 32,
-    )(wide_out, parts, line(detail_entry_scale), line(detail_entry_bias), wx, wz)
+    )(wide_out, parts, line(detail_entry_scale), line(detail_entry_bias), detail_entry_kernel)
     parts = swap(parts)
-    main, side = call(
-        pack_inner_kernel, (shape(1536, 512), shape(768, 256)), name="pack_inner", flops=1 << 22
-    )(detail_inner_kernel)
     decoded = call(
         detail_inner_kernel_body,
         shape(COLS, 16, 32, 128),
-        [pltpu.VMEM((18, W, 512), BF16), pltpu.VMEM((4, 4 * W, 128), F32)],
+        [
+            pltpu.VMEM((18, W, 512), BF16),
+            pltpu.VMEM((4, 4 * W, 128), F32),
+            pltpu.VMEM((1536, 512), BF16),
+            pltpu.VMEM((768, 256), BF16),
+        ],
         name="detail_inner",
         flops=1 << 32,
     )(
@@ -394,8 +400,7 @@
         parts,
         line(detail_inner_scale),
         line(detail_inner_bias),
-        main,
-        side,
+        detail_inner_kernel,
         detail_skip_projection,
     )
     return lax.all_to_all(decoded, "cols", 0, 0, tiled=True)

time: 117 us -> 106 us (0.906)
  blocking collectives: 50 us -> 75.7 us
  starting transfers between devices: 18.5 us -> 5.68 us
  waiting for transfers between devices: 9.94 us -> 0.01 us
  Pallas kernels: 27.5 us -> 18.7 us
  local copies, waits for them, and re-layouts: 10.2 us -> 5.45 us
    all_to_all x1 -> x4, blocking collectives: 9.32 us -> 35.9 us  [swap(): return lax.all_to_all(parts, 'rows', 0, 0, tiled=True)]
    all_to_all x3 -> x0, starting transfers between devices: 12.8 us -> none  [swap(): return lax.all_to_all(parts, 'rows', 0, 0, tiled=True)]
    all_to_all x3 -> x0, waiting for transfers between devices: 9.93 us -> none  [swap(): return lax.all_to_all(parts, 'rows', 0, 0, tiled=True)]
    unnamed x41 -> x31, local copies, waits for them, and re-layouts: 9.18 us -> 5.45 us
    pallas_call x4 -> x1, Pallas kernels: 4.06 us -> 0.33 us  [body(): call(coarse_stats_kernel, (stat(512), shape(2, W, 512), shape(2, W, 512))...]
    pallas_call x1, Pallas kernels: 6.67 us -> 4.53 us  [body(): call(broad_entry_kernel_body, (shape(12, W, 512), stat(256)), [pltpu.VMEM...]
    pallas_call x1, Pallas kernels: 6.9 us -> 5.24 us  [body(): call(detail_inner_kernel_body, shape(COLS, 16, 32, 128), [pltpu.VMEM((18,...]
  transfers between devices with their start and end apart: 5 -> 2, of which waited for: 3 -> 0; matrix products, arithmetic and copies ran while one was open for 0% -> 0% of each run, Pallas kernels for 3% -> 0%
where the time goes in v2:
time: 106 us
  blocking collectives  75.7 us (71%)
  Pallas kernels  18.7 us (18%)
  starting transfers between devices  5.68 us (5%)
  local copies, waits for them, and re-layouts  5.45 us (5%)
    all_to_all x1, blocking collectives, body(): return lax.all_to_all(decoded, 'cols', 0, 0, tiled=True)  39.8 us
    all_to_all x4, blocking collectives, swap(): return lax.all_to_all(parts, 'rows', 0, 0, tiled=True)  35.9 us
    unnamed x31, local copies, waits for them, and re-layouts  5.45 us
    pallas_call x1, Pallas kernels, body(): call(detail_inner_kernel_body, shape(COLS, 16, 32, 128), [pltpu.VMEM((18,...  5.24 us
    pallas_call x1, Pallas kernels, body(): call(broad_entry_kernel_body, (shape(12, W, 512), stat(256)), [pltpu.VMEM...  4.53 us
    ppermute x1, starting transfers between devices, body(): up = lax.ppermute(tail, 'rows', [(i, i + 1) for i in range(ROWS - 1)])  4.39 us
    pallas_call x1, Pallas kernels, body(): call(broad_inner_kernel_body, (shape(10, W, 512), stat(256)), [pltpu.VMEM...  4.38 us
    pallas_call x1, Pallas kernels, body(): call(detail_entry_kernel_body, (shape(18, W, 512), stat(128)), [pltpu.VME...  4.27 us
  transfers between devices with their start and end apart: 2, of which 0 were waited for; matrix products, arithmetic and copies ran while one was open for 0% of the time, Pallas kernels for 0%

profile of v2, /device:TPU:1, one launch (start us, length us, event | category | flops | bytes accessed | tf_op | source)
XLA Modules:
  0.0 105.7 jit_solution(4966667782274796138)
XLA Ops:
  0.0 1.0 copy-done
  1.0 0.3 coarse_stats.1
  1.4 4.4 %collective-permute-start = (bf16[2,128,512]{2,1,0:T(8,128)(2,1)S(1)}, bf16[2,128,512]{2,1,0:T(8,128)(2,1)S(1)}, u32[]{:S(2)}, u32[]{:S(2)}) collective-permute-start(bf16[2,128,512]{2,1,0:T(8,128)(2,1)S(1)} %get-tuple-element.14), channel_id=1, source_target_pairs={{0,16},{16,32},{32,48},{48,64},{64,80},{80,96},{96,112},{1,17},{17... | collective-permute-start | bytes 786440 | tf_op jit(solution)/shard_map/ppermute | solution.py:350
  5.8 1.3 %collective-permute-start.1 = (bf16[2,128,512]{2,1,0:T(8,128)(2,1)S(1)}, bf16[2,128,512]{2,1,0:T(8,128)(2,1)S(1)}, u32[]{:S(2)}, u32[]{:S(2)}) collective-permute-start(bf16[2,128,512]{2,1,0:T(8,128)(2,1)S(1)} %get-tuple-element.15), channel_id=1, source_target_pairs={{16,0},{32,16},{48,32},{64,48},{80,64},{96,80},{112,96},{17,1},{33... | collective-permute-start | bytes 786440 | tf_op jit(solution)/shard_map/ppermute | solution.py:351
  7.1 10.8 %all_to_all.25.parts_ref = f32[8,1,1024]{2,1,0:T(1,128)S(1)} all-to-all(f32[8,1,1024]{2,1,0:T(1,128)S(1)} %get-tuple-element.16), channel_id=1, replica_groups=mesh['rows'=8,'cols'=16] {'rows'}, dimensions={0} | all-to-all | bytes 65536 | tf_op jit(solution)/shard_map/all_to_all | solution.py:316
  17.9 0.0 collective-permute-done.up_ref
  17.9 0.0 collective-permute-done.1.down_ref
  17.9 1.7 %copy-done.1 = bf16[3,3,512,256]{3,2,1,0:T(8,128)(2,1)S(1)} copy-done((bf16[3,3,512,256]{3,2,1,0:T(8,128)(2,1)S(1)}, bf16[3,3,512,256]{3,2,1,0:T(8,128)(2,1)}, u32[]{:S(2)}) %copy-start.1) | copy-done | bytes 2359320
  19.6 0.7 copy-done.7
  20.3 0.7 copy-done.8
  21.0 4.5 %broad_entry.1 = (bf16[12,128,512]{2,1,0:T(8,128)(2,1)S(1)}, f32[8,1,512]{2,1,0:T(1,128)S(1)}) custom-call(bf16[4,128,512]{2,1,0:T(8,128)(2,1)S(1)} %bitcast.11, bf16[2,128,512]{2,1,0:T(8,128)(2,1)S(1)} %collective-permute-done.up_ref, bf16[2,128,512]{2,1,0:T(8,128)(2,1)S(1)} %collective-permute-done.1.down_ref, f32[8,1,1024]{2,1,0:T(1,128)S(1)} %all_to_all.25.parts_ref, ...), custom_call_target="tpu_custom_call" | custom-call | flops 4294967296 | tf_op jit(solution)/shard_map/broad_entry/pallas_call | solution.py:352
  25.5 10.3 %all_to_all.26.parts_ref = f32[8,1,512]{2,1,0:T(1,128)S(1)} all-to-all(f32[8,1,512]{2,1,0:T(1,128)S(1)} %get-tuple-element.18), channel_id=1, replica_groups=mesh['rows'=8,'cols'=16] {'rows'}, dimensions={0} | all-to-all | bytes 32768 | tf_op jit(solution)/shard_map/all_to_all | solution.py:316
  35.8 0.0 copy-done.2
  35.8 0.0 copy-done.5
  35.8 0.0 copy-done.9
  35.8 0.0 copy-done.10
  35.8 0.0 copy-start.3
  35.8 0.0 copy-start.11
  35.8 0.0 copy-start.12
  35.9 4.4 %broad_inner.1 = (bf16[10,128,512]{2,1,0:T(8,128)(2,1)S(1)}, f32[8,1,512]{2,1,0:T(1,128)S(1)}) custom-call(bf16[12,128,512]{2,1,0:T(8,128)(2,1)S(1)} %get-tuple-element.17.h_ref, bf16[4,128,512]{2,1,0:T(8,128)(2,1)S(1)} %bitcast.12, bf16[2,128,512]{2,1,0:T(8,128)(2,1)S(1)} %collective-permute-done.up_ref, ...), custom_call_target="tpu_custom_call" | custom-call | flops 4294967296 | tf_op jit(solution)/shard_map/broad_inner/pallas_call | solution.py:360
  40.2 7.4 %all_to_all.27.parts_ref = f32[8,1,512]{2,1,0:T(1,128)S(1)} all-to-all(f32[8,1,512]{2,1,0:T(1,128)S(1)} %get-tuple-element.20), channel_id=1, replica_groups=mesh['rows'=8,'cols'=16] {'rows'}, dimensions={0} | all-to-all | bytes 32768 | tf_op jit(solution)/shard_map/all_to_all | solution.py:316
  47.6 0.0 copy-done.3
  47.7 0.0 copy-start.4
  47.7 0.0 copy-start.6
  47.7 0.0 copy-start.13
  47.7 0.0 copy-start.14
  47.7 4.3 %detail_entry.1 = (bf16[18,128,512]{2,1,0:T(8,128)(2,1)S(1)}, f32[8,1,256]{2,1,0:T(1,128)S(1)}) custom-call(bf16[10,128,512]{2,1,0:T(8,128)(2,1)S(1)} %get-tuple-element.19.x_ref, f32[8,1,512]{2,1,0:T(1,128)S(1)} %all_to_all.27.parts_ref, f32[1,256]{1,0:T(1,128)S(1)} %bitcast.18, f32[1,256]{1,0:T(1,128)S(1)} %bitcast.19, bf16[3,3,256,128]{3,2,1,0:T(8,128)(2,1)S(1)} %copy-done.3), custom_call_target="tpu_custom_call" | custom-call | flops 4294967296 | tf_op jit(solution)/shard_map/detail_entry/pallas_call | solution.py:378
  52.0 7.4 %all_to_all.28.parts_ref = f32[8,1,256]{2,1,0:T(1,128)S(1)} all-to-all(f32[8,1,256]{2,1,0:T(1,128)S(1)} %get-tuple-element.22), channel_id=1, replica_groups=mesh['rows'=8,'cols'=16] {'rows'}, dimensions={0} | all-to-all | bytes 16384 | tf_op jit(solution)/shard_map/all_to_all | solution.py:316
  59.4 0.0 copy-done.13
  59.4 5.2 %detail_inner.1 = bf16[16,16,32,128]{3,2,1,0:T(8,128)(2,1)S(1)} custom-call(bf16[18,128,512]{2,1,0:T(8,128)(2,1)S(1)} %get-tuple-element.21.h_ref, bf16[10,128,512]{2,1,0:T(8,128)(2,1)S(1)} %get-tuple-element.19.x_ref, f32[8,1,256]{2,1,0:T(1,128)S(1)} %all_to_all.28.parts_ref, f32[1,128]{1,0:T(1,128)S(1)} %bitcast.20, f32[1,128]{1,0:T(1,128)S(1)} %bitcast.21, ...), custom_call_target="tpu_custom_call" | custom-call | flops 4294967296 | tf_op jit(solution)/shard_map/detail_inner/pallas_call | solution.py:386
  64.6 39.8 %all_to_all.29 = bf16[16,16,32,128]{3,2,1,0:T(8,128)(2,1)S(1)} all-to-all(bf16[16,16,32,128]{3,2,1,0:T(8,128)(2,1)S(1)} %detail_inner.1), channel_id=1, replica_groups=mesh['rows'=8,'cols'=16] {'cols'}, dimensions={0} | all-to-all | bytes 4194304 | tf_op jit(solution)/shard_map/all_to_all | solution.py:406
  104.4 1.3 %copy.17 = bf16[16,16,32,128]{3,2,1,0:T(8,128)(2,1)} copy(bf16[16,16,32,128]{3,2,1,0:T(8,128)(2,1)S(1)} %all_to_all.29) | data formatting | bytes 4194304
  (13 shorter events, 0.0 us)
Async XLA Ops:
  0.0 1.0 copy-start
  1.4 16.5 %collective-permute-start = (bf16[2,128,512]{2,1,0:T(8,128)(2,1)S(1)}, bf16[2,128,512]{2,1,0:T(8,128)(2,1)S(1)}, u32[]{:S(2)}, u32[]{:S(2)}) collective-permute-start(bf16[2,128,512]{2,1,0:T(8,128)(2,1)S(1)} %get-tuple-element.14), channel_id=1, source_target_pairs={{0,16},{16,32},{32,48},{48,64},{64,80},{80,96},{96,112},{1,17},{17... | collective-permute-start | bytes 786440 | tf_op jit(solution)/shard_map/ppermute | solution.py:350
  5.8 12.1 %collective-permute-start.1 = (bf16[2,128,512]{2,1,0:T(8,128)(2,1)S(1)}, bf16[2,128,512]{2,1,0:T(8,128)(2,1)S(1)}, u32[]{:S(2)}, u32[]{:S(2)}) collective-permute-start(bf16[2,128,512]{2,1,0:T(8,128)(2,1)S(1)} %get-tuple-element.15), channel_id=1, source_target_pairs={{16,0},{32,16},{48,32},{64,48},{80,64},{96,80},{112,96},{17,1},{33... | collective-permute-start | bytes 786440 | tf_op jit(solution)/shard_map/ppermute | solution.py:351
  17.9 1.7 %copy-start.1 = (bf16[3,3,512,256]{3,2,1,0:T(8,128)(2,1)S(1)}, bf16[3,3,512,256]{3,2,1,0:T(8,128)(2,1)}, u32[]{:S(2)}) copy-start(bf16[3,3,512,256]{3,2,1,0:T(8,128)(2,1)} %k_ref.3) | copy-start | bytes 7077892
  19.6 0.7 copy-start.7
  20.3 0.7 copy-start.8
  20.9 14.9 %copy-start.2 = (bf16[3,3,256,256]{3,2,1,0:T(8,128)(2,1)S(1)}, bf16[3,3,256,256]{3,2,1,0:T(8,128)(2,1)}, u32[]{:S(2)}) copy-start(bf16[3,3,256,256]{3,2,1,0:T(8,128)(2,1)} %param.21) | copy-start | bytes 3538948
  20.9 14.9 %copy-start.5 = (bf16[512,256]{1,0:T(8,128)(2,1)S(1)}, bf16[512,256]{1,0:T(8,128)(2,1)}, u32[]{:S(2)}) copy-start(bf16[512,256]{1,0:T(8,128)(2,1)} %p_ref.2) | copy-start | bytes 786436
  20.9 14.9 %copy-start.9 = (f32[256]{0:T(256)S(1)}, f32[256]{0:T(256)}, u32[]{:S(2)}) copy-start(f32[256]{0:T(256)} %param.19) | copy-start | bytes 3076
  21.0 14.9 %copy-start.10 = (f32[256]{0:T(256)S(1)}, f32[256]{0:T(256)}, u32[]{:S(2)}) copy-start(f32[256]{0:T(256)} %param.20) | copy-start | bytes 3076
  35.8 11.8 %copy-start.3 = (bf16[3,3,256,128]{3,2,1,0:T(8,128)(2,1)S(1)}, bf16[3,3,256,128]{3,2,1,0:T(8,128)(2,1)}, u32[]{:S(2)}) copy-start(bf16[3,3,256,128]{3,2,1,0:T(8,128)(2,1)} %k_ref.4) | copy-start | bytes 1769476
  35.8 11.8 %copy-start.11 = (f32[256]{0:T(256)S(1)}, f32[256]{0:T(256)}, u32[]{:S(2)}) copy-start(f32[256]{0:T(256)} %param.23) | copy-start | bytes 3076
  35.8 11.8 %copy-start.12 = (f32[256]{0:T(256)S(1)}, f32[256]{0:T(256)}, u32[]{:S(2)}) copy-start(f32[256]{0:T(256)} %param.24) | copy-start | bytes 3076
  47.7 11.7 %copy-start.4 = (bf16[3,3,128,128]{3,2,1,0:T(8,128)(2,1)S(1)}, bf16[3,3,128,128]{3,2,1,0:T(8,128)(2,1)}, u32[]{:S(2)}) copy-start(bf16[3,3,128,128]{3,2,1,0:T(8,128)(2,1)} %k_ref.5) | copy-start | bytes 884740
  47.7 11.7 %copy-start.6 = (bf16[256,128]{1,0:T(8,128)(2,1)S(1)}, bf16[256,128]{1,0:T(8,128)(2,1)}, u32[]{:S(2)}) copy-start(bf16[256,128]{1,0:T(8,128)(2,1)} %p_ref.3) | copy-start | bytes 196612
  47.7 11.7 %copy-start.13 = (f32[128]{0:T(128)S(1)}, f32[128]{0:T(128)}, u32[]{:S(2)}) copy-start(f32[128]{0:T(128)} %param.26) | copy-start | bytes 1540
  47.7 11.7 %copy-start.14 = (f32[128]{0:T(128)S(1)}, f32[128]{0:T(128)}, u32[]{:S(2)}) copy-start(f32[128]{0:T(128)} %param.27) | copy-start | bytes 1540

commit v3 on v2

--- a/solution.py
+++ b/solution.py
@@ -17,10 +17,15 @@
 VMEM_LIMIT = 24 * 1024 * 1024
 
 
-def call(kernel, out_shape, scratch=(), flops=0, name=None):
+VMEM = pl.BlockSpec(memory_space=pltpu.VMEM)
+HBM = pl.BlockSpec(memory_space=pltpu.HBM)
+
+
+def call(kernel, out_shape, scratch=(), flops=0, name=None, specs=None):
     return pl.pallas_call(
         kernel,
         out_shape=out_shape,
+        **({} if specs is None else {"in_specs": specs}),
         scratch_shapes=list(scratch),
         name=name,
         cost_estimate=pl.CostEstimate(flops=flops, bytes_accessed=0, transcendentals=0),
@@ -164,8 +169,23 @@
         side_ref[base + 128 : base + 256, 128:256] = k[2]
 
 
-def broad_entry_kernel_body(x_ref, up_ref, down_ref, parts_ref, gain_ref, shift_ref, k_ref, out_ref, stat_ref, an, w_ref):
+def prepare_kernel_body(
+    parts_ref, gain_hbm, shift_hbm, k_hbm, parts_out, gain_ref, shift_ref, w_ref, k_ref, sems
+):
+    pairs = ((gain_hbm, gain_ref), (shift_hbm, shift_ref)) + tuple((k_hbm.at[i], k_ref.at[i]) for i in range(3))
+    copies = [pltpu.make_async_copy(src, dst, sems.at[i]) for i, (src, dst) in enumerate(pairs)]
+    for copy in copies:
+        copy.start()
+    for d in range(ROWS):
+        parts_out[d] = parts_ref[d]
+    for copy in copies:
+        copy.wait()
     pack_broad(k_ref, w_ref)
+
+
+def broad_entry_kernel_body(
+    x_ref, up_ref, down_ref, parts_ref, gain_ref, shift_ref, w_ref, out_ref, stat_ref, an
+):
     first, last = edge_flags()
     mean, rate = moments(parts_ref, 4 * W)
     mean, gain, shift = mean[:1], rate[:1] * gain_ref[...], shift_ref[...]
@@ -320,6 +340,10 @@
     return jax.ShapeDtypeStruct(dims, dtype)
 
 
+def stay(v):
+    return pltpu.with_memory_space_constraint(v, pltpu.HBM)
+
+
 def line(v):
     return v.reshape(1, -1)
 
@@ -346,16 +370,24 @@
     parts, head, tail = call(
         coarse_stats_kernel, (stat(512), shape(2, W, 512), shape(2, W, 512)), name="coarse_stats"
     )(x)
+    up = lax.ppermute(tail, "rows", [(i, (i + 1) % ROWS) for i in range(ROWS)])
+    down = lax.ppermute(head, "rows", [((i + 1) % ROWS, i) for i in range(ROWS)])
+    parts, gain, shift, packed = call(
+        prepare_kernel_body,
+        (stat(512), shape(1, 512, dtype=F32), shape(1, 512, dtype=F32), shape(2, 1024, 1024)),
+        [pltpu.VMEM((3, 3, 512, 256), BF16), pltpu.SemaphoreType.DMA((5,))],
+        name="prepare",
+        flops=1 << 30,
+        specs=[VMEM] + [HBM] * 3,
+    )(parts, *(stay(v) for v in (line(broad_entry_scale), line(broad_entry_bias), broad_entry_kernel)))
     parts = swap(parts)
-    up = lax.ppermute(tail, "rows", [(i, i + 1) for i in range(ROWS - 1)])
-    down = lax.ppermute(head, "rows", [(i + 1, i) for i in range(ROWS - 1)])
     wide_h, parts = call(
         broad_entry_kernel_body,
         (shape(12, W, 512), stat(256)),
-        [pltpu.VMEM((8, W, 512), BF16), pltpu.VMEM((2, 1024, 1024), BF16)],
+        [pltpu.VMEM((8, W, 512), BF16)],
         name="broad_entry",
         flops=1 << 32,
-    )(x, up, down, parts, line(broad_entry_scale), line(broad_entry_bias), broad_entry_kernel)
+    )(x, up, down, parts, gain, shift, packed)
     parts = swap(parts)
     wide_out, parts = call(
         broad_inner_kernel_body,

time: 106 us -> 101 us (0.953)
  blocking collectives: 75.7 us -> 72.1 us
  local copies, waits for them, and re-layouts: 5.45 us -> 2.44 us
  Pallas kernels: 18.7 us -> 21.1 us
    all_to_all x4, blocking collectives: 35.9 us -> 32.3 us  [swap(): return lax.all_to_all(parts, 'rows', 0, 0, tiled=True)]
    unnamed x31 -> x27, local copies, waits for them, and re-layouts: 5.45 us -> 2.44 us
    pallas_call x0 -> x1, Pallas kernels: none -> 2.47 us  [body(): call(prepare_kernel_body, (stat(512), shape(1, 512, dtype=F32), shape(1,...]
  transfers between devices with their start and end apart: 2 -> 2, of which waited for: 0 -> 0; matrix products, arithmetic and copies ran while one was open for 0% -> 0% of each run, Pallas kernels for 0% -> 2%
where the time goes in v3:
time: 101 us
  blocking collectives  72.1 us (71%)
  Pallas kernels  21.1 us (21%)
  starting transfers between devices  5.07 us (5%)
  local copies, waits for them, and re-layouts  2.44 us (2%)
    all_to_all x1, blocking collectives, body(): return lax.all_to_all(decoded, 'cols', 0, 0, tiled=True)  39.8 us
    all_to_all x4, blocking collectives, swap(): return lax.all_to_all(parts, 'rows', 0, 0, tiled=True)  32.3 us
    pallas_call x1, Pallas kernels, body(): call(detail_inner_kernel_body, shape(COLS, 16, 32, 128), [pltpu.VMEM((18,...  5.25 us
    pallas_call x1, Pallas kernels, body(): call(broad_entry_kernel_body, (shape(12, W, 512), stat(256)), [pltpu.VMEM...  4.42 us
    pallas_call x1, Pallas kernels, body(): call(broad_inner_kernel_body, (shape(10, W, 512), stat(256)), [pltpu.VMEM...  4.38 us
    pallas_call x1, Pallas kernels, body(): call(detail_entry_kernel_body, (shape(18, W, 512), stat(128)), [pltpu.VME...  4.28 us
    ppermute x1, starting transfers between devices, body(): up = lax.ppermute(tail, 'rows', [(i, (i + 1) % ROWS) for i in range(ROWS)])  2.54 us
    ppermute x1, starting transfers between devices, body(): lax.ppermute(head, 'rows', [((i + 1) % ROWS, i) for i in range(ROWS)])  2.53 us
  transfers between devices with their start and end apart: 2, of which 0 were waited for; matrix products, arithmetic and copies ran while one was open for 0% of the time, Pallas kernels for 2%

profile of v3, /device:TPU:1, one launch (start us, length us, event | category | flops | bytes accessed | tf_op | source)
XLA Modules:
  0.0 100.8 jit_solution(17937729583462328500)
XLA Ops:
  0.0 1.0 %copy-done = bf16[1,4,128,512]{3,2,1,0:T(8,128)(2,1)S(1)} copy-done((bf16[1,4,128,512]{3,2,1,0:T(8,128)(2,1)S(1)}, bf16[1,4,128,512]{3,2,1,0:T(8,128)(2,1)}, u32[]{:S(2)}) %copy-start) | copy-done | bytes 524312
  1.0 0.3 coarse_stats.1
  1.4 0.0 copy-start.1
  1.4 2.5 %collective-permute-start = (bf16[2,128,512]{2,1,0:T(8,128)(2,1)S(1)}, bf16[2,128,512]{2,1,0:T(8,128)(2,1)S(1)}, u32[]{:S(2)}, u32[]{:S(2)}) collective-permute-start(bf16[2,128,512]{2,1,0:T(8,128)(2,1)S(1)} %get-tuple-element.18), channel_id=1, source_target_pairs={{0,16},{16,32},{32,48},{48,64},{64,80},{80,96},{96,112},{112,0},{1... | collective-permute-start | bytes 786440 | tf_op jit(solution)/shard_map/ppermute | solution.py:373
  3.9 2.5 %collective-permute-start.1 = (bf16[2,128,512]{2,1,0:T(8,128)(2,1)S(1)}, bf16[2,128,512]{2,1,0:T(8,128)(2,1)S(1)}, u32[]{:S(2)}, u32[]{:S(2)}) collective-permute-start(bf16[2,128,512]{2,1,0:T(8,128)(2,1)S(1)} %get-tuple-element.19), channel_id=1, source_target_pairs={{16,0},{32,16},{48,32},{64,48},{80,64},{96,80},{112,96},{0,112},{1... | collective-permute-start | bytes 786440 | tf_op jit(solution)/shard_map/ppermute | solution.py:374
  6.5 2.5 %prepare.1 = (f32[8,1,1024]{2,1,0:T(1,128)S(1)}, f32[1,512]{1,0:T(1,128)S(1)}, f32[1,512]{1,0:T(1,128)S(1)}, bf16[2,1024,1024]{2,1,0:T(8,128)(2,1)S(1)}) custom-call(f32[8,1,1024]{2,1,0:T(1,128)S(1)} %get-tuple-element.20.parts_ref, f32[1,512]{1,0:T(1,128)} %bitcast.20, f32[1,512]{1,0:T(1,128)} %bitcast.21, bf16[3,3,512,256]{3,2,1,0:T(8,128)(2,1)} %k_hbm.1), custom_call_target="tpu_custom_call" | custom-call | flops 1073741824 | tf_op jit(solution)/shard_map/prepare/pallas_call | solution.py:375
  8.9 8.0 %all_to_all.25.parts_ref = f32[8,1,1024]{2,1,0:T(1,128)S(1)} all-to-all(f32[8,1,1024]{2,1,0:T(1,128)S(1)} %get-tuple-element.21), channel_id=1, replica_groups=mesh['rows'=8,'cols'=16] {'rows'}, dimensions={0} | all-to-all | bytes 65536 | tf_op jit(solution)/shard_map/all_to_all | solution.py:336
  16.9 0.0 collective-permute-done.up_ref
  16.9 0.0 collective-permute-done.1.down_ref
  16.9 0.0 copy-done.1
  16.9 0.0 copy-start.2
  17.0 0.0 copy-start.5
  17.0 0.0 copy-start.7
  17.0 0.0 copy-start.8
  17.0 4.4 %broad_entry.1 = (bf16[12,128,512]{2,1,0:T(8,128)(2,1)S(1)}, f32[8,1,512]{2,1,0:T(1,128)S(1)}) custom-call(bf16[4,128,512]{2,1,0:T(8,128)(2,1)S(1)} %bitcast.11, bf16[2,128,512]{2,1,0:T(8,128)(2,1)S(1)} %collective-permute-done.up_ref, bf16[2,128,512]{2,1,0:T(8,128)(2,1)S(1)} %collective-permute-done.1.down_ref, f32[8,1,1024]{2,1,0:T(1,128)S(1)} %all_to_all.25.parts_ref, ...), custom_call_target="tpu_custom_call" | custom-call | flops 4294967296 | tf_op jit(solution)/shard_map/broad_entry/pallas_call | solution.py:384
  21.4 9.5 %all_to_all.26.parts_ref = f32[8,1,512]{2,1,0:T(1,128)S(1)} all-to-all(f32[8,1,512]{2,1,0:T(1,128)S(1)} %get-tuple-element.26), channel_id=1, replica_groups=mesh['rows'=8,'cols'=16] {'rows'}, dimensions={0} | all-to-all | bytes 32768 | tf_op jit(solution)/shard_map/all_to_all | solution.py:336
  30.9 0.0 copy-done.2
  30.9 0.0 copy-start.3
  30.9 0.0 copy-start.9
  30.9 0.0 copy-start.10
  30.9 4.4 %broad_inner.1 = (bf16[10,128,512]{2,1,0:T(8,128)(2,1)S(1)}, f32[8,1,512]{2,1,0:T(1,128)S(1)}) custom-call(bf16[12,128,512]{2,1,0:T(8,128)(2,1)S(1)} %get-tuple-element.25.h_ref, bf16[4,128,512]{2,1,0:T(8,128)(2,1)S(1)} %bitcast.12, bf16[2,128,512]{2,1,0:T(8,128)(2,1)S(1)} %collective-permute-done.up_ref, ...), custom_call_target="tpu_custom_call" | custom-call | flops 4294967296 | tf_op jit(solution)/shard_map/broad_inner/pallas_call | solution.py:392
  35.3 7.4 %all_to_all.27.parts_ref = f32[8,1,512]{2,1,0:T(1,128)S(1)} all-to-all(f32[8,1,512]{2,1,0:T(1,128)S(1)} %get-tuple-element.28), channel_id=1, replica_groups=mesh['rows'=8,'cols'=16] {'rows'}, dimensions={0} | all-to-all | bytes 32768 | tf_op jit(solution)/shard_map/all_to_all | solution.py:336
  42.7 0.0 copy-done.10
  42.7 0.0 copy-start.4
  42.7 0.0 copy-start.6
  42.8 0.0 copy-start.11
  42.8 0.0 copy-start.12
  42.8 4.3 %detail_entry.1 = (bf16[18,128,512]{2,1,0:T(8,128)(2,1)S(1)}, f32[8,1,256]{2,1,0:T(1,128)S(1)}) custom-call(bf16[10,128,512]{2,1,0:T(8,128)(2,1)S(1)} %get-tuple-element.27.x_ref, f32[8,1,512]{2,1,0:T(1,128)S(1)} %all_to_all.27.parts_ref, f32[1,256]{1,0:T(1,128)S(1)} %bitcast.16, f32[1,256]{1,0:T(1,128)S(1)} %bitcast.17, bf16[3,3,256,128]{3,2,1,0:T(8,128)(2,1)S(1)} %copy-done.3), custom_call_target="tpu_custom_call" | custom-call | flops 4294967296 | tf_op jit(solution)/shard_map/detail_entry/pallas_call | solution.py:410
  47.1 7.4 %all_to_all.28.parts_ref = f32[8,1,256]{2,1,0:T(1,128)S(1)} all-to-all(f32[8,1,256]{2,1,0:T(1,128)S(1)} %get-tuple-element.30), channel_id=1, replica_groups=mesh['rows'=8,'cols'=16] {'rows'}, dimensions={0} | all-to-all | bytes 16384 | tf_op jit(solution)/shard_map/all_to_all | solution.py:336
  54.5 5.3 %detail_inner.1 = bf16[16,16,32,128]{3,2,1,0:T(8,128)(2,1)S(1)} custom-call(bf16[18,128,512]{2,1,0:T(8,128)(2,1)S(1)} %get-tuple-element.29.h_ref, bf16[10,128,512]{2,1,0:T(8,128)(2,1)S(1)} %get-tuple-element.27.x_ref, f32[8,1,256]{2,1,0:T(1,128)S(1)} %all_to_all.28.parts_ref, f32[1,128]{1,0:T(1,128)S(1)} %bitcast.18, f32[1,128]{1,0:T(1,128)S(1)} %bitcast.19, ...), custom_call_target="tpu_custom_call" | custom-call | flops 4294967296 | tf_op jit(solution)/shard_map/detail_inner/pallas_call | solution.py:418
  59.7 39.8 %all_to_all.29 = bf16[16,16,32,128]{3,2,1,0:T(8,128)(2,1)S(1)} all-to-all(bf16[16,16,32,128]{3,2,1,0:T(8,128)(2,1)S(1)} %detail_inner.1), channel_id=1, replica_groups=mesh['rows'=8,'cols'=16] {'cols'}, dimensions={0} | all-to-all | bytes 4194304 | tf_op jit(solution)/shard_map/all_to_all | solution.py:438
  99.5 1.3 %copy.17 = bf16[16,16,32,128]{3,2,1,0:T(8,128)(2,1)} copy(bf16[16,16,32,128]{3,2,1,0:T(8,128)(2,1)S(1)} %all_to_all.29) | data formatting | bytes 4194304
  (10 shorter events, 0.0 us)
Async XLA Ops:
  0.0 1.0 %copy-start = (bf16[1,4,128,512]{3,2,1,0:T(8,128)(2,1)S(1)}, bf16[1,4,128,512]{3,2,1,0:T(8,128)(2,1)}, u32[]{:S(2)}) copy-start(bf16[1,4,128,512]{3,2,1,0:T(8,128)(2,1)} %param.15) | copy-start | bytes 1572868
  1.4 15.6 %copy-start.1 = (bf16[1,4,128,512]{3,2,1,0:T(8,128)(2,1)S(1)}, bf16[1,4,128,512]{3,2,1,0:T(8,128)(2,1)}, u32[]{:S(2)}) copy-start(bf16[1,4,128,512]{3,2,1,0:T(8,128)(2,1)} %param.15) | copy-start | bytes 1572868
  1.4 15.6 %collective-permute-start = (bf16[2,128,512]{2,1,0:T(8,128)(2,1)S(1)}, bf16[2,128,512]{2,1,0:T(8,128)(2,1)S(1)}, u32[]{:S(2)}, u32[]{:S(2)}) collective-permute-start(bf16[2,128,512]{2,1,0:T(8,128)(2,1)S(1)} %get-tuple-element.18), channel_id=1, source_target_pairs={{0,16},{16,32},{32,48},{48,64},{64,80},{80,96},{96,112},{112,0},{1... | collective-permute-start | bytes 786440 | tf_op jit(solution)/shard_map/ppermute | solution.py:373
  3.9 13.0 %collective-permute-start.1 = (bf16[2,128,512]{2,1,0:T(8,128)(2,1)S(1)}, bf16[2,128,512]{2,1,0:T(8,128)(2,1)S(1)}, u32[]{:S(2)}, u32[]{:S(2)}) collective-permute-start(bf16[2,128,512]{2,1,0:T(8,128)(2,1)S(1)} %get-tuple-element.19), channel_id=1, source_target_pairs={{16,0},{32,16},{48,32},{64,48},{80,64},{96,80},{112,96},{0,112},{1... | collective-permute-start | bytes 786440 | tf_op jit(solution)/shard_map/ppermute | solution.py:374
  16.9 13.9 %copy-start.2 = (bf16[3,3,256,256]{3,2,1,0:T(8,128)(2,1)S(1)}, bf16[3,3,256,256]{3,2,1,0:T(8,128)(2,1)}, u32[]{:S(2)}) copy-start(bf16[3,3,256,256]{3,2,1,0:T(8,128)(2,1)} %param.21) | copy-start | bytes 3538948
  17.0 13.9 %copy-start.5 = (bf16[512,256]{1,0:T(8,128)(2,1)S(1)}, bf16[512,256]{1,0:T(8,128)(2,1)}, u32[]{:S(2)}) copy-start(bf16[512,256]{1,0:T(8,128)(2,1)} %p_ref.2) | copy-start | bytes 786436
  17.0 13.9 %copy-start.7 = (f32[256]{0:T(256)S(1)}, f32[256]{0:T(256)}, u32[]{:S(2)}) copy-start(f32[256]{0:T(256)} %param.19) | copy-start | bytes 3076
  17.0 13.9 %copy-start.8 = (f32[256]{0:T(256)S(1)}, f32[256]{0:T(256)}, u32[]{:S(2)}) copy-start(f32[256]{0:T(256)} %param.20) | copy-start | bytes 3076
  30.9 11.8 %copy-start.3 = (bf16[3,3,256,128]{3,2,1,0:T(8,128)(2,1)S(1)}, bf16[3,3,256,128]{3,2,1,0:T(8,128)(2,1)}, u32[]{:S(2)}) copy-start(bf16[3,3,256,128]{3,2,1,0:T(8,128)(2,1)} %k_ref.2) | copy-start | bytes 1769476
  30.9 11.8 %copy-start.9 = (f32[256]{0:T(256)S(1)}, f32[256]{0:T(256)}, u32[]{:S(2)}) copy-start(f32[256]{0:T(256)} %param.23) | copy-start | bytes 3076
  30.9 11.8 %copy-start.10 = (f32[256]{0:T(256)S(1)}, f32[256]{0:T(256)}, u32[]{:S(2)}) copy-start(f32[256]{0:T(256)} %param.24) | copy-start | bytes 3076
  42.7 11.7 %copy-start.4 = (bf16[3,3,128,128]{3,2,1,0:T(8,128)(2,1)S(1)}, bf16[3,3,128,128]{3,2,1,0:T(8,128)(2,1)}, u32[]{:S(2)}) copy-start(bf16[3,3,128,128]{3,2,1,0:T(8,128)(2,1)} %k_ref.3) | copy-start | bytes 884740
  42.7 11.7 %copy-start.6 = (bf16[256,128]{1,0:T(8,128)(2,1)S(1)}, bf16[256,128]{1,0:T(8,128)(2,1)}, u32[]{:S(2)}) copy-start(bf16[256,128]{1,0:T(8,128)(2,1)} %p_ref.3) | copy-start | bytes 196612
  42.8 11.7 %copy-start.11 = (f32[128]{0:T(128)S(1)}, f32[128]{0:T(128)}, u32[]{:S(2)}) copy-start(f32[128]{0:T(128)} %param.26) | copy-start | bytes 1540
  42.8 11.7 %copy-start.12 = (f32[128]{0:T(128)S(1)}, f32[128]{0:T(128)}, u32[]{:S(2)}) copy-start(f32[128]{0:T(128)} %param.27) | copy-start | bytes 1540

commit v4 on v3

v4 whole, which is shorter than its diff:
```python
import functools

import jax
import jax.numpy as jnp
from jax import lax
from jax.experimental import pallas as pl
from jax.experimental.pallas import tpu as pltpu
from jax.sharding import PartitionSpec as P

GROUPS = 32
EPSILON = 1e-06
F32 = jnp.float32
BF16 = jnp.bfloat16
ROWS = 8
COLS = 16
W = 128
VMEM_LIMIT = 24 * 1024 * 1024


VMEM = pl.BlockSpec(memory_space=pltpu.VMEM)
HBM = pl.BlockSpec(memory_space=pltpu.HBM)


def call(kernel, out_shape, scratch=(), flops=0, name=None, specs=None):
    return pl.pallas_call(
        kernel,
        out_shape=out_shape,
        **({} if specs is None else {"in_specs": specs}),
        scratch_shapes=list(scratch),
        name=name,
        cost_estimate=pl.CostEstimate(flops=flops, bytes_accessed=0, transcendentals=0),
        compiler_params=pltpu.CompilerParams(vmem_limit_bytes=VMEM_LIMIT),
    )


def group_sum(v, size):
    count = v.shape[-1]
    lane = lax.broadcasted_iota(jnp.int32, v.shape, 1)
    step = 1
    while step < size:
        before = pltpu.roll(v, step, 1)
        after = pltpu.roll(v, count - step, 1)
        v = v + jnp.where((lane & step) != 0, before, after)
        step *= 2
    return v


def moments(parts, held):
    lines = []
    for ref in parts:
        lines += [ref[d] for d in range(ref.shape[0])] if len(ref.shape) == 3 else [ref[...]]
    both = jnp.concatenate(lines, axis=0)
    chans = both.shape[1] // 2
    size = chans // GROUPS
    sums, squares = both[:, :chans], both[:, chans:]
    entries = float(ROWS * held * size)
    total = jnp.broadcast_to(jnp.sum(sums, axis=0, keepdims=True), sums.shape)
    mean = group_sum(total, size) / entries
    off = sums / float(held) - mean
    spread = jnp.sum(squares + float(held) * off * off, axis=0, keepdims=True)
    spread = group_sum(jnp.broadcast_to(spread, sums.shape), size) / entries
    return mean, lax.rsqrt(spread + EPSILON)


def tile_lanes(v, times):
    return jnp.concatenate([v] * times, axis=1) if times > 1 else v


def active(value, mean, gain, shift):
    half = (value.astype(F32) - mean) * gain + shift
    return half + half * jnp.tanh(half)


def block_moments(blocks):
    sums, squares, sizes = [], [], []
    for block in blocks:
        n = block.shape[0]
        if n == 0:
            continue
        origin = jnp.mean(block[0:16], axis=0, keepdims=True)
        d = block - origin
        s = jnp.sum(d, axis=0, keepdims=True)
        q = jnp.sum(d * d, axis=0, keepdims=True)
        sums.append(s + float(n) * origin)
        squares.append(jnp.maximum(q - s * s / float(n), 0.0))
        sizes.append(n)
    total = functools.reduce(jnp.add, sums)
    mean = total / float(sum(sizes))
    out = functools.reduce(jnp.add, squares)
    for s, n in zip(sums, sizes):
        off = s / float(n) - mean
        out = out + float(n) * off * off
    return jnp.concatenate([total, out], axis=1)


def publish(ref, vector):
    for d in range(ROWS):
        ref[d] = vector


def next_col(v):
    col = lax.broadcasted_iota(jnp.int32, v.shape, 0) % W
    return jnp.where(col == W - 1, 0.0, pltpu.roll(v, v.shape[0] - 1, 0))


def last_col(v):
    col = lax.broadcasted_iota(jnp.int32, v.shape, 0) % W
    return jnp.where(col == 0, 0.0, pltpu.roll(v, 1, 0))


def edge_flags():
    row = lax.axis_index("rows")
    return row == 0, row == ROWS - 1


def mm(a, b):
    return jnp.dot(a, b, preferred_element_type=F32)


def coarse_stats_kernel(x_ref, out_ref, head_ref, tail_ref):
    x = x_ref[...].astype(F32).reshape(4 * W, 512)
    head_ref[...] = x_ref[0:2]
    tail_ref[...] = x_ref[2:4]
    publish(out_ref, block_moments([x]))


def pack_broad(k_ref, out_ref):
    rows = (((0,), (1, 2)), ((0, 1), (2,)))
    step = 128
    for a in range(2):
        for t in range(2):
            for c in range(0, 512, step):
                col = [
                    functools.reduce(
                        jnp.add, [k_ref[ky, kx, c : c + step, :].astype(F32) for ky in rows[a][t]]
                    )
                    for kx in range(3)
                ]
                for n, v in enumerate((col[0], col[1] + col[2], col[0] + col[1], col[2])):
                    out_ref[a, t * 512 + c : t * 512 + c + step, n * 256 : (n + 1) * 256] = v.astype(BF16)


def pack_detail(k_ref, x_ref, z_ref):
    rows = (((0,), (1, 2)), ((0, 1), (2,)))
    for a in range(2):
        for t in range(2):
            col = [
                functools.reduce(jnp.add, [k_ref[ky, kx].astype(F32) for ky in rows[a][t]])
                for kx in range(3)
            ]
            x_ref[a, t] = jnp.concatenate([col[0] + col[1], col[0]], axis=1).astype(BF16)
            z_ref[a, t] = jnp.concatenate([col[2], col[1] + col[2]], axis=1).astype(BF16)


def prepare_kernel_body(
    parts_ref, gain_hbm, shift_hbm, k_hbm, parts_out, gain_ref, shift_ref, w_ref, k_ref, sems
):
    pairs = ((gain_hbm, gain_ref), (shift_hbm, shift_ref)) + tuple((k_hbm.at[i], k_ref.at[i]) for i in range(3))
    copies = [pltpu.make_async_copy(src, dst, sems.at[i]) for i, (src, dst) in enumerate(pairs)]
    for copy in copies:
        copy.start()
    for d in range(ROWS):
        parts_out[d] = parts_ref[d]
    for copy in copies:
        copy.wait()
    pack_broad(k_ref, w_ref)


def broad_entry_kernel_body(
    x_ref, up_ref, down_ref, parts_ref, gain_ref, shift_ref, w_ref, out_ref, stat_ref, an
):
    first, last = edge_flags()
    mean, rate = moments([parts_ref], 4 * W)
    mean, gain, shift = mean[:1], 0.5 * rate[:1] * gain_ref[...], 0.5 * shift_ref[...]
    keep_up = jnp.where(first, 0.0, 1.0)
    keep_down = jnp.where(last, 0.0, 1.0)
    def norm(h):
        if h < 2:
            v = active(up_ref[h], mean, gain, shift) * keep_up
        elif h < 6:
            v = active(x_ref[h - 2], mean, gain, shift)
        else:
            v = active(down_ref[h - 6], mean, gain, shift) * keep_down
        an[h] = v.astype(BF16)

    ready, blocks, count = 0, [], 1
    for start in range(0, 6, count):
        while ready < start + count + 2:
            norm(ready)
            ready += 1
        lo, hi = max(start, 1) - start, min(start + count, 5) - start
        for a in range(2):
            near = an[start + a : start + a + count].reshape(count * W, 512)
            far = an[start + a + 1 : start + a + 1 + count].reshape(count * W, 512)
            both = jnp.concatenate([near, far], axis=1)
            for b in range(2):
                z = [mm(both, w_ref[a, :, n * 256 : (n + 1) * 256]) for n in (2 * b, 2 * b + 1)]
                v = last_col(z[0]) + z[1] if b == 0 else z[0] + next_col(z[1])
                for h in range(count):
                    out_ref[2 * (start + h) + a, :, b * 256 : (b + 1) * 256] = v[h * W : (h + 1) * W].astype(BF16)
                blocks.append(v[lo * W : hi * W])
    publish(stat_ref, block_moments(blocks))


def broad_inner_kernel_body(
    h_ref, x_ref, up_ref, down_ref, parts_ref, gain_ref, shift_ref, w_ref, p_ref,
    out_ref, send_ref, stat_ref, an, odd_line, even_line, rim,
):
    first, last = edge_flags()
    mean, rate = moments([parts_ref], 8 * 2 * W)
    mean, gain, shift = mean[:1], 0.5 * rate[:1] * gain_ref[...], 0.5 * shift_ref[...]
    mean, gain, shift = (tile_lanes(v, 2) for v in (mean, gain, shift))
    keep_up = jnp.where(first, 0.0, 1.0)
    keep_down = jnp.where(last, 0.0, 1.0)
    for i in range(12):
        v = active(h_ref[i], mean, gain, shift)
        if i < 2:
            v = v * keep_up
        elif i >= 10:
            v = v * keep_down
        an[i] = v.astype(BF16)
    skip_in = jnp.concatenate([up_ref[1]] + [x_ref[h] for h in range(4)] + [down_ref[0]], axis=0)
    skip = mm(skip_in, p_ref[...])
    w = w_ref
    even_w = jnp.concatenate([w[ky * 768 + 256 : ky * 768 + 768] for ky in range(3)], axis=0)
    odd_w = jnp.concatenate([w[ky * 768 : ky * 768 + 512] for ky in range(3)], axis=0)
    even_side = jnp.concatenate([w[ky * 768 : ky * 768 + 256] for ky in range(3)], axis=0)
    odd_side = jnp.concatenate([w[ky * 768 + 512 : ky * 768 + 768] for ky in range(3)], axis=0)
    evens, odds = [], []
    even_line[...] = jnp.zeros(even_line.shape, F32)
    rim[...] = jnp.zeros(rim.shape, F32)
    count = 5
    for j in range(0, 10, count):
        main = jnp.concatenate([an[j + ky : j + ky + count].reshape(count * W, 512) for ky in range(3)], axis=1)
        even_in = jnp.concatenate(
            [an[j + ky : j + ky + count, :, 0:256].reshape(count * W, 256) for ky in range(3)], axis=1
        )
        odd_in = jnp.concatenate(
            [an[j + ky : j + ky + count, :, 256:512].reshape(count * W, 256) for ky in range(3)], axis=1
        )
        extra = jnp.concatenate([skip[(i + 1) // 2 * W : ((i + 1) // 2 + 1) * W] for i in range(j, j + count)], axis=0)
        even = mm(main, even_w) + last_col(mm(odd_in, even_side)) + extra
        odd = mm(main, odd_w) + next_col(mm(even_in, odd_side)) + extra
        before = last_col(odd)
        for i in range(count):
            e, o, p = (v[i * W : (i + 1) * W] for v in (even, odd, before))
            out_ref[j + i, :, 0:256] = e.astype(BF16)
            out_ref[j + i, :, 256:512] = o.astype(BF16)
            block = jnp.concatenate([p.reshape(COLS, 8, 256), e.reshape(COLS, 8, 256)], axis=1)
            send_ref[:, (j + i) * 16 : (j + i + 1) * 16, :] = block.astype(BF16)
            for n in range(2):
                odd_line[i, n] = o[:, n * 128 : (n + 1) * 128]
                even_line[i, n, 0:W] = e[:, n * 128 : (n + 1) * 128]
                rim[n, pl.ds(j + i, COLS, stride=24), :] = odd_line[i, n, pl.ds(7, COLS, stride=8), :]
                rim[n, pl.ds(10 + j + i, COLS, stride=24), :] = even_line[i, n, pl.ds(8, COLS, stride=8), :]
        lo, hi = (W, count * W) if j == 0 else (0, (count - 1) * W)
        evens.append(even[lo:hi])
        odds.append(odd[lo:hi])
    for n in range(2):
        send_ref[:, 160:184, n * 128 : (n + 1) * 128] = rim[n].reshape(COLS, 24, 128).astype(BF16)
    stat_ref[...] = block_moments(evens + odds)


def detail_stats_kernel_body(
    x_ref, a_ref, b_ref, c_ref, d_ref, gain_ref, shift_ref, k_ref, stat_ref, norm_ref, an, wx_ref, wz_ref
):
    pack_detail(k_ref, wx_ref, wz_ref)
    first, last = edge_flags()
    mean, rate = moments([a_ref, b_ref, c_ref, d_ref], 8 * 2 * W)
    norm_ref[...] = jnp.concatenate([mean[:1], rate[:1]], axis=1)
    mean, gain, shift = mean[:1], 0.5 * rate[:1] * gain_ref[...], 0.5 * shift_ref[...]
    mean, gain, shift = (tile_lanes(v, 2) for v in (mean, gain, shift))
    keep_up = jnp.where(first, 0.0, 1.0)
    keep_down = jnp.where(last, 0.0, 1.0)
    for i in range(10):
        v = active(x_ref[i], mean, gain, shift)
        if i < 1:
            v = v * keep_up
        elif i >= 9:
            v = v * keep_down
        an[i] = v.astype(BF16)
    blocks = []
    for a in range(2):
        lhs = [an[a + t : a + t + 8].reshape(8 * W, 512) for t in range(2)]
        main = jnp.concatenate(lhs, axis=1)
        odd = jnp.concatenate([v[:, 256:512] for v in lhs], axis=1)
        even = jnp.concatenate([v[:, 0:256] for v in lhs], axis=1)
        wx = [wx_ref[a, t] for t in range(2)]
        wz = [wz_ref[a, t] for t in range(2)]
        middle = mm(main, jnp.concatenate([wx[0], wz[0], wx[1], wz[1]], axis=0))
        right = mm(odd, jnp.concatenate(wx, axis=0))
        left = mm(even, jnp.concatenate(wz, axis=0))
        q3 = right[:, 0:128] + next_col(left[:, 0:128])
        q0 = last_col(right[:, 128:256]) + left[:, 128:256]
        for v in (q3, q0, middle[:, 0:128], middle[:, 128:256]):
            blocks.append(v)
    stat_ref[...] = block_moments(blocks)


def summary_kernel_body(here_ref, there_ref, norm_ref, out_ref):
    mean, rate = moments([here_ref, there_ref], 16 * 4 * W)
    both = jnp.concatenate([mean[:1], rate[:1], norm_ref[...]], axis=1)
    for c in range(COLS):
        out_ref[c] = both


def pixel(j, u):
    if u == 15:
        return 160 + j
    if u == 16:
        return 170 + j
    return j * 16 + (8 + u // 2 if u % 2 == 0 else (u + 1) // 2)


def detail_kernel_body(
    x_ref, norm_ref, gain3_ref, shift3_ref, gain4_ref, shift4_ref, k3_ref, k4_ref, p_ref,
    out_ref, an3, an4, wx_ref, wz_ref, w_ref, tmp,
):
    step = pl.program_id(0)

    @pl.when(step == 0)
    def _():
        pack_detail(k3_ref, wx_ref, wz_ref)
        zero = jnp.zeros((128, 128), BF16)
        for ky in range(3):
            k = [k4_ref[ky, kx] for kx in range(3)]
            table = ((k[0], zero), (k[1], k[0]), (k[2], k[1]), (zero, k[2]))
            for i, pair in enumerate(table):
                at = ky * 512 + i * 128
                w_ref[at : at + 128, 0:128] = pair[0]
                w_ref[at : at + 128, 128:256] = pair[1]
        first, last = edge_flags()
        keep_up = jnp.where(first, 0.0, 1.0)
        keep_down = jnp.where(last, 0.0, 1.0)
        col = lax.axis_index("cols")
        keep_left = jnp.where(col == 0, 0.0, 1.0)
        keep_right = jnp.where(col == COLS - 1, 0.0, 1.0)
        norm = jnp.concatenate([norm_ref[i] for i in range(COLS)], axis=0)
        mean4, rate4 = (tile_lanes(norm[:, n * 128 : (n + 1) * 128], 2) for n in range(2))
        mean3, rate3 = norm[:, 256:512], norm[:, 512:768]
        gain3, shift3 = 0.5 * rate3 * gain3_ref[...], 0.5 * shift3_ref[...]
        gain4, shift4 = 0.5 * rate4 * tile_lanes(gain4_ref[...], 2), 0.5 * tile_lanes(shift4_ref[...], 2)
        for j in range(10):
            for u in range(-1, 17):
                v = active(x_ref[pixel(j, u)], mean3, gain3, shift3)
                if j == 0:
                    v = v * keep_up
                elif j == 9:
                    v = v * keep_down
                if u == -1:
                    v = v * keep_left
                elif u == 16:
                    v = v * keep_right
                an3[j, (u + 1) * 16 : (u + 2) * 16] = v.astype(BF16)
        size = 17 * 16
        count = 3
        lane = lax.broadcasted_iota(jnp.int32, (16, 256), 1)
        left_mask = jnp.where(lane < 128, keep_left, 1.0)
        right_mask = jnp.where(lane >= 128, keep_right, 1.0)
        for a in range(2):
            w = jnp.concatenate([wx_ref[a, 0], wz_ref[a, 0], wx_ref[a, 1], wz_ref[a, 1]], axis=0)
            for i in range(0, 9, count):
                lhs = jnp.concatenate(
                    [
                        an3[i + t : i + t + count, s : s + size].reshape(count * size, 256)
                        for t in range(2)
                        for s in (0, 16)
                    ],
                    axis=1,
                )
                v = mm(lhs, w).astype(BF16).reshape(count * 17, 16, 256)
                v = active(v, mean4, gain4, shift4)
                for n in range(count):
                    f = 2 * (i + n) + 1 - a
                    line = v[n * 17 : (n + 1) * 17]
                    if f == 0:
                        line = line * keep_up
                    elif f == 17:
                        line = line * keep_down
                    an4[f, 16 : size - 16] = line[1:16].reshape(15 * 16, 256).astype(BF16)
                    an4[f, 0:16] = (line[0] * left_mask).astype(BF16)
                    an4[f, size - 16 : size] = (line[16] * right_mask).astype(BF16)

    count = 4
    base = step * count
    lhs = jnp.concatenate(
        [an4[pl.ds(base + ky, count), s : s + 256].reshape(count * 256, 256) for ky in range(3) for s in (0, 16)],
        axis=1,
    )
    v = mm(lhs, w_ref[...])
    raw = []
    for n in range(count // 2):
        j = step * (count // 2) + n + 1
        raw += [x_ref[160 + j if u == 15 else j * 16 + (8 + u // 2 if u % 2 == 0 else (u + 1) // 2)] for u in range(16)]
    skip = mm(jnp.concatenate(raw, axis=0), p_ref[...])
    for n in range(count):
        for b in range(2):
            part = v[n * 256 : (n + 1) * 256, b * 128 : (b + 1) * 128] + skip[n // 2 * 256 : (n // 2 + 1) * 256]
            for u in range(16):
                at = (2 * u + b) * 16
                tmp[n, at : at + 16] = part[u * 16 : (u + 1) * 16]
        for image in range(16):
            out_ref[image, n] = tmp[n, pl.ds(image, 32, stride=16), :].astype(BF16)


def swap(parts):
    return lax.all_to_all(parts, "rows", 0, 0, tiled=True)


def across_z(v):
    return lax.ppermute(v, "rows", [(i, i ^ 1) for i in range(ROWS)])


def along_y(v):
    return [lax.ppermute(v, "rows", [(i, (i + 2 * k) % ROWS) for i in range(ROWS)]) for k in range(1, 4)]


def shape(*dims, dtype=BF16):
    return jax.ShapeDtypeStruct(dims, dtype)


def stay(v):
    return pltpu.with_memory_space_constraint(v, pltpu.HBM)


def line(v):
    return v.reshape(1, -1)


def body(
    coarse,
    broad_entry_scale,
    broad_entry_bias,
    broad_entry_kernel,
    broad_inner_scale,
    broad_inner_bias,
    broad_inner_kernel,
    broad_skip_projection,
    detail_entry_scale,
    detail_entry_bias,
    detail_entry_kernel,
    detail_inner_scale,
    detail_inner_bias,
    detail_inner_kernel,
    detail_skip_projection,
):
    x = coarse.reshape(4, W, 512)
    stat = lambda c: shape(ROWS, 1, 2 * c, dtype=F32)
    parts, head, tail = call(
        coarse_stats_kernel, (stat(512), shape(2, W, 512), shape(2, W, 512)), name="coarse_stats"
    )(x)
    up = lax.ppermute(tail, "rows", [(i, (i + 1) % ROWS) for i in range(ROWS)])
    down = lax.ppermute(head, "rows", [((i + 1) % ROWS, i) for i in range(ROWS)])
    parts, gain, shift, packed = call(
        prepare_kernel_body,
        (stat(512), shape(1, 512, dtype=F32), shape(1, 512, dtype=F32), shape(2, 1024, 1024)),
        [pltpu.VMEM((3, 3, 512, 256), BF16), pltpu.SemaphoreType.DMA((5,))],
        name="prepare",
        flops=1 << 30,
        specs=[VMEM] + [HBM] * 3,
    )(parts, *(stay(v) for v in (line(broad_entry_scale), line(broad_entry_bias), broad_entry_kernel)))
    parts = swap(parts)
    wide_h, parts = call(
        broad_entry_kernel_body,
        (shape(12, W, 512), stat(256)),
        [pltpu.VMEM((8, W, 512), BF16)],
        name="broad_entry",
        flops=1 << 32,
    )(x, up, down, parts, gain, shift, packed)
    parts = swap(parts)
    wide_out, send, part = call(
        broad_inner_kernel_body,
        (shape(10, W, 512), shape(COLS, 184, 256), shape(1, 512, dtype=F32)),
        [
            pltpu.VMEM((12, W, 512), BF16),
            pltpu.VMEM((5, 2, W, 128), F32),
            pltpu.VMEM((5, 2, W + 8, 128), F32),
            pltpu.VMEM((2, COLS * 24, 128), F32),
        ],
        name="broad_inner",
        flops=1 << 32,
    )(
        wide_h,
        x,
        up,
        down,
        parts,
        line(broad_inner_scale),
        line(broad_inner_bias),
        broad_inner_kernel.reshape(9 * 256, 256),
        broad_skip_projection,
    )
    pair = jnp.concatenate([part, across_z(part)], axis=0)
    send, pair = lax.optimization_barrier((send, pair))
    blocks = lax.all_to_all(send, "cols", 0, 0, tiled=True)
    part, norm = call(
        detail_stats_kernel_body,
        (shape(1, 256, dtype=F32), shape(1, 512, dtype=F32)),
        [pltpu.VMEM((10, W, 512), BF16)] + [pltpu.VMEM((2, 2, 256, 256), BF16)] * 2,
        name="detail_stats",
        flops=1 << 32,
    )(wide_out, pair, *along_y(pair), line(detail_entry_scale), line(detail_entry_bias), detail_entry_kernel)
    here = jnp.concatenate([part] + along_y(part), axis=0)
    there = across_z(here)
    norms = call(summary_kernel_body, shape(COLS, 1, 768, dtype=F32), name="summary")(here, there, norm)
    blocks, norms = lax.optimization_barrier((blocks, norms))
    norms = lax.all_to_all(norms, "cols", 0, 0, tiled=True)
    blocks = jnp.transpose(blocks, (1, 0, 2))
    operands = (
        blocks,
        norms,
        line(detail_entry_scale),
        line(detail_entry_bias),
        line(detail_inner_scale),
        line(detail_inner_bias),
        detail_entry_kernel,
        detail_inner_kernel,
        detail_skip_projection,
    )
    return pl.pallas_call(
        detail_kernel_body,
        grid=(4,),
        in_specs=[pl.BlockSpec(v.shape, functools.partial(lambda n, i: (0,) * n, v.ndim)) for v in operands],
        out_specs=pl.BlockSpec((COLS, 4, 32, 128), lambda i: (0, i, 0, 0)),
        out_shape=shape(COLS, 16, 32, 128),
        scratch_shapes=[
            pltpu.VMEM((10, 18 * 16, 256), BF16),
            pltpu.VMEM((18, 17 * 16, 256), BF16),
            pltpu.VMEM((2, 2, 256, 256), BF16),
            pltpu.VMEM((2, 2, 256, 256), BF16),
            pltpu.VMEM((1536, 256), BF16),
            pltpu.VMEM((4, 512, 128), F32),
        ],
        name="detail",
        cost_estimate=pl.CostEstimate(flops=1 << 33, bytes_accessed=0, transcendentals=0),
        compiler_params=pltpu.CompilerParams(vmem_limit_bytes=VMEM_LIMIT),
    )(*operands)


def solution(mesh):
    return jax.shard_map(
        body,
        mesh=mesh,
        in_specs=(P("cols", "rows", None, None),) + (P(),) * 14,
        out_specs=P(None, "rows", "cols", None),
        check_vma=False,
    )
```

time: 101 us -> 96.7 us (0.957)
  blocking collectives: 72.1 us -> 17.4 us
  starting transfers between devices: 5.07 us -> 27.1 us
  waiting for transfers between devices: 0.01 us -> 22 us
  Pallas kernels: 21.1 us -> 26.8 us
    all_to_all x1 -> x0, blocking collectives: 39.8 us -> none  [body(): return lax.all_to_all(decoded, 'cols', 0, 0, tiled=True)]
    all_to_all x0 -> x2, starting transfers between devices: none -> 18 us  [the longest x1 11 us: body(): blocks = lax.all_to_all(send, 'cols', 0, 0, tiled=True)]
    all_to_all x4 -> x2, blocking collectives: 32.3 us -> 17.4 us  [swap(): return lax.all_to_all(parts, 'rows', 0, 0, tiled=True)]
    ppermute x0 -> x8, waiting for transfers between devices: none -> 13 us  [the longest x6 7.69 us: along_y(): lax.ppermute(v, 'rows', [(i, (i + 2 * k) % ROWS) for i in range(ROWS)])]
    all_to_all x0 -> x2, waiting for transfers between devices: none -> 8.93 us  [the longest x1 5.57 us: body(): norms = lax.all_to_all(norms, 'cols', 0, 0, tiled=True)]
    pallas_call x3 -> x4, Pallas kernels: 13.9 us -> 19.5 us  [the longest x1 9.99 us: body(): pl.pallas_call(detail_kernel_body, grid=(4,), in_specs=[pl.BlockSpec(v.sh...]
    ppermute x0 -> x8, starting transfers between devices: none -> 4.07 us  [the longest x6 3.63 us: along_y(): lax.ppermute(v, 'rows', [(i, (i + 2 * k) % ROWS) for i in range(ROWS)])]
    optimization_barrier x0 -> x1, local copies, waits for them, and re-layouts: none -> 1.73 us  [body(): blocks, norms = lax.optimization_barrier((blocks, norms))]
  transfers between devices with their start and end apart: 2 -> 12, of which waited for: 0 -> 10; matrix products, arithmetic and copies ran while one was open for 0% -> 2% of each run, Pallas kernels for 2% -> 7%
where the time goes in v4:
time: 96.7 us; the launch traced here: 96.3 us
  starting transfers between devices  27.1 us (28%)
  Pallas kernels  26.8 us (28%)
  waiting for transfers between devices  22 us (23%)
  blocking collectives  17.4 us (18%)
  local copies, waits for them, and re-layouts  2.84 us (3%)
    all_to_all x2, blocking collectives, swap(): return lax.all_to_all(parts, 'rows', 0, 0, tiled=True)  17.4 us
    all_to_all x1, starting transfers between devices, body(): blocks = lax.all_to_all(send, 'cols', 0, 0, tiled=True)  11 us
    pallas_call x1, Pallas kernels, body(): pl.pallas_call(detail_kernel_body, grid=(4,), in_specs=[pl.BlockSpec(v.sh...  9.99 us
    ppermute x6, waiting for transfers between devices, along_y(): lax.ppermute(v, 'rows', [(i, (i + 2 * k) % ROWS) for i in range(ROWS)])  7.69 us
    all_to_all x1, starting transfers between devices, body(): norms = lax.all_to_all(norms, 'cols', 0, 0, tiled=True)  6.96 us
    all_to_all x1, waiting for transfers between devices, body(): norms = lax.all_to_all(norms, 'cols', 0, 0, tiled=True)  5.57 us
    pallas_call x1, Pallas kernels, body(): call(broad_inner_kernel_body, (shape(10, W, 512), shape(COLS, 184, 256),...  5.35 us
    ppermute x2, waiting for transfers between devices, across_z(): return lax.ppermute(v, 'rows', [(i, i ^ 1) for i in range(ROWS)])  5.33 us
  transfers between devices with their start and end apart: 12, of which 10 were waited for; matrix products, arithmetic and copies ran while one was open for 2% of the time, Pallas kernels for 7%

profile of v4, /device:TPU:1, one launch (start us, length us, event | category | flops | bytes accessed | tf_op | source)
XLA Modules:
  0.0 96.3 jit_solution(15805112905820055187)
XLA Ops:
  0.0 1.0 %copy-done = bf16[1,4,128,512]{3,2,1,0:T(8,128)(2,1)S(1)} copy-done((bf16[1,4,128,512]{3,2,1,0:T(8,128)(2,1)S(1)}, bf16[1,4,128,512]{3,2,1,0:T(8,128)(2,1)}, u32[]{:S(2)}) %copy-start) | copy-done | bytes 524312
  1.0 0.3 coarse_stats.1
  1.3 2.5 %collective-permute-start = (bf16[2,128,512]{2,1,0:T(8,128)(2,1)S(1)}, bf16[2,128,512]{2,1,0:T(8,128)(2,1)S(1)}, u32[]{:S(2)}, u32[]{:S(2)}) collective-permute-start(bf16[2,128,512]{2,1,0:T(8,128)(2,1)S(1)} %get-tuple-element.23), channel_id=1, source_target_pairs={{0,16},{16,32},{32,48},{48,64},{64,80},{80,96},{96,112},{112,0},{1... | collective-permute-start | bytes 786440 | tf_op jit(solution)/shard_map/ppermute | solution.py:452
  3.9 2.5 %collective-permute-start.1 = (bf16[2,128,512]{2,1,0:T(8,128)(2,1)S(1)}, bf16[2,128,512]{2,1,0:T(8,128)(2,1)S(1)}, u32[]{:S(2)}, u32[]{:S(2)}) collective-permute-start(bf16[2,128,512]{2,1,0:T(8,128)(2,1)S(1)} %get-tuple-element.24), channel_id=1, source_target_pairs={{16,0},{32,16},{48,32},{64,48},{80,64},{96,80},{112,96},{0,112},{1... | collective-permute-start | bytes 786440 | tf_op jit(solution)/shard_map/ppermute | solution.py:453
  6.4 2.5 %prepare.1 = (f32[8,1,1024]{2,1,0:T(1,128)S(1)}, f32[1,512]{1,0:T(1,128)S(1)}, f32[1,512]{1,0:T(1,128)S(1)}, bf16[2,1024,1024]{2,1,0:T(8,128)(2,1)S(1)}) custom-call(f32[8,1,1024]{2,1,0:T(1,128)S(1)} %get-tuple-element.25.parts_ref, f32[1,512]{1,0:T(1,128)} %bitcast.26, f32[1,512]{1,0:T(1,128)} %bitcast.27, bf16[3,3,512,256]{3,2,1,0:T(8,128)(2,1)} %k_hbm.1), custom_call_target="tpu_custom_call" | custom-call | flops 1073741824 | tf_op jit(solution)/shard_map/prepare/pallas_call | solution.py:454
  8.9 7.9 %all_to_all.20.parts_ref = f32[8,1,1024]{2,1,0:T(1,128)S(1)} all-to-all(f32[8,1,1024]{2,1,0:T(1,128)S(1)} %get-tuple-element.26), channel_id=1, replica_groups=mesh['rows'=8,'cols'=16] {'rows'}, dimensions={0} | all-to-all | bytes 65536 | tf_op jit(solution)/shard_map/all_to_all | solution.py:407
  16.9 0.0 copy-start.2
  16.9 4.5 %broad_entry.1 = (bf16[12,128,512]{2,1,0:T(8,128)(2,1)S(1)}, f32[8,1,512]{2,1,0:T(1,128)S(1)}) custom-call(bf16[4,128,512]{2,1,0:T(8,128)(2,1)S(1)} %bitcast.15, bf16[2,128,512]{2,1,0:T(8,128)(2,1)S(1)} %collective-permute-done.up_ref, bf16[2,128,512]{2,1,0:T(8,128)(2,1)S(1)} %collective-permute-done.1.down_ref, f32[8,1,1024]{2,1,0:T(1,128)S(1)} %all_to_all.20.parts_ref, ...), custom_call_target="tpu_custom_call" | custom-call | flops 4294967296 | tf_op jit(solution)/shard_map/broad_entry/pallas_call | solution.py:463
  21.4 9.5 %all_to_all.21.parts_ref = f32[8,1,512]{2,1,0:T(1,128)S(1)} all-to-all(f32[8,1,512]{2,1,0:T(1,128)S(1)} %get-tuple-element.31), channel_id=1, replica_groups=mesh['rows'=8,'cols'=16] {'rows'}, dimensions={0} | all-to-all | bytes 32768 | tf_op jit(solution)/shard_map/all_to_all | solution.py:407
  30.9 5.3 %broad_inner.1 = (bf16[10,128,512]{2,1,0:T(8,128)(2,1)S(1)}, bf16[16,184,256]{2,1,0:T(8,128)(2,1)}, f32[1,512]{1,0:T(1,128)S(1)}) custom-call(bf16[12,128,512]{2,1,0:T(8,128)(2,1)S(1)} %get-tuple-element.30.h_ref, bf16[4,128,512]{2,1,0:T(8,128)(2,1)S(1)} %bitcast.16, bf16[2,128,512]{2,1,0:T(8,128)(2,1)S(1)} %collective-permute-done.up_ref, ...), custom_call_target="tpu_custom_call" | custom-call | flops 4294967296 | tf_op jit(solution)/shard_map/broad_inner/pallas_call | solution.py:471
  36.3 0.4 collective-permute-start.2
  36.6 2.1 %collective-permute-done.2 = f32[1,512]{1,0:T(1,128)S(1)} collective-permute-done((f32[1,512]{1,0:T(1,128)S(1)}, f32[1,512]{1,0:T(1,128)S(1)}, u32[]{:S(2)}, u32[]{:S(2)}) %collective-permute-start.2) | collective-permute-done | bytes 2080 | tf_op jit(solution)/shard_map/ppermute | solution.py:411
  38.8 11.0 %all-to-all-start.2 = ((bf16[16,184,256]{2,1,0:T(8,128)(2,1)}), bf16[16,184,256]{2,1,0:T(8,128)(2,1)}, u32[]{:S(2)}, u32[]{:S(2)}) async-start(bf16[16,184,256]{2,1,0:T(8,128)(2,1)} %get-tuple-element.34), calls=%async_computation.2 | async-start | bytes 3014656 | tf_op jit(solution)/shard_map/all_to_all | solution.py:495
  49.8 0.9 collective-permute-start.5
  50.7 1.2 %collective-permute-start.4 = (f32[2,512]{1,0:T(2,128)S(1)}, f32[2,512]{1,0:T(2,128)S(1)}, u32[]{:S(2)}, u32[]{:S(2)}) collective-permute-start(f32[2,512]{1,0:T(2,128)S(1)} %pad_maximum_fusion.a_ref), channel_id=1, source_target_pairs={{0,64},{16,80},{32,96},{48,112},{64,0},{80,16},{96,32},{112,48},{1... | collective-permute-start | bytes 12296 | tf_op jit(solution)/shard_map/ppermute | solution.py:415
  51.9 0.4 collective-permute-done.5.d_ref
  52.2 2.8 %collective-permute-done.4.c_ref = f32[2,512]{1,0:T(2,128)S(1)} collective-permute-done((f32[2,512]{1,0:T(2,128)S(1)}, f32[2,512]{1,0:T(2,128)S(1)}, u32[]{:S(2)}, u32[]{:S(2)}) %collective-permute-start.4) | collective-permute-done | bytes 4128 | tf_op jit(solution)/shard_map/ppermute | solution.py:415
  55.0 0.9 collective-permute-done.3.b_ref
  55.9 3.2 %detail_stats.1 = (f32[1,256]{1,0:T(1,128)S(1)}, f32[1,512]{1,0:T(1,128)S(1)}) custom-call(bf16[10,128,512]{2,1,0:T(8,128)(2,1)S(1)} %get-tuple-element.35.x_ref, f32[2,512]{1,0:T(2,128)S(1)} %pad_maximum_fusion.a_ref, f32[2,512]{1,0:T(2,128)S(1)} %collective-permute-done.3.b_ref, f32[2,512]{1,0:T(2,128)S(1)} %collective-permute-done.4.c_ref, ...), custom_call_target="tpu_custom_call" | custom-call | flops 4294967296 | tf_op jit(solution)/shard_map/detail_stats/pallas_call | solution.py:496
  59.2 0.6 collective-permute-start.8
  59.8 0.9 collective-permute-start.7
  60.7 1.3 %collective-permute-done.8 = f32[1,256]{1,0:T(1,128)S(1)} collective-permute-done((f32[1,256]{1,0:T(1,128)S(1)}, f32[1,256]{1,0:T(1,128)S(1)}, u32[]{:S(2)}, u32[]{:S(2)}) %collective-permute-start.8) | collective-permute-done | bytes 1056 | tf_op jit(solution)/shard_map/ppermute | solution.py:415
  62.1 1.9 %collective-permute-done.7 = f32[1,256]{1,0:T(1,128)S(1)} collective-permute-done((f32[1,256]{1,0:T(1,128)S(1)}, f32[1,256]{1,0:T(1,128)S(1)}, u32[]{:S(2)}, u32[]{:S(2)}) %collective-permute-start.7) | collective-permute-done | bytes 1056 | tf_op jit(solution)/shard_map/ppermute | solution.py:415
  63.9 0.4 collective-permute-done.6
  64.4 0.1 collective-permute-start.9
  64.5 3.2 %collective-permute-done.9.there_ref = f32[4,256]{1,0:T(4,128)S(1)} collective-permute-done((f32[4,256]{1,0:T(4,128)S(1)}, f32[4,256]{1,0:T(4,128)S(1)}, u32[]{:S(2)}, u32[]{:S(2)}) %collective-permute-start.9) | collective-permute-done | bytes 4128 | tf_op jit(solution)/shard_map/ppermute | solution.py:411
  67.7 0.9 summary.1
  68.6 3.4 %all-to-all-done.2 = bf16[16,184,256]{2,1,0:T(8,128)(2,1)} async-done(((bf16[16,184,256]{2,1,0:T(8,128)(2,1)}), bf16[16,184,256]{2,1,0:T(8,128)(2,1)}, u32[]{:S(2)}, u32[]{:S(2)}) %all-to-all-start.2) | async-done | bytes 1507360 | tf_op jit(solution)/shard_map/all_to_all | solution.py:495
  72.0 7.0 %all-to-all-start.3 = ((f32[16,1,768]{2,1,0:T(1,128)}), f32[16,1,768]{2,1,0:T(1,128)S(1)}, u32[]{:S(2)}, u32[]{:S(2)}) async-start(f32[16,1,768]{2,1,0:T(1,128)} %summary.1), calls=%async_computation.3 | async-start | bytes 98304 | tf_op jit(solution)/shard_map/all_to_all | solution.py:507
  79.0 1.7 %copy.19 = bf16[16,184,256]{2,0,1:T(8,128)(2,1)S(1)} copy(bf16[16,184,256]{2,1,0:T(8,128)(2,1)} %all-to-all-done.2) | data formatting | bytes 3014656 | tf_op jit(solution)/shard_map/optimization_barrier | solution.py:506
  80.7 5.6 %all-to-all-done.3.norm_ref = f32[16,1,768]{2,1,0:T(1,128)S(1)} async-done(((f32[16,1,768]{2,1,0:T(1,128)}), f32[16,1,768]{2,1,0:T(1,128)S(1)}, u32[]{:S(2)}, u32[]{:S(2)}) %all-to-all-start.3) | async-done | bytes 49184 | tf_op jit(solution)/shard_map/all_to_all | solution.py:507
  86.3 10.0 %detail.1 = bf16[16,16,32,128]{3,2,1,0:T(8,128)(2,1)} custom-call(bf16[184,16,256]{2,1,0:T(8,128)(2,1)S(1)} %bitcast.13, f32[16,1,768]{2,1,0:T(1,128)S(1)} %all-to-all-done.3.norm_ref, f32[1,256]{1,0:T(1,128)S(1)} %bitcast.21, f32[1,256]{1,0:T(1,128)S(1)} %bitcast.23, f32[1,128]{1,0:T(1,128)S(1)} %bitcast.24, f32[1,128]{1,0:T(1,128)S(1)} %bitcast.25, ...), custom_call_target="tpu_custom_call" | custom-call | flops 8589934592 | tf_op jit(solution)/shard_map/detail/pallas_call | solution.py:520
  (30 shorter events, 0.1 us)
Async XLA Ops:
  0.0 1.0 %copy-start = (bf16[1,4,128,512]{3,2,1,0:T(8,128)(2,1)S(1)}, bf16[1,4,128,512]{3,2,1,0:T(8,128)(2,1)}, u32[]{:S(2)}) copy-start(bf16[1,4,128,512]{3,2,1,0:T(8,128)(2,1)} %param.15) | copy-start | bytes 1572868
  1.3 15.5 %collective-permute-start = (bf16[2,128,512]{2,1,0:T(8,128)(2,1)S(1)}, bf16[2,128,512]{2,1,0:T(8,128)(2,1)S(1)}, u32[]{:S(2)}, u32[]{:S(2)}) collective-permute-start(bf16[2,128,512]{2,1,0:T(8,128)(2,1)S(1)} %get-tuple-element.23), channel_id=1, source_target_pairs={{0,16},{16,32},{32,48},{48,64},{64,80},{80,96},{96,112},{112,0},{1... | collective-permute-start | bytes 786440 | tf_op jit(solution)/shard_map/ppermute | solution.py:452
  3.9 13.0 %collective-permute-start.1 = (bf16[2,128,512]{2,1,0:T(8,128)(2,1)S(1)}, bf16[2,128,512]{2,1,0:T(8,128)(2,1)S(1)}, u32[]{:S(2)}, u32[]{:S(2)}) collective-permute-start(bf16[2,128,512]{2,1,0:T(8,128)(2,1)S(1)} %get-tuple-element.24), channel_id=1, source_target_pairs={{16,0},{32,16},{48,32},{64,48},{80,64},{96,80},{112,96},{0,112},{1... | collective-permute-start | bytes 786440 | tf_op jit(solution)/shard_map/ppermute | solution.py:453
  6.4 10.4 %copy-start.1 = (bf16[1,4,128,512]{3,2,1,0:T(8,128)(2,1)S(1)}, bf16[1,4,128,512]{3,2,1,0:T(8,128)(2,1)}, u32[]{:S(2)}) copy-start(bf16[1,4,128,512]{3,2,1,0:T(8,128)(2,1)} %param.15) | copy-start | bytes 1572868
  16.9 14.1 %copy-start.2 = (bf16[3,3,256,256]{3,2,1,0:T(8,128)(2,1)S(1)}, bf16[3,3,256,256]{3,2,1,0:T(8,128)(2,1)}, u32[]{:S(2)}) copy-start(bf16[3,3,256,256]{3,2,1,0:T(8,128)(2,1)} %param.21) | copy-start | bytes 3538948
  16.9 14.0 %copy-start.5 = (bf16[512,256]{1,0:T(8,128)(2,1)S(1)}, bf16[512,256]{1,0:T(8,128)(2,1)}, u32[]{:S(2)}) copy-start(bf16[512,256]{1,0:T(8,128)(2,1)} %p_ref.2) | copy-start | bytes 786436
  16.9 14.0 %copy-start.7 = (f32[256]{0:T(256)S(1)}, f32[256]{0:T(256)}, u32[]{:S(2)}) copy-start(f32[256]{0:T(256)} %param.19) | copy-start | bytes 3076
  16.9 14.0 %copy-start.8 = (f32[256]{0:T(256)S(1)}, f32[256]{0:T(256)}, u32[]{:S(2)}) copy-start(f32[256]{0:T(256)} %param.20) | copy-start | bytes 3076
  36.3 2.4 %collective-permute-start.2 = (f32[1,512]{1,0:T(1,128)S(1)}, f32[1,512]{1,0:T(1,128)S(1)}, u32[]{:S(2)}, u32[]{:S(2)}) collective-permute-start(f32[1,512]{1,0:T(1,128)S(1)} %get-tuple-element.33), channel_id=1, source_target_pairs={{0,16},{16,0},{32,48},{48,32},{64,80},{80,64},{96,112},{112,96},{1... | collective-permute-start | bytes 6152 | tf_op jit(solution)/shard_map/ppermute | solution.py:411
  38.7 17.2 %copy-start.3 = (bf16[3,3,256,128]{3,2,1,0:T(8,128)(2,1)S(1)}, bf16[3,3,256,128]{3,2,1,0:T(8,128)(2,1)}, u32[]{:S(2)}) copy-start(bf16[3,3,256,128]{3,2,1,0:T(8,128)(2,1)} %k3_ref.1) | copy-start | bytes 1769476
  38.7 17.2 %copy-start.9 = (f32[256]{0:T(256)S(1)}, f32[256]{0:T(256)}, u32[]{:S(2)}) copy-start(f32[256]{0:T(256)} %param.23) | copy-start | bytes 3076
  38.8 17.2 %copy-start.10 = (f32[256]{0:T(256)S(1)}, f32[256]{0:T(256)}, u32[]{:S(2)}) copy-start(f32[256]{0:T(256)} %param.24) | copy-start | bytes 3076
  38.8 33.2 %all-to-all-start.2 = ((bf16[16,184,256]{2,1,0:T(8,128)(2,1)}), bf16[16,184,256]{2,1,0:T(8,128)(2,1)}, u32[]{:S(2)}, u32[]{:S(2)}) async-start(bf16[16,184,256]{2,1,0:T(8,128)(2,1)} %get-tuple-element.34), calls=%async_computation.2 | async-start | bytes 3014656 | tf_op jit(solution)/shard_map/all_to_all | solution.py:495
  49.8 2.5 %collective-permute-start.5 = (f32[2,512]{1,0:T(2,128)S(1)}, f32[2,512]{1,0:T(2,128)S(1)}, u32[]{:S(2)}, u32[]{:S(2)}) collective-permute-start(f32[2,512]{1,0:T(2,128)S(1)} %pad_maximum_fusion.a_ref), channel_id=1, source_target_pairs={{0,96},{16,112},{32,0},{48,16},{64,32},{80,48},{96,64},{112,80},{1... | collective-permute-start | bytes 12296 | tf_op jit(solution)/shard_map/ppermute | solution.py:415
  50.7 4.4 %collective-permute-start.4 = (f32[2,512]{1,0:T(2,128)S(1)}, f32[2,512]{1,0:T(2,128)S(1)}, u32[]{:S(2)}, u32[]{:S(2)}) collective-permute-start(f32[2,512]{1,0:T(2,128)S(1)} %pad_maximum_fusion.a_ref), channel_id=1, source_target_pairs={{0,64},{16,80},{32,96},{48,112},{64,0},{80,16},{96,32},{112,48},{1... | collective-permute-start | bytes 12296 | tf_op jit(solution)/shard_map/ppermute | solution.py:415
  51.8 4.1 %collective-permute-start.3 = (f32[2,512]{1,0:T(2,128)S(1)}, f32[2,512]{1,0:T(2,128)S(1)}, u32[]{:S(2)}, u32[]{:S(2)}) collective-permute-start(f32[2,512]{1,0:T(2,128)S(1)} %pad_maximum_fusion.a_ref), channel_id=1, source_target_pairs={{0,32},{16,48},{32,64},{48,80},{64,96},{80,112},{96,0},{112,16},{1... | collective-permute-start | bytes 12296 | tf_op jit(solution)/shard_map/ppermute | solution.py:415
  59.2 2.9 %collective-permute-start.8 = (f32[1,256]{1,0:T(1,128)S(1)}, f32[1,256]{1,0:T(1,128)S(1)}, u32[]{:S(2)}, u32[]{:S(2)}) collective-permute-start(f32[1,256]{1,0:T(1,128)S(1)} %get-tuple-element.37), channel_id=1, source_target_pairs={{0,96},{16,112},{32,0},{48,16},{64,32},{80,48},{96,64},{112,80},{1... | collective-permute-start | bytes 3080 | tf_op jit(solution)/shard_map/ppermute | solution.py:415
  59.8 4.1 %collective-permute-start.7 = (f32[1,256]{1,0:T(1,128)S(1)}, f32[1,256]{1,0:T(1,128)S(1)}, u32[]{:S(2)}, u32[]{:S(2)}) collective-permute-start(f32[1,256]{1,0:T(1,128)S(1)} %get-tuple-element.37), channel_id=1, source_target_pairs={{0,64},{16,80},{32,96},{48,112},{64,0},{80,16},{96,32},{112,48},{1... | collective-permute-start | bytes 3080 | tf_op jit(solution)/shard_map/ppermute | solution.py:415
  60.7 3.6 %collective-permute-start.6 = (f32[1,256]{1,0:T(1,128)S(1)}, f32[1,256]{1,0:T(1,128)S(1)}, u32[]{:S(2)}, u32[]{:S(2)}) collective-permute-start(f32[1,256]{1,0:T(1,128)S(1)} %get-tuple-element.37), channel_id=1, source_target_pairs={{0,32},{16,48},{32,64},{48,80},{64,96},{80,112},{96,0},{112,16},{1... | collective-permute-start | bytes 3080 | tf_op jit(solution)/shard_map/ppermute | solution.py:415
  64.4 3.3 %collective-permute-start.9 = (f32[4,256]{1,0:T(4,128)S(1)}, f32[4,256]{1,0:T(4,128)S(1)}, u32[]{:S(2)}, u32[]{:S(2)}) collective-permute-start(f32[4,256]{1,0:T(4,128)S(1)} %pad_maximum_fusion.1.here_ref), channel_id=1, source_target_pairs={{0,16},{16,0},{32,48},{48,32},{64,80},{80,64},{96,112},{112,96},{1... | collective-permute-start | bytes 12296 | tf_op jit(solution)/shard_map/ppermute | solution.py:411
  72.0 14.3 %all-to-all-start.3 = ((f32[16,1,768]{2,1,0:T(1,128)}), f32[16,1,768]{2,1,0:T(1,128)S(1)}, u32[]{:S(2)}, u32[]{:S(2)}) async-start(f32[16,1,768]{2,1,0:T(1,128)} %summary.1), calls=%async_computation.3 | async-start | bytes 98304 | tf_op jit(solution)/shard_map/all_to_all | solution.py:507
  79.0 7.4 %copy-start.4 = (bf16[3,3,128,128]{3,2,1,0:T(8,128)(2,1)S(1)}, bf16[3,3,128,128]{3,2,1,0:T(8,128)(2,1)}, u32[]{:S(2)}) copy-start(bf16[3,3,128,128]{3,2,1,0:T(8,128)(2,1)} %k4_ref.1) | copy-start | bytes 884740
  79.0 7.3 %copy-start.6 = (bf16[256,128]{1,0:T(8,128)(2,1)S(1)}, bf16[256,128]{1,0:T(8,128)(2,1)}, u32[]{:S(2)}) copy-start(bf16[256,128]{1,0:T(8,128)(2,1)} %p_ref.3) | copy-start | bytes 196612
  79.0 7.3 %copy-start.11 = (f32[128]{0:T(128)S(1)}, f32[128]{0:T(128)}, u32[]{:S(2)}) copy-start(f32[128]{0:T(128)} %param.26) | copy-start | bytes 1540
  79.0 7.3 %copy-start.12 = (f32[128]{0:T(128)S(1)}, f32[128]{0:T(128)}, u32[]{:S(2)}) copy-start(f32[128]{0:T(128)} %param.27) | copy-start | bytes 1540

commit v5 on v4

--- a/solution.py
+++ b/solution.py
@@ -21,11 +21,12 @@
 HBM = pl.BlockSpec(memory_space=pltpu.HBM)
 
 
-def call(kernel, out_shape, scratch=(), flops=0, name=None, specs=None):
+def call(kernel, out_shape, scratch=(), flops=0, name=None, specs=None, outs=None):
     return pl.pallas_call(
         kernel,
         out_shape=out_shape,
         **({} if specs is None else {"in_specs": specs}),
+        **({} if outs is None else {"out_specs": outs}),
         scratch_shapes=list(scratch),
         name=name,
         cost_estimate=pl.CostEstimate(flops=flops, bytes_accessed=0, transcendentals=0),
@@ -204,7 +205,7 @@
 
 def broad_inner_kernel_body(
     h_ref, x_ref, up_ref, down_ref, parts_ref, gain_ref, shift_ref, w_ref, p_ref,
-    out_ref, send_ref, stat_ref, an, odd_line, even_line, rim,
+    out_ref, send_hbm, stat_ref, an, odd_line, even_line, rim, send_ref, sems,
 ):
     first, last = edge_flags()
     mean, rate = moments([parts_ref], 8 * 2 * W)
@@ -212,13 +213,14 @@
     mean, gain, shift = (tile_lanes(v, 2) for v in (mean, gain, shift))
     keep_up = jnp.where(first, 0.0, 1.0)
     keep_down = jnp.where(last, 0.0, 1.0)
-    for i in range(12):
+    def norm(i):
         v = active(h_ref[i], mean, gain, shift)
         if i < 2:
             v = v * keep_up
         elif i >= 10:
             v = v * keep_down
         an[i] = v.astype(BF16)
+
     skip_in = jnp.concatenate([up_ref[1]] + [x_ref[h] for h in range(4)] + [down_ref[0]], axis=0)
     skip = mm(skip_in, p_ref[...])
     w = w_ref
@@ -226,11 +228,20 @@
     odd_w = jnp.concatenate([w[ky * 768 : ky * 768 + 512] for ky in range(3)], axis=0)
     even_side = jnp.concatenate([w[ky * 768 : ky * 768 + 256] for ky in range(3)], axis=0)
     odd_side = jnp.concatenate([w[ky * 768 + 512 : ky * 768 + 768] for ky in range(3)], axis=0)
-    evens, odds = [], []
+    copies = []
+
+    def ship(at, size):
+        rows = pl.ds(at, size)
+        copies.append(pltpu.make_async_copy(send_ref.at[:, rows], send_hbm.at[:, rows], sems.at[len(copies)]))
+        copies[-1].start()
+
+    blocks, ready, count = [], 0, 2
     even_line[...] = jnp.zeros(even_line.shape, F32)
     rim[...] = jnp.zeros(rim.shape, F32)
-    count = 5
     for j in range(0, 10, count):
+        while ready < j + count + 2:
+            norm(ready)
+            ready += 1
         main = jnp.concatenate([an[j + ky : j + ky + count].reshape(count * W, 512) for ky in range(3)], axis=1)
         even_in = jnp.concatenate(
             [an[j + ky : j + ky + count, :, 0:256].reshape(count * W, 256) for ky in range(3)], axis=1
@@ -253,12 +264,16 @@
                 even_line[i, n, 0:W] = e[:, n * 128 : (n + 1) * 128]
                 rim[n, pl.ds(j + i, COLS, stride=24), :] = odd_line[i, n, pl.ds(7, COLS, stride=8), :]
                 rim[n, pl.ds(10 + j + i, COLS, stride=24), :] = even_line[i, n, pl.ds(8, COLS, stride=8), :]
-        lo, hi = (W, count * W) if j == 0 else (0, (count - 1) * W)
-        evens.append(even[lo:hi])
-        odds.append(odd[lo:hi])
+        lo, hi = max(j, 1) - j, min(j + count, 9) - j
+        blocks += [even[lo * W : hi * W], odd[lo * W : hi * W]]
+        if j in (2, 6):
+            ship((j - 2) * 16, 64)
     for n in range(2):
         send_ref[:, 160:184, n * 128 : (n + 1) * 128] = rim[n].reshape(COLS, 24, 128).astype(BF16)
-    stat_ref[...] = block_moments(evens + odds)
+    ship(128, 56)
+    stat_ref[...] = block_moments(blocks)
+    for copy in copies:
+        copy.wait()
 
 
 def detail_stats_kernel_body(
@@ -312,95 +327,112 @@
     return j * 16 + (8 + u // 2 if u % 2 == 0 else (u + 1) // 2)
 
 
+PLAN = (('entry', 0, 3), ('entry', 3, 3), ('entry', 6, 3), ('inner', 0, 4), ('inner', 4, 4), ('send', 0, 8), ('inner', 8, 4), ('inner', 12, 4), ('send', 8, 8))
+
+
 def detail_kernel_body(
     x_ref, norm_ref, gain3_ref, shift3_ref, gain4_ref, shift4_ref, k3_ref, k4_ref, p_ref,
-    out_ref, an3, an4, wx_ref, wz_ref, w_ref, tmp,
+    out_hbm, an3, an4, wx_ref, wz_ref, w_ref, tmp, out_ref, sems,
 ):
-    step = pl.program_id(0)
-
-    @pl.when(step == 0)
-    def _():
-        pack_detail(k3_ref, wx_ref, wz_ref)
-        zero = jnp.zeros((128, 128), BF16)
-        for ky in range(3):
-            k = [k4_ref[ky, kx] for kx in range(3)]
-            table = ((k[0], zero), (k[1], k[0]), (k[2], k[1]), (zero, k[2]))
-            for i, pair in enumerate(table):
-                at = ky * 512 + i * 128
-                w_ref[at : at + 128, 0:128] = pair[0]
-                w_ref[at : at + 128, 128:256] = pair[1]
-        first, last = edge_flags()
-        keep_up = jnp.where(first, 0.0, 1.0)
-        keep_down = jnp.where(last, 0.0, 1.0)
-        col = lax.axis_index("cols")
-        keep_left = jnp.where(col == 0, 0.0, 1.0)
-        keep_right = jnp.where(col == COLS - 1, 0.0, 1.0)
-        norm = jnp.concatenate([norm_ref[i] for i in range(COLS)], axis=0)
-        mean4, rate4 = (tile_lanes(norm[:, n * 128 : (n + 1) * 128], 2) for n in range(2))
-        mean3, rate3 = norm[:, 256:512], norm[:, 512:768]
-        gain3, shift3 = 0.5 * rate3 * gain3_ref[...], 0.5 * shift3_ref[...]
-        gain4, shift4 = 0.5 * rate4 * tile_lanes(gain4_ref[...], 2), 0.5 * tile_lanes(shift4_ref[...], 2)
-        for j in range(10):
-            for u in range(-1, 17):
-                v = active(x_ref[pixel(j, u)], mean3, gain3, shift3)
-                if j == 0:
-                    v = v * keep_up
-                elif j == 9:
-                    v = v * keep_down
-                if u == -1:
-                    v = v * keep_left
-                elif u == 16:
-                    v = v * keep_right
-                an3[j, (u + 1) * 16 : (u + 2) * 16] = v.astype(BF16)
-        size = 17 * 16
-        count = 3
-        lane = lax.broadcasted_iota(jnp.int32, (16, 256), 1)
-        left_mask = jnp.where(lane < 128, keep_left, 1.0)
-        right_mask = jnp.where(lane >= 128, keep_right, 1.0)
+    pack_detail(k3_ref, wx_ref, wz_ref)
+    zero = jnp.zeros((128, 128), BF16)
+    for ky in range(3):
+        k = [k4_ref[ky, kx] for kx in range(3)]
+        table = ((k[0], zero), (k[1], k[0]), (k[2], k[1]), (zero, k[2]))
+        for i, pair in enumerate(table):
+            at = ky * 512 + i * 128
+            w_ref[at : at + 128, 0:128] = pair[0]
+            w_ref[at : at + 128, 128:256] = pair[1]
+    first, last = edge_flags()
+    keep_up = jnp.where(first, 0.0, 1.0)
+    keep_down = jnp.where(last, 0.0, 1.0)
+    col = lax.axis_index("cols")
+    keep_left = jnp.where(col == 0, 0.0, 1.0)
+    keep_right = jnp.where(col == COLS - 1, 0.0, 1.0)
+    norm = jnp.concatenate([norm_ref[i] for i in range(COLS)], axis=0)
+    mean4, rate4 = (tile_lanes(norm[:, n * 128 : (n + 1) * 128], 2) for n in range(2))
+    mean3, rate3 = norm[:, 256:512], norm[:, 512:768]
+    gain3, shift3 = 0.5 * rate3 * gain3_ref[...], 0.5 * shift3_ref[...]
+    gain4, shift4 = 0.5 * rate4 * tile_lanes(gain4_ref[...], 2), 0.5 * tile_lanes(shift4_ref[...], 2)
+    def norm3(j):
+        for u in range(-1, 17):
+            v = active(x_ref[pixel(j, u)], mean3, gain3, shift3)
+            if j == 0:
+                v = v * keep_up
+            elif j == 9:
+                v = v * keep_down
+            if u == -1:
+                v = v * keep_left
+            elif u == 16:
+                v = v * keep_right
+            an3[j, (u + 1) * 16 : (u + 2) * 16] = v.astype(BF16)
+
+    size = 17 * 16
+    lane = lax.broadcasted_iota(jnp.int32, (16, 256), 1)
+    left_mask = jnp.where(lane < 128, keep_left, 1.0)
+    right_mask = jnp.where(lane >= 128, keep_right, 1.0)
+
+    def entry(i, count):
+        lhs = jnp.concatenate(
+            [
+                an3[i + t : i + t + count, s : s + size].reshape(count * size, 256)
+                for t in range(2)
+                for s in (0, 16)
+            ],
+            axis=1,
+        )
         for a in range(2):
             w = jnp.concatenate([wx_ref[a, 0], wz_ref[a, 0], wx_ref[a, 1], wz_ref[a, 1]], axis=0)
-            for i in range(0, 9, count):
-                lhs = jnp.concatenate(
-                    [
-                        an3[i + t : i + t + count, s : s + size].reshape(count * size, 256)
-                        for t in range(2)
-                        for s in (0, 16)
-                    ],
-                    axis=1,
-                )
-                v = mm(lhs, w).astype(BF16).reshape(count * 17, 16, 256)
-                v = active(v, mean4, gain4, shift4)
-                for n in range(count):
-                    f = 2 * (i + n) + 1 - a
-                    line = v[n * 17 : (n + 1) * 17]
-                    if f == 0:
-                        line = line * keep_up
-                    elif f == 17:
-                        line = line * keep_down
-                    an4[f, 16 : size - 16] = line[1:16].reshape(15 * 16, 256).astype(BF16)
-                    an4[f, 0:16] = (line[0] * left_mask).astype(BF16)
-                    an4[f, size - 16 : size] = (line[16] * right_mask).astype(BF16)
-
-    count = 4
-    base = step * count
-    lhs = jnp.concatenate(
-        [an4[pl.ds(base + ky, count), s : s + 256].reshape(count * 256, 256) for ky in range(3) for s in (0, 16)],
-        axis=1,
-    )
-    v = mm(lhs, w_ref[...])
-    raw = []
-    for n in range(count // 2):
-        j = step * (count // 2) + n + 1
-        raw += [x_ref[160 + j if u == 15 else j * 16 + (8 + u // 2 if u % 2 == 0 else (u + 1) // 2)] for u in range(16)]
-    skip = mm(jnp.concatenate(raw, axis=0), p_ref[...])
-    for n in range(count):
-        for b in range(2):
-            part = v[n * 256 : (n + 1) * 256, b * 128 : (b + 1) * 128] + skip[n // 2 * 256 : (n // 2 + 1) * 256]
-            for u in range(16):
-                at = (2 * u + b) * 16
-                tmp[n, at : at + 16] = part[u * 16 : (u + 1) * 16]
-        for image in range(16):
-            out_ref[image, n] = tmp[n, pl.ds(image, 32, stride=16), :].astype(BF16)
+            v = mm(lhs, w).astype(BF16).reshape(count * 17, 16, 256)
+            v = active(v, mean4, gain4, shift4)
+            for n in range(count):
+                f = 2 * (i + n) + 1 - a
+                line = v[n * 17 : (n + 1) * 17]
+                if f == 0:
+                    line = line * keep_up
+                elif f == 17:
+                    line = line * keep_down
+                an4[f, 16 : size - 16] = line[1:16].reshape(15 * 16, 256).astype(BF16)
+                an4[f, 0:16] = (line[0] * left_mask).astype(BF16)
+                an4[f, size - 16 : size] = (line[16] * right_mask).astype(BF16)
+
+    def inner(base, count):
+        lhs = jnp.concatenate(
+            [an4[base + ky : base + ky + count, s : s + 256].reshape(count * 256, 256) for ky in range(3) for s in (0, 16)],
+            axis=1,
+        )
+        v = mm(lhs, w_ref[...])
+        raw = [x_ref[pixel(j, u)] for j in range(base // 2 + 1, (base + count) // 2 + 1) for u in range(16)]
+        skip = mm(jnp.concatenate(raw, axis=0), p_ref[...])
+        for n in range(count):
+            for b in range(2):
+                part = v[n * 256 : (n + 1) * 256, b * 128 : (b + 1) * 128] + skip[n // 2 * 256 : (n // 2 + 1) * 256]
+                for u in range(16):
+                    at = (2 * u + b) * 16
+                    tmp[n, at : at + 16] = part[u * 16 : (u + 1) * 16]
+            for image in range(16):
+                out_ref[image, base + n] = tmp[n, pl.ds(image, 32, stride=16), :].astype(BF16)
+
+    copies = []
+
+    def send(base, count):
+        rows = pl.ds(base, count)
+        copies.append(pltpu.make_async_copy(out_ref.at[:, rows], out_hbm.at[:, rows], sems.at[len(copies)]))
+        copies[-1].start()
+
+    ready = 0
+    for kind, base, count in PLAN:
+        if kind == "entry":
+            while ready < base + count + 1:
+                norm3(ready)
+                ready += 1
+            entry(base, count)
+        elif kind == "inner":
+            inner(base, count)
+        else:
+            send(base, count)
+    for copy in copies:
+        copy.wait()
 
 
 def swap(parts):
@@ -425,6 +457,28 @@
 
 def line(v):
     return v.reshape(1, -1)
+
+
+def detail_call(*operands):
+    return pl.pallas_call(
+        detail_kernel_body,
+        in_specs=[VMEM] * len(operands),
+        out_specs=HBM,
+        out_shape=shape(COLS, 16, 32, 128),
+        scratch_shapes=[
+            pltpu.VMEM((10, 18 * 16, 256), BF16),
+            pltpu.VMEM((18, 17 * 16, 256), BF16),
+            pltpu.VMEM((2, 2, 256, 256), BF16),
+            pltpu.VMEM((2, 2, 256, 256), BF16),
+            pltpu.VMEM((1536, 256), BF16),
+            pltpu.VMEM((8, 512, 128), F32),
+            pltpu.VMEM((COLS, 16, 32, 128), BF16),
+            pltpu.SemaphoreType.DMA((6,)),
+        ],
+        name="detail",
+        cost_estimate=pl.CostEstimate(flops=1 << 33, bytes_accessed=0, transcendentals=0),
+        compiler_params=pltpu.CompilerParams(vmem_limit_bytes=VMEM_LIMIT),
+    )(*operands)
 
 
 def body(
@@ -476,9 +530,12 @@
             pltpu.VMEM((5, 2, W, 128), F32),
             pltpu.VMEM((5, 2, W + 8, 128), F32),
             pltpu.VMEM((2, COLS * 24, 128), F32),
+            pltpu.VMEM((COLS, 184, 256), BF16),
+            pltpu.SemaphoreType.DMA((3,)),
         ],
         name="broad_inner",
         flops=1 << 32,
+        outs=(VMEM, HBM, VMEM),
     )(
         wide_h,
         x,
@@ -506,7 +563,7 @@
     blocks, norms = lax.optimization_barrier((blocks, norms))
     norms = lax.all_to_all(norms, "cols", 0, 0, tiled=True)
     blocks = jnp.transpose(blocks, (1, 0, 2))
-    operands = (
+    return detail_call(
         blocks,
         norms,
         line(detail_entry_scale),
@@ -517,24 +574,6 @@
         detail_inner_kernel,
         detail_skip_projection,
     )
-    return pl.pallas_call(
-        detail_kernel_body,
-        grid=(4,),
-        in_specs=[pl.BlockSpec(v.shape, functools.partial(lambda n, i: (0,) * n, v.ndim)) for v in operands],
-        out_specs=pl.BlockSpec((COLS, 4, 32, 128), lambda i: (0, i, 0, 0)),
-        out_shape=shape(COLS, 16, 32, 128),
-        scratch_shapes=[
-            pltpu.VMEM((10, 18 * 16, 256), BF16),
-            pltpu.VMEM((18, 17 * 16, 256), BF16),
-            pltpu.VMEM((2, 2, 256, 256), BF16),
-            pltpu.VMEM((2, 2, 256, 256), BF16),
-            pltpu.VMEM((1536, 256), BF16),
-            pltpu.VMEM((4, 512, 128), F32),
-        ],
-        name="detail",
-        cost_estimate=pl.CostEstimate(flops=1 << 33, bytes_accessed=0, transcendentals=0),
-        compiler_params=pltpu.CompilerParams(vmem_limit_bytes=VMEM_LIMIT),
-    )(*operands)
 
 
 def solution(mesh):

time: 96.7 us -> 95.7 us (0.990)
  Pallas kernels: 26.8 us -> 25.5 us
    pallas_call x1, Pallas kernels: 9.99 us -> 8.98 us  [detail_call(): pl.pallas_call(detail_kernel_body, in_specs=[VMEM] * len(operands), out_s...]
where the time goes in v5:
time: 95.7 us; the launch traced here: 95.3 us
  starting transfers between devices  27.2 us (28%)
  Pallas kernels  25.5 us (27%)
  waiting for transfers between devices  22 us (23%)
  blocking collectives  17.4 us (18%)
  local copies, waits for them, and re-layouts  2.84 us (3%)
    all_to_all x2, blocking collectives, swap(): return lax.all_to_all(parts, 'rows', 0, 0, tiled=True)  17.4 us
    all_to_all x1, starting transfers between devices, body(): blocks = lax.all_to_all(send, 'cols', 0, 0, tiled=True)  11 us
    pallas_call x1, Pallas kernels, detail_call(): pl.pallas_call(detail_kernel_body, in_specs=[VMEM] * len(operands), out_s...  8.98 us
    ppermute x6, waiting for transfers between devices, along_y(): lax.ppermute(v, 'rows', [(i, (i + 2 * k) % ROWS) for i in range(ROWS)])  7.69 us
    all_to_all x1, starting transfers between devices, body(): norms = lax.all_to_all(norms, 'cols', 0, 0, tiled=True)  6.96 us
    all_to_all x1, waiting for transfers between devices, body(): norms = lax.all_to_all(norms, 'cols', 0, 0, tiled=True)  5.57 us
    ppermute x2, waiting for transfers between devices, across_z(): return lax.ppermute(v, 'rows', [(i, i ^ 1) for i in range(ROWS)])  5.34 us
    pallas_call x1, Pallas kernels, body(): call(broad_inner_kernel_body, (shape(10, W, 512), shape(COLS, 184, 256),...  5.06 us
  transfers between devices with their start and end apart: 12, of which 10 were waited for; matrix products, arithmetic and copies ran while one was open for 2% of the time, Pallas kernels for 7%

profile of v5, /device:TPU:1, one launch (start us, length us, event | category | flops | bytes accessed | tf_op | source)
XLA Modules:
  0.0 95.3 jit_solution(13055261048353625422)
XLA Ops:
  0.0 1.0 %copy-done = bf16[1,4,128,512]{3,2,1,0:T(8,128)(2,1)S(1)} copy-done((bf16[1,4,128,512]{3,2,1,0:T(8,128)(2,1)S(1)}, bf16[1,4,128,512]{3,2,1,0:T(8,128)(2,1)}, u32[]{:S(2)}) %copy-start) | copy-done | bytes 524312
  1.0 0.3 coarse_stats.1
  1.3 2.5 %collective-permute-start = (bf16[2,128,512]{2,1,0:T(8,128)(2,1)S(1)}, bf16[2,128,512]{2,1,0:T(8,128)(2,1)S(1)}, u32[]{:S(2)}, u32[]{:S(2)}) collective-permute-start(bf16[2,128,512]{2,1,0:T(8,128)(2,1)S(1)} %get-tuple-element.23), channel_id=1, source_target_pairs={{0,16},{16,32},{32,48},{48,64},{64,80},{80,96},{96,112},{112,0},{1... | collective-permute-start | bytes 786440 | tf_op jit(solution)/shard_map/ppermute | solution.py:506
  3.9 2.5 %collective-permute-start.1 = (bf16[2,128,512]{2,1,0:T(8,128)(2,1)S(1)}, bf16[2,128,512]{2,1,0:T(8,128)(2,1)S(1)}, u32[]{:S(2)}, u32[]{:S(2)}) collective-permute-start(bf16[2,128,512]{2,1,0:T(8,128)(2,1)S(1)} %get-tuple-element.24), channel_id=1, source_target_pairs={{16,0},{32,16},{48,32},{64,48},{80,64},{96,80},{112,96},{0,112},{1... | collective-permute-start | bytes 786440 | tf_op jit(solution)/shard_map/ppermute | solution.py:507
  6.4 2.5 %prepare.1 = (f32[8,1,1024]{2,1,0:T(1,128)S(1)}, f32[1,512]{1,0:T(1,128)S(1)}, f32[1,512]{1,0:T(1,128)S(1)}, bf16[2,1024,1024]{2,1,0:T(8,128)(2,1)S(1)}) custom-call(f32[8,1,1024]{2,1,0:T(1,128)S(1)} %get-tuple-element.25.parts_ref, f32[1,512]{1,0:T(1,128)} %bitcast.26, f32[1,512]{1,0:T(1,128)} %bitcast.27, bf16[3,3,512,256]{3,2,1,0:T(8,128)(2,1)} %k_hbm.1), custom_call_target="tpu_custom_call" | custom-call | flops 1073741824 | tf_op jit(solution)/shard_map/prepare/pallas_call | solution.py:508
  8.9 7.9 %all_to_all.20.parts_ref = f32[8,1,1024]{2,1,0:T(1,128)S(1)} all-to-all(f32[8,1,1024]{2,1,0:T(1,128)S(1)} %get-tuple-element.26), channel_id=1, replica_groups=mesh['rows'=8,'cols'=16] {'rows'}, dimensions={0} | all-to-all | bytes 65536 | tf_op jit(solution)/shard_map/all_to_all | solution.py:439
  16.9 0.0 copy-start.2
  16.9 4.5 %broad_entry.1 = (bf16[12,128,512]{2,1,0:T(8,128)(2,1)S(1)}, f32[8,1,512]{2,1,0:T(1,128)S(1)}) custom-call(bf16[4,128,512]{2,1,0:T(8,128)(2,1)S(1)} %bitcast.15, bf16[2,128,512]{2,1,0:T(8,128)(2,1)S(1)} %collective-permute-done.up_ref, bf16[2,128,512]{2,1,0:T(8,128)(2,1)S(1)} %collective-permute-done.1.down_ref, f32[8,1,1024]{2,1,0:T(1,128)S(1)} %all_to_all.20.parts_ref, ...), custom_call_target="tpu_custom_call" | custom-call | flops 4294967296 | tf_op jit(solution)/shard_map/broad_entry/pallas_call | solution.py:517
  21.4 9.5 %all_to_all.21.parts_ref = f32[8,1,512]{2,1,0:T(1,128)S(1)} all-to-all(f32[8,1,512]{2,1,0:T(1,128)S(1)} %get-tuple-element.31), channel_id=1, replica_groups=mesh['rows'=8,'cols'=16] {'rows'}, dimensions={0} | all-to-all | bytes 32768 | tf_op jit(solution)/shard_map/all_to_all | solution.py:439
  30.9 5.1 %broad_inner.1 = (bf16[10,128,512]{2,1,0:T(8,128)(2,1)S(1)}, bf16[16,184,256]{2,1,0:T(8,128)(2,1)}, f32[1,512]{1,0:T(1,128)S(1)}) custom-call(bf16[12,128,512]{2,1,0:T(8,128)(2,1)S(1)} %get-tuple-element.30.h_ref, bf16[4,128,512]{2,1,0:T(8,128)(2,1)S(1)} %bitcast.16, bf16[2,128,512]{2,1,0:T(8,128)(2,1)S(1)} %collective-permute-done.up_ref, ...), custom_call_target="tpu_custom_call" | custom-call | flops 4294967296 | tf_op jit(solution)/shard_map/broad_inner/pallas_call | solution.py:525
  36.0 0.4 collective-permute-start.2
  36.4 2.1 %collective-permute-done.2 = f32[1,512]{1,0:T(1,128)S(1)} collective-permute-done((f32[1,512]{1,0:T(1,128)S(1)}, f32[1,512]{1,0:T(1,128)S(1)}, u32[]{:S(2)}, u32[]{:S(2)}) %collective-permute-start.2) | collective-permute-done | bytes 2080 | tf_op jit(solution)/shard_map/ppermute | solution.py:443
  38.6 11.0 %all-to-all-start.2 = ((bf16[16,184,256]{2,1,0:T(8,128)(2,1)}), bf16[16,184,256]{2,1,0:T(8,128)(2,1)}, u32[]{:S(2)}, u32[]{:S(2)}) async-start(bf16[16,184,256]{2,1,0:T(8,128)(2,1)} %get-tuple-element.34), calls=%async_computation.2 | async-start | bytes 3014656 | tf_op jit(solution)/shard_map/all_to_all | solution.py:552
  49.6 0.9 collective-permute-start.5
  50.4 1.2 %collective-permute-start.4 = (f32[2,512]{1,0:T(2,128)S(1)}, f32[2,512]{1,0:T(2,128)S(1)}, u32[]{:S(2)}, u32[]{:S(2)}) collective-permute-start(f32[2,512]{1,0:T(2,128)S(1)} %pad_maximum_fusion.a_ref), channel_id=1, source_target_pairs={{0,64},{16,80},{32,96},{48,112},{64,0},{80,16},{96,32},{112,48},{1... | collective-permute-start | bytes 12296 | tf_op jit(solution)/shard_map/ppermute | solution.py:447
  51.6 0.4 collective-permute-done.5.d_ref
  52.0 2.8 %collective-permute-done.4.c_ref = f32[2,512]{1,0:T(2,128)S(1)} collective-permute-done((f32[2,512]{1,0:T(2,128)S(1)}, f32[2,512]{1,0:T(2,128)S(1)}, u32[]{:S(2)}, u32[]{:S(2)}) %collective-permute-start.4) | collective-permute-done | bytes 4128 | tf_op jit(solution)/shard_map/ppermute | solution.py:447
  54.8 0.9 collective-permute-done.3.b_ref
  55.7 3.2 %detail_stats.1 = (f32[1,256]{1,0:T(1,128)S(1)}, f32[1,512]{1,0:T(1,128)S(1)}) custom-call(bf16[10,128,512]{2,1,0:T(8,128)(2,1)S(1)} %get-tuple-element.35.x_ref, f32[2,512]{1,0:T(2,128)S(1)} %pad_maximum_fusion.a_ref, f32[2,512]{1,0:T(2,128)S(1)} %collective-permute-done.3.b_ref, f32[2,512]{1,0:T(2,128)S(1)} %collective-permute-done.4.c_ref, ...), custom_call_target="tpu_custom_call" | custom-call | flops 4294967296 | tf_op jit(solution)/shard_map/detail_stats/pallas_call | solution.py:553
  59.0 0.6 collective-permute-start.8
  59.6 0.9 collective-permute-start.7
  60.5 1.3 %collective-permute-done.8 = f32[1,256]{1,0:T(1,128)S(1)} collective-permute-done((f32[1,256]{1,0:T(1,128)S(1)}, f32[1,256]{1,0:T(1,128)S(1)}, u32[]{:S(2)}, u32[]{:S(2)}) %collective-permute-start.8) | collective-permute-done | bytes 1056 | tf_op jit(solution)/shard_map/ppermute | solution.py:447
  61.8 1.9 %collective-permute-done.7 = f32[1,256]{1,0:T(1,128)S(1)} collective-permute-done((f32[1,256]{1,0:T(1,128)S(1)}, f32[1,256]{1,0:T(1,128)S(1)}, u32[]{:S(2)}, u32[]{:S(2)}) %collective-permute-start.7) | collective-permute-done | bytes 1056 | tf_op jit(solution)/shard_map/ppermute | solution.py:447
  63.7 0.4 collective-permute-done.6
  64.2 0.1 collective-permute-start.9
  64.2 3.2 %collective-permute-done.9.there_ref = f32[4,256]{1,0:T(4,128)S(1)} collective-permute-done((f32[4,256]{1,0:T(4,128)S(1)}, f32[4,256]{1,0:T(4,128)S(1)}, u32[]{:S(2)}, u32[]{:S(2)}) %collective-permute-start.9) | collective-permute-done | bytes 4128 | tf_op jit(solution)/shard_map/ppermute | solution.py:443
  67.5 0.9 summary.1
  68.4 3.4 %all-to-all-done.2 = bf16[16,184,256]{2,1,0:T(8,128)(2,1)} async-done(((bf16[16,184,256]{2,1,0:T(8,128)(2,1)}), bf16[16,184,256]{2,1,0:T(8,128)(2,1)}, u32[]{:S(2)}, u32[]{:S(2)}) %all-to-all-start.2) | async-done | bytes 1507360 | tf_op jit(solution)/shard_map/all_to_all | solution.py:552
  71.8 7.0 %all-to-all-start.3 = ((f32[16,1,768]{2,1,0:T(1,128)}), f32[16,1,768]{2,1,0:T(1,128)S(1)}, u32[]{:S(2)}, u32[]{:S(2)}) async-start(f32[16,1,768]{2,1,0:T(1,128)} %summary.1), calls=%async_computation.3 | async-start | bytes 98304 | tf_op jit(solution)/shard_map/all_to_all | solution.py:564
  78.8 1.7 %copy.19 = bf16[16,184,256]{2,0,1:T(8,128)(2,1)S(1)} copy(bf16[16,184,256]{2,1,0:T(8,128)(2,1)} %all-to-all-done.2) | data formatting | bytes 3014656 | tf_op jit(solution)/shard_map/optimization_barrier | solution.py:563
  80.5 5.6 %all-to-all-done.3.norm_ref = f32[16,1,768]{2,1,0:T(1,128)S(1)} async-done(((f32[16,1,768]{2,1,0:T(1,128)}), f32[16,1,768]{2,1,0:T(1,128)S(1)}, u32[]{:S(2)}, u32[]{:S(2)}) %all-to-all-start.3) | async-done | bytes 49184 | tf_op jit(solution)/shard_map/all_to_all | solution.py:564
  86.1 9.0 %detail.1 = bf16[16,16,32,128]{3,2,1,0:T(8,128)(2,1)} custom-call(bf16[184,16,256]{2,1,0:T(8,128)(2,1)S(1)} %bitcast.13, f32[16,1,768]{2,1,0:T(1,128)S(1)} %all-to-all-done.3.norm_ref, f32[1,256]{1,0:T(1,128)S(1)} %bitcast.21, f32[1,256]{1,0:T(1,128)S(1)} %bitcast.23, f32[1,128]{1,0:T(1,128)S(1)} %bitcast.24, f32[1,128]{1,0:T(1,128)S(1)} %bitcast.25, ...), custom_call_target="tpu_custom_call" | custom-call | flops 8589934592 | tf_op jit(solution)/shard_map/detail/pallas_call | solution.py:463
  (30 shorter events, 0.1 us)
Async XLA Ops:
  0.0 1.0 %copy-start = (bf16[1,4,128,512]{3,2,1,0:T(8,128)(2,1)S(1)}, bf16[1,4,128,512]{3,2,1,0:T(8,128)(2,1)}, u32[]{:S(2)}) copy-start(bf16[1,4,128,512]{3,2,1,0:T(8,128)(2,1)} %param.15) | copy-start | bytes 1572868
  1.3 15.5 %collective-permute-start = (bf16[2,128,512]{2,1,0:T(8,128)(2,1)S(1)}, bf16[2,128,512]{2,1,0:T(8,128)(2,1)S(1)}, u32[]{:S(2)}, u32[]{:S(2)}) collective-permute-start(bf16[2,128,512]{2,1,0:T(8,128)(2,1)S(1)} %get-tuple-element.23), channel_id=1, source_target_pairs={{0,16},{16,32},{32,48},{48,64},{64,80},{80,96},{96,112},{112,0},{1... | collective-permute-start | bytes 786440 | tf_op jit(solution)/shard_map/ppermute | solution.py:506
  3.9 13.0 %collective-permute-start.1 = (bf16[2,128,512]{2,1,0:T(8,128)(2,1)S(1)}, bf16[2,128,512]{2,1,0:T(8,128)(2,1)S(1)}, u32[]{:S(2)}, u32[]{:S(2)}) collective-permute-start(bf16[2,128,512]{2,1,0:T(8,128)(2,1)S(1)} %get-tuple-element.24), channel_id=1, source_target_pairs={{16,0},{32,16},{48,32},{64,48},{80,64},{96,80},{112,96},{0,112},{1... | collective-permute-start | bytes 786440 | tf_op jit(solution)/shard_map/ppermute | solution.py:507
  6.4 10.4 %copy-start.1 = (bf16[1,4,128,512]{3,2,1,0:T(8,128)(2,1)S(1)}, bf16[1,4,128,512]{3,2,1,0:T(8,128)(2,1)}, u32[]{:S(2)}) copy-start(bf16[1,4,128,512]{3,2,1,0:T(8,128)(2,1)} %param.15) | copy-start | bytes 1572868
  16.9 14.1 %copy-start.2 = (bf16[3,3,256,256]{3,2,1,0:T(8,128)(2,1)S(1)}, bf16[3,3,256,256]{3,2,1,0:T(8,128)(2,1)}, u32[]{:S(2)}) copy-start(bf16[3,3,256,256]{3,2,1,0:T(8,128)(2,1)} %param.21) | copy-start | bytes 3538948
  16.9 14.0 %copy-start.5 = (bf16[512,256]{1,0:T(8,128)(2,1)S(1)}, bf16[512,256]{1,0:T(8,128)(2,1)}, u32[]{:S(2)}) copy-start(bf16[512,256]{1,0:T(8,128)(2,1)} %p_ref.2) | copy-start | bytes 786436
  16.9 14.0 %copy-start.7 = (f32[256]{0:T(256)S(1)}, f32[256]{0:T(256)}, u32[]{:S(2)}) copy-start(f32[256]{0:T(256)} %param.19) | copy-start | bytes 3076
  16.9 14.0 %copy-start.8 = (f32[256]{0:T(256)S(1)}, f32[256]{0:T(256)}, u32[]{:S(2)}) copy-start(f32[256]{0:T(256)} %param.20) | copy-start | bytes 3076
  36.0 2.5 %collective-permute-start.2 = (f32[1,512]{1,0:T(1,128)S(1)}, f32[1,512]{1,0:T(1,128)S(1)}, u32[]{:S(2)}, u32[]{:S(2)}) collective-permute-start(f32[1,512]{1,0:T(1,128)S(1)} %get-tuple-element.33), channel_id=1, source_target_pairs={{0,16},{16,0},{32,48},{48,32},{64,80},{80,64},{96,112},{112,96},{1... | collective-permute-start | bytes 6152 | tf_op jit(solution)/shard_map/ppermute | solution.py:443
  38.5 17.2 %copy-start.3 = (bf16[3,3,256,128]{3,2,1,0:T(8,128)(2,1)S(1)}, bf16[3,3,256,128]{3,2,1,0:T(8,128)(2,1)}, u32[]{:S(2)}) copy-start(bf16[3,3,256,128]{3,2,1,0:T(8,128)(2,1)} %k3_ref.1) | copy-start | bytes 1769476
  38.5 17.2 %copy-start.9 = (f32[256]{0:T(256)S(1)}, f32[256]{0:T(256)}, u32[]{:S(2)}) copy-start(f32[256]{0:T(256)} %param.23) | copy-start | bytes 3076
  38.6 17.2 %copy-start.10 = (f32[256]{0:T(256)S(1)}, f32[256]{0:T(256)}, u32[]{:S(2)}) copy-start(f32[256]{0:T(256)} %param.24) | copy-start | bytes 3076
  38.6 33.2 %all-to-all-start.2 = ((bf16[16,184,256]{2,1,0:T(8,128)(2,1)}), bf16[16,184,256]{2,1,0:T(8,128)(2,1)}, u32[]{:S(2)}, u32[]{:S(2)}) async-start(bf16[16,184,256]{2,1,0:T(8,128)(2,1)} %get-tuple-element.34), calls=%async_computation.2 | async-start | bytes 3014656 | tf_op jit(solution)/shard_map/all_to_all | solution.py:552
  49.6 2.5 %collective-permute-start.5 = (f32[2,512]{1,0:T(2,128)S(1)}, f32[2,512]{1,0:T(2,128)S(1)}, u32[]{:S(2)}, u32[]{:S(2)}) collective-permute-start(f32[2,512]{1,0:T(2,128)S(1)} %pad_maximum_fusion.a_ref), channel_id=1, source_target_pairs={{0,96},{16,112},{32,0},{48,16},{64,32},{80,48},{96,64},{112,80},{1... | collective-permute-start | bytes 12296 | tf_op jit(solution)/shard_map/ppermute | solution.py:447
  50.4 4.4 %collective-permute-start.4 = (f32[2,512]{1,0:T(2,128)S(1)}, f32[2,512]{1,0:T(2,128)S(1)}, u32[]{:S(2)}, u32[]{:S(2)}) collective-permute-start(f32[2,512]{1,0:T(2,128)S(1)} %pad_maximum_fusion.a_ref), channel_id=1, source_target_pairs={{0,64},{16,80},{32,96},{48,112},{64,0},{80,16},{96,32},{112,48},{1... | collective-permute-start | bytes 12296 | tf_op jit(solution)/shard_map/ppermute | solution.py:447
  51.6 4.1 %collective-permute-start.3 = (f32[2,512]{1,0:T(2,128)S(1)}, f32[2,512]{1,0:T(2,128)S(1)}, u32[]{:S(2)}, u32[]{:S(2)}) collective-permute-start(f32[2,512]{1,0:T(2,128)S(1)} %pad_maximum_fusion.a_ref), channel_id=1, source_target_pairs={{0,32},{16,48},{32,64},{48,80},{64,96},{80,112},{96,0},{112,16},{1... | collective-permute-start | bytes 12296 | tf_op jit(solution)/shard_map/ppermute | solution.py:447
  59.0 2.9 %collective-permute-start.8 = (f32[1,256]{1,0:T(1,128)S(1)}, f32[1,256]{1,0:T(1,128)S(1)}, u32[]{:S(2)}, u32[]{:S(2)}) collective-permute-start(f32[1,256]{1,0:T(1,128)S(1)} %get-tuple-element.37), channel_id=1, source_target_pairs={{0,96},{16,112},{32,0},{48,16},{64,32},{80,48},{96,64},{112,80},{1... | collective-permute-start | bytes 3080 | tf_op jit(solution)/shard_map/ppermute | solution.py:447
  59.6 4.1 %collective-permute-start.7 = (f32[1,256]{1,0:T(1,128)S(1)}, f32[1,256]{1,0:T(1,128)S(1)}, u32[]{:S(2)}, u32[]{:S(2)}) collective-permute-start(f32[1,256]{1,0:T(1,128)S(1)} %get-tuple-element.37), channel_id=1, source_target_pairs={{0,64},{16,80},{32,96},{48,112},{64,0},{80,16},{96,32},{112,48},{1... | collective-permute-start | bytes 3080 | tf_op jit(solution)/shard_map/ppermute | solution.py:447
  60.5 3.6 %collective-permute-start.6 = (f32[1,256]{1,0:T(1,128)S(1)}, f32[1,256]{1,0:T(1,128)S(1)}, u32[]{:S(2)}, u32[]{:S(2)}) collective-permute-start(f32[1,256]{1,0:T(1,128)S(1)} %get-tuple-element.37), channel_id=1, source_target_pairs={{0,32},{16,48},{32,64},{48,80},{64,96},{80,112},{96,0},{112,16},{1... | collective-permute-start | bytes 3080 | tf_op jit(solution)/shard_map/ppermute | solution.py:447
  64.2 3.3 %collective-permute-start.9 = (f32[4,256]{1,0:T(4,128)S(1)}, f32[4,256]{1,0:T(4,128)S(1)}, u32[]{:S(2)}, u32[]{:S(2)}) collective-permute-start(f32[4,256]{1,0:T(4,128)S(1)} %pad_maximum_fusion.1.here_ref), channel_id=1, source_target_pairs={{0,16},{16,0},{32,48},{48,32},{64,80},{80,64},{96,112},{112,96},{1... | collective-permute-start | bytes 12296 | tf_op jit(solution)/shard_map/ppermute | solution.py:443
  71.8 14.3 %all-to-all-start.3 = ((f32[16,1,768]{2,1,0:T(1,128)}), f32[16,1,768]{2,1,0:T(1,128)S(1)}, u32[]{:S(2)}, u32[]{:S(2)}) async-start(f32[16,1,768]{2,1,0:T(1,128)} %summary.1), calls=%async_computation.3 | async-start | bytes 98304 | tf_op jit(solution)/shard_map/all_to_all | solution.py:564
  78.7 7.4 %copy-start.4 = (bf16[3,3,128,128]{3,2,1,0:T(8,128)(2,1)S(1)}, bf16[3,3,128,128]{3,2,1,0:T(8,128)(2,1)}, u32[]{:S(2)}) copy-start(bf16[3,3,128,128]{3,2,1,0:T(8,128)(2,1)} %k4_ref.1) | copy-start | bytes 884740
  78.8 7.3 %copy-start.6 = (bf16[256,128]{1,0:T(8,128)(2,1)S(1)}, bf16[256,128]{1,0:T(8,128)(2,1)}, u32[]{:S(2)}) copy-start(bf16[256,128]{1,0:T(8,128)(2,1)} %p_ref.3) | copy-start | bytes 196612
  78.8 7.3 %copy-start.11 = (f32[128]{0:T(128)S(1)}, f32[128]{0:T(128)}, u32[]{:S(2)}) copy-start(f32[128]{0:T(128)} %param.26) | copy-start | bytes 1540
  78.8 7.3 %copy-start.12 = (f32[128]{0:T(128)S(1)}, f32[128]{0:T(128)}, u32[]{:S(2)}) copy-start(f32[128]{0:T(128)} %param.27) | copy-start | bytes 1540

commit v6 on v5

--- a/solution.py
+++ b/solution.py
@@ -72,23 +72,20 @@
     return half + half * jnp.tanh(half)
 
 
-def block_moments(blocks):
-    sums, squares, sizes = [], [], []
-    for block in blocks:
-        n = block.shape[0]
-        if n == 0:
-            continue
-        origin = jnp.mean(block[0:16], axis=0, keepdims=True)
-        d = block - origin
-        s = jnp.sum(d, axis=0, keepdims=True)
-        q = jnp.sum(d * d, axis=0, keepdims=True)
-        sums.append(s + float(n) * origin)
-        squares.append(jnp.maximum(q - s * s / float(n), 0.0))
-        sizes.append(n)
-    total = functools.reduce(jnp.add, sums)
-    mean = total / float(sum(sizes))
-    out = functools.reduce(jnp.add, squares)
-    for s, n in zip(sums, sizes):
+def piece(block):
+    n = block.shape[0]
+    origin = jnp.mean(block[0:16], axis=0, keepdims=True)
+    d = block - origin
+    s = jnp.sum(d, axis=0, keepdims=True)
+    q = jnp.sum(d * d, axis=0, keepdims=True)
+    return n, s + float(n) * origin, jnp.maximum(q - s * s / float(n), 0.0)
+
+
+def merge(pieces):
+    total = functools.reduce(jnp.add, [s for _, s, _ in pieces])
+    mean = total / float(sum(n for n, _, _ in pieces))
+    out = functools.reduce(jnp.add, [q for _, _, q in pieces])
+    for n, s, _ in pieces:
         off = s / float(n) - mean
         out = out + float(n) * off * off
     return jnp.concatenate([total, out], axis=1)
@@ -122,7 +119,7 @@
     x = x_ref[...].astype(F32).reshape(4 * W, 512)
     head_ref[...] = x_ref[0:2]
     tail_ref[...] = x_ref[2:4]
-    publish(out_ref, block_moments([x]))
+    publish(out_ref, merge([piece(x)]))
 
 
 def pack_broad(k_ref, out_ref):
@@ -184,7 +181,7 @@
             v = active(down_ref[h - 6], mean, gain, shift) * keep_down
         an[h] = v.astype(BF16)
 
-    ready, blocks, count = 0, [], 1
+    ready, pieces, count = 0, [], 1
     for start in range(0, 6, count):
         while ready < start + count + 2:
             norm(ready)
@@ -195,17 +192,19 @@
             far = an[start + a + 1 : start + a + 1 + count].reshape(count * W, 512)
             both = jnp.concatenate([near, far], axis=1)
             for b in range(2):
-                z = [mm(both, w_ref[a, :, n * 256 : (n + 1) * 256]) for n in (2 * b, 2 * b + 1)]
+                z = mm(both, w_ref[a, :, b * 512 : (b + 1) * 512])
+                z = [z[:, 0:256], z[:, 256:512]]
                 v = last_col(z[0]) + z[1] if b == 0 else z[0] + next_col(z[1])
                 for h in range(count):
                     out_ref[2 * (start + h) + a, :, b * 256 : (b + 1) * 256] = v[h * W : (h + 1) * W].astype(BF16)
-                blocks.append(v[lo * W : hi * W])
-    publish(stat_ref, block_moments(blocks))
+                if lo < hi:
+                    pieces.append(piece(v[lo * W : hi * W]))
+    publish(stat_ref, merge(pieces))
 
 
 def broad_inner_kernel_body(
     h_ref, x_ref, up_ref, down_ref, parts_ref, gain_ref, shift_ref, w_ref, p_ref,
-    out_ref, send_hbm, stat_ref, an, odd_line, even_line, rim, send_ref, sems,
+    out_ref, stat_ref, an,
 ):
     first, last = edge_flags()
     mean, rate = moments([parts_ref], 8 * 2 * W)
@@ -228,16 +227,7 @@
     odd_w = jnp.concatenate([w[ky * 768 : ky * 768 + 512] for ky in range(3)], axis=0)
     even_side = jnp.concatenate([w[ky * 768 : ky * 768 + 256] for ky in range(3)], axis=0)
     odd_side = jnp.concatenate([w[ky * 768 + 512 : ky * 768 + 768] for ky in range(3)], axis=0)
-    copies = []
-
-    def ship(at, size):
-        rows = pl.ds(at, size)
-        copies.append(pltpu.make_async_copy(send_ref.at[:, rows], send_hbm.at[:, rows], sems.at[len(copies)]))
-        copies[-1].start()
-
-    blocks, ready, count = [], 0, 2
-    even_line[...] = jnp.zeros(even_line.shape, F32)
-    rim[...] = jnp.zeros(rim.shape, F32)
+    pieces, ready, count = [], 0, 2
     for j in range(0, 10, count):
         while ready < j + count + 2:
             norm(ready)
@@ -252,26 +242,38 @@
         extra = jnp.concatenate([skip[(i + 1) // 2 * W : ((i + 1) // 2 + 1) * W] for i in range(j, j + count)], axis=0)
         even = mm(main, even_w) + last_col(mm(odd_in, even_side)) + extra
         odd = mm(main, odd_w) + next_col(mm(even_in, odd_side)) + extra
-        before = last_col(odd)
         for i in range(count):
-            e, o, p = (v[i * W : (i + 1) * W] for v in (even, odd, before))
-            out_ref[j + i, :, 0:256] = e.astype(BF16)
-            out_ref[j + i, :, 256:512] = o.astype(BF16)
-            block = jnp.concatenate([p.reshape(COLS, 8, 256), e.reshape(COLS, 8, 256)], axis=1)
-            send_ref[:, (j + i) * 16 : (j + i + 1) * 16, :] = block.astype(BF16)
-            for n in range(2):
-                odd_line[i, n] = o[:, n * 128 : (n + 1) * 128]
-                even_line[i, n, 0:W] = e[:, n * 128 : (n + 1) * 128]
-                rim[n, pl.ds(j + i, COLS, stride=24), :] = odd_line[i, n, pl.ds(7, COLS, stride=8), :]
-                rim[n, pl.ds(10 + j + i, COLS, stride=24), :] = even_line[i, n, pl.ds(8, COLS, stride=8), :]
+            out_ref[j + i, :, 0:256] = even[i * W : (i + 1) * W].astype(BF16)
+            out_ref[j + i, :, 256:512] = odd[i * W : (i + 1) * W].astype(BF16)
         lo, hi = max(j, 1) - j, min(j + count, 9) - j
-        blocks += [even[lo * W : hi * W], odd[lo * W : hi * W]]
-        if j in (2, 6):
-            ship((j - 2) * 16, 64)
+        pieces += [piece(v[lo * W : hi * W]) for v in (even, odd)]
+    stat_ref[...] = merge(pieces)
+
+
+def arrange_kernel_body(x_ref, send_hbm, odd_line, even_line, rim, send_ref, sems):
+    copies = []
+
+    def ship(at, size):
+        rows = pl.ds(at, size)
+        copies.append(pltpu.make_async_copy(send_ref.at[:, rows], send_hbm.at[:, rows], sems.at[len(copies)]))
+        copies[-1].start()
+
+    even_line[...] = jnp.zeros(even_line.shape, F32)
+    rim[...] = jnp.zeros(rim.shape, F32)
+    for j in range(10):
+        e, o = x_ref[j, :, 0:256].astype(F32), x_ref[j, :, 256:512].astype(F32)
+        block = jnp.concatenate([last_col(o).reshape(COLS, 8, 256), e.reshape(COLS, 8, 256)], axis=1)
+        send_ref[:, j * 16 : (j + 1) * 16, :] = block.astype(BF16)
+        for n in range(2):
+            odd_line[j, n] = o[:, n * 128 : (n + 1) * 128]
+            even_line[j, n, 0:W] = e[:, n * 128 : (n + 1) * 128]
+            rim[n, pl.ds(j, COLS, stride=24), :] = odd_line[j, n, pl.ds(7, COLS, stride=8), :]
+            rim[n, pl.ds(10 + j, COLS, stride=24), :] = even_line[j, n, pl.ds(8, COLS, stride=8), :]
+        if j in (3, 7):
+            ship((j - 3) * 16, 64)
     for n in range(2):
         send_ref[:, 160:184, n * 128 : (n + 1) * 128] = rim[n].reshape(COLS, 24, 128).astype(BF16)
     ship(128, 56)
-    stat_ref[...] = block_moments(blocks)
     for copy in copies:
         copy.wait()
 
@@ -287,29 +289,33 @@
     mean, gain, shift = (tile_lanes(v, 2) for v in (mean, gain, shift))
     keep_up = jnp.where(first, 0.0, 1.0)
     keep_down = jnp.where(last, 0.0, 1.0)
-    for i in range(10):
+    def norm(i):
         v = active(x_ref[i], mean, gain, shift)
         if i < 1:
             v = v * keep_up
         elif i >= 9:
             v = v * keep_down
         an[i] = v.astype(BF16)
-    blocks = []
-    for a in range(2):
-        lhs = [an[a + t : a + t + 8].reshape(8 * W, 512) for t in range(2)]
-        main = jnp.concatenate(lhs, axis=1)
-        odd = jnp.concatenate([v[:, 256:512] for v in lhs], axis=1)
-        even = jnp.concatenate([v[:, 0:256] for v in lhs], axis=1)
-        wx = [wx_ref[a, t] for t in range(2)]
-        wz = [wz_ref[a, t] for t in range(2)]
-        middle = mm(main, jnp.concatenate([wx[0], wz[0], wx[1], wz[1]], axis=0))
-        right = mm(odd, jnp.concatenate(wx, axis=0))
-        left = mm(even, jnp.concatenate(wz, axis=0))
-        q3 = right[:, 0:128] + next_col(left[:, 0:128])
-        q0 = last_col(right[:, 128:256]) + left[:, 128:256]
-        for v in (q3, q0, middle[:, 0:128], middle[:, 128:256]):
-            blocks.append(v)
-    stat_ref[...] = block_moments(blocks)
+
+    pieces, ready, count = [], 0, 4
+    for start in range(0, 9 - count, count):
+        while ready < start + count + 2:
+            norm(ready)
+            ready += 1
+        for a in range(2):
+            lhs = [an[start + a + t : start + a + t + count].reshape(count * W, 512) for t in range(2)]
+            main = jnp.concatenate(lhs, axis=1)
+            odd = jnp.concatenate([v[:, 256:512] for v in lhs], axis=1)
+            even = jnp.concatenate([v[:, 0:256] for v in lhs], axis=1)
+            wx = [wx_ref[a, t] for t in range(2)]
+            wz = [wz_ref[a, t] for t in range(2)]
+            middle = mm(main, jnp.concatenate([wx[0], wz[0], wx[1], wz[1]], axis=0))
+            right = mm(odd, jnp.concatenate(wx, axis=0))
+            left = mm(even, jnp.concatenate(wz, axis=0))
+            q3 = right[:, 0:128] + next_col(left[:, 0:128])
+            q0 = last_col(right[:, 128:256]) + left[:, 128:256]
+            pieces += [piece(v) for v in (q3, q0, middle[:, 0:128], middle[:, 128:256])]
+    stat_ref[...] = merge(pieces)
 
 
 def summary_kernel_body(here_ref, there_ref, norm_ref, out_ref):
@@ -381,9 +387,10 @@
             ],
             axis=1,
         )
+        w = [jnp.concatenate([wx_ref[a, 0], wz_ref[a, 0], wx_ref[a, 1], wz_ref[a, 1]], axis=0) for a in range(2)]
+        both = mm(lhs, jnp.concatenate(w, axis=1))
         for a in range(2):
-            w = jnp.concatenate([wx_ref[a, 0], wz_ref[a, 0], wx_ref[a, 1], wz_ref[a, 1]], axis=0)
-            v = mm(lhs, w).astype(BF16).reshape(count * 17, 16, 256)
+            v = both[:, a * 256 : (a + 1) * 256].astype(BF16).reshape(count * 17, 16, 256)
             v = active(v, mean4, gain4, shift4)
             for n in range(count):
                 f = 2 * (i + n) + 1 - a
@@ -522,20 +529,12 @@
         flops=1 << 32,
     )(x, up, down, parts, gain, shift, packed)
     parts = swap(parts)
-    wide_out, send, part = call(
+    wide_out, part = call(
         broad_inner_kernel_body,
-        (shape(10, W, 512), shape(COLS, 184, 256), shape(1, 512, dtype=F32)),
-        [
-            pltpu.VMEM((12, W, 512), BF16),
-            pltpu.VMEM((5, 2, W, 128), F32),
-            pltpu.VMEM((5, 2, W + 8, 128), F32),
-            pltpu.VMEM((2, COLS * 24, 128), F32),
-            pltpu.VMEM((COLS, 184, 256), BF16),
-            pltpu.SemaphoreType.DMA((3,)),
-        ],
+        (shape(10, W, 512), shape(1, 512, dtype=F32)),
+        [pltpu.VMEM((12, W, 512), BF16)],
         name="broad_inner",
         flops=1 << 32,
-        outs=(VMEM, HBM, VMEM),
     )(
         wide_h,
         x,
@@ -547,6 +546,20 @@
         broad_inner_kernel.reshape(9 * 256, 256),
         broad_skip_projection,
     )
+    send = call(
+        arrange_kernel_body,
+        shape(COLS, 184, 256),
+        [
+            pltpu.VMEM((10, 2, W, 128), F32),
+            pltpu.VMEM((10, 2, W + 8, 128), F32),
+            pltpu.VMEM((2, COLS * 24, 128), F32),
+            pltpu.VMEM((COLS, 184, 256), BF16),
+            pltpu.SemaphoreType.DMA((3,)),
+        ],
+        name="arrange",
+        flops=1 << 30,
+        outs=HBM,
+    )(wide_out)
     pair = jnp.concatenate([part, across_z(part)], axis=0)
     send, pair = lax.optimization_barrier((send, pair))
     blocks = lax.all_to_all(send, "cols", 0, 0, tiled=True)

time: 95.7 us -> 94.7 us (0.990)
  waiting for transfers between devices: 22 us -> 20.8 us
    ppermute x2, waiting for transfers between devices: 5.34 us -> 4.02 us  [across_z(): return lax.ppermute(v, 'rows', [(i, i ^ 1) for i in range(ROWS)])]
    pallas_call x1 -> x2, Pallas kernels: 5.06 us -> 5.49 us  [the longest x1 4.18 us: body(): call(broad_inner_kernel_body, (shape(10, W, 512), shape(1, 512, dtype=F32...]
  transfers between devices with their start and end apart: 12 -> 12, of which waited for: 10 -> 10; matrix products, arithmetic and copies ran while one was open for 2% -> 2% of each run, Pallas kernels for 7% -> 8%
where the time goes in v6:
time: 94.7 us; the launch traced here: 94.3 us
  starting transfers between devices  27.1 us (29%)
  Pallas kernels  25.9 us (27%)
  waiting for transfers between devices  20.8 us (22%)
  blocking collectives  17.4 us (18%)
  local copies, waits for them, and re-layouts  2.84 us (3%)
    all_to_all x2, blocking collectives, swap(): return lax.all_to_all(parts, 'rows', 0, 0, tiled=True)  17.4 us
    all_to_all x1, starting transfers between devices, body(): blocks = lax.all_to_all(send, 'cols', 0, 0, tiled=True)  11 us
    pallas_call x1, Pallas kernels, detail_call(): pl.pallas_call(detail_kernel_body, in_specs=[VMEM] * len(operands), out_s...  8.98 us
    ppermute x6, waiting for transfers between devices, along_y(): lax.ppermute(v, 'rows', [(i, (i + 2 * k) % ROWS) for i in range(ROWS)])  7.69 us
    all_to_all x1, starting transfers between devices, body(): norms = lax.all_to_all(norms, 'cols', 0, 0, tiled=True)  6.85 us
    all_to_all x1, waiting for transfers between devices, body(): norms = lax.all_to_all(norms, 'cols', 0, 0, tiled=True)  5.57 us
    pallas_call x1, Pallas kernels, body(): call(broad_entry_kernel_body, (shape(12, W, 512), stat(256)), [pltpu.VMEM...  4.53 us
    pallas_call x1, Pallas kernels, body(): call(broad_inner_kernel_body, (shape(10, W, 512), shape(1, 512, dtype=F32...  4.18 us
  transfers between devices with their start and end apart: 12, of which 10 were waited for; matrix products, arithmetic and copies ran while one was open for 2% of the time, Pallas kernels for 8%

profile of v6, /device:TPU:1, one launch (start us, length us, event | category | flops | bytes accessed | tf_op | source)
XLA Modules:
  0.0 94.3 jit_solution(360941160683791710)
XLA Ops:
  0.0 1.0 %copy-done = bf16[1,4,128,512]{3,2,1,0:T(8,128)(2,1)S(1)} copy-done((bf16[1,4,128,512]{3,2,1,0:T(8,128)(2,1)S(1)}, bf16[1,4,128,512]{3,2,1,0:T(8,128)(2,1)}, u32[]{:S(2)}) %copy-start) | copy-done | bytes 524312
  1.0 0.3 coarse_stats.1
  1.3 2.5 %collective-permute-start = (bf16[2,128,512]{2,1,0:T(8,128)(2,1)S(1)}, bf16[2,128,512]{2,1,0:T(8,128)(2,1)S(1)}, u32[]{:S(2)}, u32[]{:S(2)}) collective-permute-start(bf16[2,128,512]{2,1,0:T(8,128)(2,1)S(1)} %get-tuple-element.22), channel_id=1, source_target_pairs={{0,16},{16,32},{32,48},{48,64},{64,80},{80,96},{96,112},{112,0},{1... | collective-permute-start | bytes 786440 | tf_op jit(solution)/shard_map/ppermute | solution.py:513
  3.9 2.5 %collective-permute-start.1 = (bf16[2,128,512]{2,1,0:T(8,128)(2,1)S(1)}, bf16[2,128,512]{2,1,0:T(8,128)(2,1)S(1)}, u32[]{:S(2)}, u32[]{:S(2)}) collective-permute-start(bf16[2,128,512]{2,1,0:T(8,128)(2,1)S(1)} %get-tuple-element.23), channel_id=1, source_target_pairs={{16,0},{32,16},{48,32},{64,48},{80,64},{96,80},{112,96},{0,112},{1... | collective-permute-start | bytes 786440 | tf_op jit(solution)/shard_map/ppermute | solution.py:514
  6.4 2.5 %prepare.1 = (f32[8,1,1024]{2,1,0:T(1,128)S(1)}, f32[1,512]{1,0:T(1,128)S(1)}, f32[1,512]{1,0:T(1,128)S(1)}, bf16[2,1024,1024]{2,1,0:T(8,128)(2,1)S(1)}) custom-call(f32[8,1,1024]{2,1,0:T(1,128)S(1)} %get-tuple-element.24.parts_ref, f32[1,512]{1,0:T(1,128)} %bitcast.26, f32[1,512]{1,0:T(1,128)} %bitcast.27, bf16[3,3,512,256]{3,2,1,0:T(8,128)(2,1)} %k_hbm.1), custom_call_target="tpu_custom_call" | custom-call | flops 1073741824 | tf_op jit(solution)/shard_map/prepare/pallas_call | solution.py:515
  8.9 7.9 %all_to_all.20.parts_ref = f32[8,1,1024]{2,1,0:T(1,128)S(1)} all-to-all(f32[8,1,1024]{2,1,0:T(1,128)S(1)} %get-tuple-element.25), channel_id=1, replica_groups=mesh['rows'=8,'cols'=16] {'rows'}, dimensions={0} | all-to-all | bytes 65536 | tf_op jit(solution)/shard_map/all_to_all | solution.py:446
  16.9 4.5 %broad_entry.1 = (bf16[12,128,512]{2,1,0:T(8,128)(2,1)S(1)}, f32[8,1,512]{2,1,0:T(1,128)S(1)}) custom-call(bf16[4,128,512]{2,1,0:T(8,128)(2,1)S(1)} %bitcast.15, bf16[2,128,512]{2,1,0:T(8,128)(2,1)S(1)} %collective-permute-done.up_ref, bf16[2,128,512]{2,1,0:T(8,128)(2,1)S(1)} %collective-permute-done.1.down_ref, f32[8,1,1024]{2,1,0:T(1,128)S(1)} %all_to_all.20.parts_ref, ...), custom_call_target="tpu_custom_call" | custom-call | flops 4294967296 | tf_op jit(solution)/shard_map/broad_entry/pallas_call | solution.py:524
  21.4 9.5 %all_to_all.21.parts_ref = f32[8,1,512]{2,1,0:T(1,128)S(1)} all-to-all(f32[8,1,512]{2,1,0:T(1,128)S(1)} %get-tuple-element.30), channel_id=1, replica_groups=mesh['rows'=8,'cols'=16] {'rows'}, dimensions={0} | all-to-all | bytes 32768 | tf_op jit(solution)/shard_map/all_to_all | solution.py:446
  31.0 4.2 %broad_inner.1 = (bf16[10,128,512]{2,1,0:T(8,128)(2,1)S(1)}, f32[1,512]{1,0:T(1,128)S(1)}) custom-call(bf16[12,128,512]{2,1,0:T(8,128)(2,1)S(1)} %get-tuple-element.29.h_ref, bf16[4,128,512]{2,1,0:T(8,128)(2,1)S(1)} %bitcast.16, bf16[2,128,512]{2,1,0:T(8,128)(2,1)S(1)} %collective-permute-done.up_ref, ...), custom_call_target="tpu_custom_call" | custom-call | flops 4294967296 | tf_op jit(solution)/shard_map/broad_inner/pallas_call | solution.py:532
  35.2 0.4 collective-permute-start.2
  35.6 1.3 %arrange.1 = bf16[16,184,256]{2,1,0:T(8,128)(2,1)} custom-call(bf16[10,128,512]{2,1,0:T(8,128)(2,1)S(1)} %get-tuple-element.31.x_ref), custom_call_target="tpu_custom_call" | custom-call | flops 1073741824 | tf_op jit(solution)/shard_map/arrange/pallas_call | solution.py:549
  36.9 0.8 collective-permute-done.2
  37.7 11.0 %all-to-all-start.2 = ((bf16[16,184,256]{2,1,0:T(8,128)(2,1)}), bf16[16,184,256]{2,1,0:T(8,128)(2,1)}, u32[]{:S(2)}, u32[]{:S(2)}) async-start(bf16[16,184,256]{2,1,0:T(8,128)(2,1)} %arrange.1), calls=%async_computation.2 | async-start | bytes 3014656 | tf_op jit(solution)/shard_map/all_to_all | solution.py:565
  48.7 0.9 collective-permute-start.5
  49.6 1.2 %collective-permute-start.4 = (f32[2,512]{1,0:T(2,128)S(1)}, f32[2,512]{1,0:T(2,128)S(1)}, u32[]{:S(2)}, u32[]{:S(2)}) collective-permute-start(f32[2,512]{1,0:T(2,128)S(1)} %pad_maximum_fusion.a_ref), channel_id=1, source_target_pairs={{0,64},{16,80},{32,96},{48,112},{64,0},{80,16},{96,32},{112,48},{1... | collective-permute-start | bytes 12296 | tf_op jit(solution)/shard_map/ppermute | solution.py:454
  50.8 0.4 collective-permute-done.5.d_ref
  51.2 2.8 %collective-permute-done.4.c_ref = f32[2,512]{1,0:T(2,128)S(1)} collective-permute-done((f32[2,512]{1,0:T(2,128)S(1)}, f32[2,512]{1,0:T(2,128)S(1)}, u32[]{:S(2)}, u32[]{:S(2)}) %collective-permute-start.4) | collective-permute-done | bytes 4128 | tf_op jit(solution)/shard_map/ppermute | solution.py:454
  54.0 0.9 collective-permute-done.3.b_ref
  54.9 3.1 %detail_stats.1 = (f32[1,256]{1,0:T(1,128)S(1)}, f32[1,512]{1,0:T(1,128)S(1)}) custom-call(bf16[10,128,512]{2,1,0:T(8,128)(2,1)S(1)} %get-tuple-element.31.x_ref, f32[2,512]{1,0:T(2,128)S(1)} %pad_maximum_fusion.a_ref, f32[2,512]{1,0:T(2,128)S(1)} %collective-permute-done.3.b_ref, f32[2,512]{1,0:T(2,128)S(1)} %collective-permute-done.4.c_ref, ...), custom_call_target="tpu_custom_call" | custom-call | flops 4294967296 | tf_op jit(solution)/shard_map/detail_stats/pallas_call | solution.py:566
  58.0 0.6 collective-permute-start.8
  58.7 0.9 collective-permute-start.7
  59.6 1.3 %collective-permute-done.8 = f32[1,256]{1,0:T(1,128)S(1)} collective-permute-done((f32[1,256]{1,0:T(1,128)S(1)}, f32[1,256]{1,0:T(1,128)S(1)}, u32[]{:S(2)}, u32[]{:S(2)}) %collective-permute-start.8) | collective-permute-done | bytes 1056 | tf_op jit(solution)/shard_map/ppermute | solution.py:454
  60.9 2.0 %collective-permute-done.7 = f32[1,256]{1,0:T(1,128)S(1)} collective-permute-done((f32[1,256]{1,0:T(1,128)S(1)}, f32[1,256]{1,0:T(1,128)S(1)}, u32[]{:S(2)}, u32[]{:S(2)}) %collective-permute-start.7) | collective-permute-done | bytes 1056 | tf_op jit(solution)/shard_map/ppermute | solution.py:454
  62.9 0.3 collective-permute-done.6
  63.2 0.1 collective-permute-start.9
  63.3 3.2 %collective-permute-done.9.there_ref = f32[4,256]{1,0:T(4,128)S(1)} collective-permute-done((f32[4,256]{1,0:T(4,128)S(1)}, f32[4,256]{1,0:T(4,128)S(1)}, u32[]{:S(2)}, u32[]{:S(2)}) %collective-permute-start.9) | collective-permute-done | bytes 4128 | tf_op jit(solution)/shard_map/ppermute | solution.py:450
  66.6 0.9 summary.1
  67.5 3.5 %all-to-all-done.2 = bf16[16,184,256]{2,1,0:T(8,128)(2,1)} async-done(((bf16[16,184,256]{2,1,0:T(8,128)(2,1)}), bf16[16,184,256]{2,1,0:T(8,128)(2,1)}, u32[]{:S(2)}, u32[]{:S(2)}) %all-to-all-start.2) | async-done | bytes 1507360 | tf_op jit(solution)/shard_map/all_to_all | solution.py:565
  71.0 6.8 %all-to-all-start.3 = ((f32[16,1,768]{2,1,0:T(1,128)}), f32[16,1,768]{2,1,0:T(1,128)S(1)}, u32[]{:S(2)}, u32[]{:S(2)}) async-start(f32[16,1,768]{2,1,0:T(1,128)} %summary.1), calls=%async_computation.3 | async-start | bytes 98304 | tf_op jit(solution)/shard_map/all_to_all | solution.py:577
  77.9 1.7 %copy.19 = bf16[16,184,256]{2,0,1:T(8,128)(2,1)S(1)} copy(bf16[16,184,256]{2,1,0:T(8,128)(2,1)} %all-to-all-done.2) | data formatting | bytes 3014656 | tf_op jit(solution)/shard_map/optimization_barrier | solution.py:576
  79.6 5.6 %all-to-all-done.3.norm_ref = f32[16,1,768]{2,1,0:T(1,128)S(1)} async-done(((f32[16,1,768]{2,1,0:T(1,128)}), f32[16,1,768]{2,1,0:T(1,128)S(1)}, u32[]{:S(2)}, u32[]{:S(2)}) %all-to-all-start.3) | async-done | bytes 49184 | tf_op jit(solution)/shard_map/all_to_all | solution.py:577
  85.2 9.0 %detail.1 = bf16[16,16,32,128]{3,2,1,0:T(8,128)(2,1)} custom-call(bf16[184,16,256]{2,1,0:T(8,128)(2,1)S(1)} %bitcast.13, f32[16,1,768]{2,1,0:T(1,128)S(1)} %all-to-all-done.3.norm_ref, f32[1,256]{1,0:T(1,128)S(1)} %bitcast.21, f32[1,256]{1,0:T(1,128)S(1)} %bitcast.23, f32[1,128]{1,0:T(1,128)S(1)} %bitcast.24, f32[1,128]{1,0:T(1,128)S(1)} %bitcast.25, ...), custom_call_target="tpu_custom_call" | custom-call | flops 8589934592 | tf_op jit(solution)/shard_map/detail/pallas_call | solution.py:470
  (31 shorter events, 0.1 us)
Async XLA Ops:
  0.0 1.0 %copy-start = (bf16[1,4,128,512]{3,2,1,0:T(8,128)(2,1)S(1)}, bf16[1,4,128,512]{3,2,1,0:T(8,128)(2,1)}, u32[]{:S(2)}) copy-start(bf16[1,4,128,512]{3,2,1,0:T(8,128)(2,1)} %param.15) | copy-start | bytes 1572868
  1.3 15.5 %collective-permute-start = (bf16[2,128,512]{2,1,0:T(8,128)(2,1)S(1)}, bf16[2,128,512]{2,1,0:T(8,128)(2,1)S(1)}, u32[]{:S(2)}, u32[]{:S(2)}) collective-permute-start(bf16[2,128,512]{2,1,0:T(8,128)(2,1)S(1)} %get-tuple-element.22), channel_id=1, source_target_pairs={{0,16},{16,32},{32,48},{48,64},{64,80},{80,96},{96,112},{112,0},{1... | collective-permute-start | bytes 786440 | tf_op jit(solution)/shard_map/ppermute | solution.py:513
  3.9 13.0 %collective-permute-start.1 = (bf16[2,128,512]{2,1,0:T(8,128)(2,1)S(1)}, bf16[2,128,512]{2,1,0:T(8,128)(2,1)S(1)}, u32[]{:S(2)}, u32[]{:S(2)}) collective-permute-start(bf16[2,128,512]{2,1,0:T(8,128)(2,1)S(1)} %get-tuple-element.23), channel_id=1, source_target_pairs={{16,0},{32,16},{48,32},{64,48},{80,64},{96,80},{112,96},{0,112},{1... | collective-permute-start | bytes 786440 | tf_op jit(solution)/shard_map/ppermute | solution.py:514
  6.4 10.4 %copy-start.1 = (bf16[1,4,128,512]{3,2,1,0:T(8,128)(2,1)S(1)}, bf16[1,4,128,512]{3,2,1,0:T(8,128)(2,1)}, u32[]{:S(2)}) copy-start(bf16[1,4,128,512]{3,2,1,0:T(8,128)(2,1)} %param.15) | copy-start | bytes 1572868
  16.9 14.1 %copy-start.2 = (bf16[3,3,256,256]{3,2,1,0:T(8,128)(2,1)S(1)}, bf16[3,3,256,256]{3,2,1,0:T(8,128)(2,1)}, u32[]{:S(2)}) copy-start(bf16[3,3,256,256]{3,2,1,0:T(8,128)(2,1)} %param.21) | copy-start | bytes 3538948
  16.9 14.1 %copy-start.5 = (bf16[512,256]{1,0:T(8,128)(2,1)S(1)}, bf16[512,256]{1,0:T(8,128)(2,1)}, u32[]{:S(2)}) copy-start(bf16[512,256]{1,0:T(8,128)(2,1)} %p_ref.2) | copy-start | bytes 786436
  16.9 14.1 %copy-start.7 = (f32[256]{0:T(256)S(1)}, f32[256]{0:T(256)}, u32[]{:S(2)}) copy-start(f32[256]{0:T(256)} %param.19) | copy-start | bytes 3076
  16.9 14.1 %copy-start.8 = (f32[256]{0:T(256)S(1)}, f32[256]{0:T(256)}, u32[]{:S(2)}) copy-start(f32[256]{0:T(256)} %param.20) | copy-start | bytes 3076
  35.2 2.5 %collective-permute-start.2 = (f32[1,512]{1,0:T(1,128)S(1)}, f32[1,512]{1,0:T(1,128)S(1)}, u32[]{:S(2)}, u32[]{:S(2)}) collective-permute-start(f32[1,512]{1,0:T(1,128)S(1)} %get-tuple-element.32), channel_id=1, source_target_pairs={{0,16},{16,0},{32,48},{48,32},{64,80},{80,64},{96,112},{112,96},{1... | collective-permute-start | bytes 6152 | tf_op jit(solution)/shard_map/ppermute | solution.py:450
  37.7 17.2 %copy-start.3 = (bf16[3,3,256,128]{3,2,1,0:T(8,128)(2,1)S(1)}, bf16[3,3,256,128]{3,2,1,0:T(8,128)(2,1)}, u32[]{:S(2)}) copy-start(bf16[3,3,256,128]{3,2,1,0:T(8,128)(2,1)} %k3_ref.1) | copy-start | bytes 1769476
  37.7 17.2 %copy-start.9 = (f32[256]{0:T(256)S(1)}, f32[256]{0:T(256)}, u32[]{:S(2)}) copy-start(f32[256]{0:T(256)} %param.23) | copy-start | bytes 3076
  37.7 17.2 %copy-start.10 = (f32[256]{0:T(256)S(1)}, f32[256]{0:T(256)}, u32[]{:S(2)}) copy-start(f32[256]{0:T(256)} %param.24) | copy-start | bytes 3076
  37.7 33.2 %all-to-all-start.2 = ((bf16[16,184,256]{2,1,0:T(8,128)(2,1)}), bf16[16,184,256]{2,1,0:T(8,128)(2,1)}, u32[]{:S(2)}, u32[]{:S(2)}) async-start(bf16[16,184,256]{2,1,0:T(8,128)(2,1)} %arrange.1), calls=%async_computation.2 | async-start | bytes 3014656 | tf_op jit(solution)/shard_map/all_to_all | solution.py:565
  48.7 2.5 %collective-permute-start.5 = (f32[2,512]{1,0:T(2,128)S(1)}, f32[2,512]{1,0:T(2,128)S(1)}, u32[]{:S(2)}, u32[]{:S(2)}) collective-permute-start(f32[2,512]{1,0:T(2,128)S(1)} %pad_maximum_fusion.a_ref), channel_id=1, source_target_pairs={{0,96},{16,112},{32,0},{48,16},{64,32},{80,48},{96,64},{112,80},{1... | collective-permute-start | bytes 12296 | tf_op jit(solution)/shard_map/ppermute | solution.py:454
  49.6 4.4 %collective-permute-start.4 = (f32[2,512]{1,0:T(2,128)S(1)}, f32[2,512]{1,0:T(2,128)S(1)}, u32[]{:S(2)}, u32[]{:S(2)}) collective-permute-start(f32[2,512]{1,0:T(2,128)S(1)} %pad_maximum_fusion.a_ref), channel_id=1, source_target_pairs={{0,64},{16,80},{32,96},{48,112},{64,0},{80,16},{96,32},{112,48},{1... | collective-permute-start | bytes 12296 | tf_op jit(solution)/shard_map/ppermute | solution.py:454
  50.8 4.1 %collective-permute-start.3 = (f32[2,512]{1,0:T(2,128)S(1)}, f32[2,512]{1,0:T(2,128)S(1)}, u32[]{:S(2)}, u32[]{:S(2)}) collective-permute-start(f32[2,512]{1,0:T(2,128)S(1)} %pad_maximum_fusion.a_ref), channel_id=1, source_target_pairs={{0,32},{16,48},{32,64},{48,80},{64,96},{80,112},{96,0},{112,16},{1... | collective-permute-start | bytes 12296 | tf_op jit(solution)/shard_map/ppermute | solution.py:454
  58.0 2.9 %collective-permute-start.8 = (f32[1,256]{1,0:T(1,128)S(1)}, f32[1,256]{1,0:T(1,128)S(1)}, u32[]{:S(2)}, u32[]{:S(2)}) collective-permute-start(f32[1,256]{1,0:T(1,128)S(1)} %get-tuple-element.35), channel_id=1, source_target_pairs={{0,96},{16,112},{32,0},{48,16},{64,32},{80,48},{96,64},{112,80},{1... | collective-permute-start | bytes 3080 | tf_op jit(solution)/shard_map/ppermute | solution.py:454
  58.7 4.2 %collective-permute-start.7 = (f32[1,256]{1,0:T(1,128)S(1)}, f32[1,256]{1,0:T(1,128)S(1)}, u32[]{:S(2)}, u32[]{:S(2)}) collective-permute-start(f32[1,256]{1,0:T(1,128)S(1)} %get-tuple-element.35), channel_id=1, source_target_pairs={{0,64},{16,80},{32,96},{48,112},{64,0},{80,16},{96,32},{112,48},{1... | collective-permute-start | bytes 3080 | tf_op jit(solution)/shard_map/ppermute | solution.py:454
  59.6 3.6 %collective-permute-start.6 = (f32[1,256]{1,0:T(1,128)S(1)}, f32[1,256]{1,0:T(1,128)S(1)}, u32[]{:S(2)}, u32[]{:S(2)}) collective-permute-start(f32[1,256]{1,0:T(1,128)S(1)} %get-tuple-element.35), channel_id=1, source_target_pairs={{0,32},{16,48},{32,64},{48,80},{64,96},{80,112},{96,0},{112,16},{1... | collective-permute-start | bytes 3080 | tf_op jit(solution)/shard_map/ppermute | solution.py:454
  63.2 3.3 %collective-permute-start.9 = (f32[4,256]{1,0:T(4,128)S(1)}, f32[4,256]{1,0:T(4,128)S(1)}, u32[]{:S(2)}, u32[]{:S(2)}) collective-permute-start(f32[4,256]{1,0:T(4,128)S(1)} %pad_maximum_fusion.1.here_ref), channel_id=1, source_target_pairs={{0,16},{16,0},{32,48},{48,32},{64,80},{80,64},{96,112},{112,96},{1... | collective-permute-start | bytes 12296 | tf_op jit(solution)/shard_map/ppermute | solution.py:450
  71.0 14.2 %all-to-all-start.3 = ((f32[16,1,768]{2,1,0:T(1,128)}), f32[16,1,768]{2,1,0:T(1,128)S(1)}, u32[]{:S(2)}, u32[]{:S(2)}) async-start(f32[16,1,768]{2,1,0:T(1,128)} %summary.1), calls=%async_computation.3 | async-start | bytes 98304 | tf_op jit(solution)/shard_map/all_to_all | solution.py:577
  77.8 7.4 %copy-start.4 = (bf16[3,3,128,128]{3,2,1,0:T(8,128)(2,1)S(1)}, bf16[3,3,128,128]{3,2,1,0:T(8,128)(2,1)}, u32[]{:S(2)}) copy-start(bf16[3,3,128,128]{3,2,1,0:T(8,128)(2,1)} %k4_ref.1) | copy-start | bytes 884740
  77.8 7.3 %copy-start.6 = (bf16[256,128]{1,0:T(8,128)(2,1)S(1)}, bf16[256,128]{1,0:T(8,128)(2,1)}, u32[]{:S(2)}) copy-start(bf16[256,128]{1,0:T(8,128)(2,1)} %p_ref.3) | copy-start | bytes 196612
  77.8 7.3 %copy-start.11 = (f32[128]{0:T(128)S(1)}, f32[128]{0:T(128)}, u32[]{:S(2)}) copy-start(f32[128]{0:T(128)} %param.26) | copy-start | bytes 1540
  77.8 7.3 %copy-start.12 = (f32[128]{0:T(128)S(1)}, f32[128]{0:T(128)}, u32[]{:S(2)}) copy-start(f32[128]{0:T(128)} %param.27) | copy-start | bytes 1540

commit v7 on v6

--- a/solution.py
+++ b/solution.py
@@ -267,13 +267,13 @@
         for n in range(2):
             odd_line[j, n] = o[:, n * 128 : (n + 1) * 128]
             even_line[j, n, 0:W] = e[:, n * 128 : (n + 1) * 128]
-            rim[n, pl.ds(j, COLS, stride=24), :] = odd_line[j, n, pl.ds(7, COLS, stride=8), :]
-            rim[n, pl.ds(10 + j, COLS, stride=24), :] = even_line[j, n, pl.ds(8, COLS, stride=8), :]
+            rim[n, pl.ds(j, COLS, stride=32), :] = odd_line[j, n, pl.ds(7, COLS, stride=8), :]
+            rim[n, pl.ds(10 + j, COLS, stride=32), :] = even_line[j, n, pl.ds(8, COLS, stride=8), :]
         if j in (3, 7):
             ship((j - 3) * 16, 64)
     for n in range(2):
-        send_ref[:, 160:184, n * 128 : (n + 1) * 128] = rim[n].reshape(COLS, 24, 128).astype(BF16)
-    ship(128, 56)
+        send_ref[:, 160:192, n * 128 : (n + 1) * 128] = rim[n].reshape(COLS, 32, 128).astype(BF16)
+    ship(128, 64)
     for copy in copies:
         copy.wait()
 
@@ -548,12 +548,12 @@
     )
     send = call(
         arrange_kernel_body,
-        shape(COLS, 184, 256),
+        shape(COLS, 192, 256),
         [
             pltpu.VMEM((10, 2, W, 128), F32),
             pltpu.VMEM((10, 2, W + 8, 128), F32),
-            pltpu.VMEM((2, COLS * 24, 128), F32),
-            pltpu.VMEM((COLS, 184, 256), BF16),
+            pltpu.VMEM((2, COLS * 32, 128), F32),
+            pltpu.VMEM((COLS, 192, 256), BF16),
             pltpu.SemaphoreType.DMA((3,)),
         ],
         name="arrange",

time: 94.7 us -> 94.7 us (level)
    all_to_all x1, waiting for transfers between devices: 3.47 us -> 4.49 us  [body(): blocks = lax.all_to_all(send, 'cols', 0, 0, tiled=True)]
  transfers between devices with their start and end apart: 12 -> 12, of which waited for: 10 -> 10; matrix products, arithmetic and copies ran while one was open for 2% -> 2% of each run, Pallas kernels for 8% -> 9%
where the time goes in v7:
time: 94.7 us; the launch traced here: 94.3 us
  starting transfers between devices  26.4 us (28%)
  Pallas kernels  26.1 us (28%)
  waiting for transfers between devices  20.7 us (22%)
  blocking collectives  17.4 us (18%)
  local copies, waits for them, and re-layouts  3.44 us (4%)
    all_to_all x2, blocking collectives, swap(): return lax.all_to_all(parts, 'rows', 0, 0, tiled=True)  17.4 us
    all_to_all x1, starting transfers between devices, body(): blocks = lax.all_to_all(send, 'cols', 0, 0, tiled=True)  11 us
    pallas_call x1, Pallas kernels, detail_call(): pl.pallas_call(detail_kernel_body, in_specs=[VMEM] * len(operands), out_s...  8.97 us
    ppermute x6, waiting for transfers between devices, along_y(): lax.ppermute(v, 'rows', [(i, (i + 2 * k) % ROWS) for i in range(ROWS)])  7.73 us
    all_to_all x1, starting transfers between devices, body(): norms = lax.all_to_all(norms, 'cols', 0, 0, tiled=True)  6.15 us
    all_to_all x1, waiting for transfers between devices, body(): norms = lax.all_to_all(norms, 'cols', 0, 0, tiled=True)  4.98 us
    pallas_call x1, Pallas kernels, body(): call(broad_entry_kernel_body, (shape(12, W, 512), stat(256)), [pltpu.VMEM...  4.53 us
    all_to_all x1, waiting for transfers between devices, body(): blocks = lax.all_to_all(send, 'cols', 0, 0, tiled=True)  4.49 us
  transfers between devices with their start and end apart: 12, of which 10 were waited for; matrix products, arithmetic and copies ran while one was open for 2% of the time, Pallas kernels for 9%

profile of v7, /device:TPU:1, one launch (start us, length us, event | category | flops | bytes accessed | tf_op | source)
XLA Modules:
  0.0 94.3 jit_solution(7157998461997378977)
XLA Ops:
  0.0 1.0 %copy-done = bf16[1,4,128,512]{3,2,1,0:T(8,128)(2,1)S(1)} copy-done((bf16[1,4,128,512]{3,2,1,0:T(8,128)(2,1)S(1)}, bf16[1,4,128,512]{3,2,1,0:T(8,128)(2,1)}, u32[]{:S(2)}) %copy-start) | copy-done | bytes 524312
  1.0 0.3 coarse_stats.1
  1.3 2.5 %collective-permute-start = (bf16[2,128,512]{2,1,0:T(8,128)(2,1)S(1)}, bf16[2,128,512]{2,1,0:T(8,128)(2,1)S(1)}, u32[]{:S(2)}, u32[]{:S(2)}) collective-permute-start(bf16[2,128,512]{2,1,0:T(8,128)(2,1)S(1)} %get-tuple-element.22), channel_id=1, source_target_pairs={{0,16},{16,32},{32,48},{48,64},{64,80},{80,96},{96,112},{112,0},{1... | collective-permute-start | bytes 786440 | tf_op jit(solution)/shard_map/ppermute | solution.py:513
  3.9 2.5 %collective-permute-start.1 = (bf16[2,128,512]{2,1,0:T(8,128)(2,1)S(1)}, bf16[2,128,512]{2,1,0:T(8,128)(2,1)S(1)}, u32[]{:S(2)}, u32[]{:S(2)}) collective-permute-start(bf16[2,128,512]{2,1,0:T(8,128)(2,1)S(1)} %get-tuple-element.23), channel_id=1, source_target_pairs={{16,0},{32,16},{48,32},{64,48},{80,64},{96,80},{112,96},{0,112},{1... | collective-permute-start | bytes 786440 | tf_op jit(solution)/shard_map/ppermute | solution.py:514
  6.4 2.5 %prepare.1 = (f32[8,1,1024]{2,1,0:T(1,128)S(1)}, f32[1,512]{1,0:T(1,128)S(1)}, f32[1,512]{1,0:T(1,128)S(1)}, bf16[2,1024,1024]{2,1,0:T(8,128)(2,1)S(1)}) custom-call(f32[8,1,1024]{2,1,0:T(1,128)S(1)} %get-tuple-element.24.parts_ref, f32[1,512]{1,0:T(1,128)} %bitcast.26, f32[1,512]{1,0:T(1,128)} %bitcast.27, bf16[3,3,512,256]{3,2,1,0:T(8,128)(2,1)} %k_hbm.1), custom_call_target="tpu_custom_call" | custom-call | flops 1073741824 | tf_op jit(solution)/shard_map/prepare/pallas_call | solution.py:515
  8.9 7.9 %all_to_all.20.parts_ref = f32[8,1,1024]{2,1,0:T(1,128)S(1)} all-to-all(f32[8,1,1024]{2,1,0:T(1,128)S(1)} %get-tuple-element.25), channel_id=1, replica_groups=mesh['rows'=8,'cols'=16] {'rows'}, dimensions={0} | all-to-all | bytes 65536 | tf_op jit(solution)/shard_map/all_to_all | solution.py:446
  16.9 4.5 %broad_entry.1 = (bf16[12,128,512]{2,1,0:T(8,128)(2,1)S(1)}, f32[8,1,512]{2,1,0:T(1,128)S(1)}) custom-call(bf16[4,128,512]{2,1,0:T(8,128)(2,1)S(1)} %bitcast.15, bf16[2,128,512]{2,1,0:T(8,128)(2,1)S(1)} %collective-permute-done.up_ref, bf16[2,128,512]{2,1,0:T(8,128)(2,1)S(1)} %collective-permute-done.1.down_ref, f32[8,1,1024]{2,1,0:T(1,128)S(1)} %all_to_all.20.parts_ref, ...), custom_call_target="tpu_custom_call" | custom-call | flops 4294967296 | tf_op jit(solution)/shard_map/broad_entry/pallas_call | solution.py:524
  21.4 9.5 %all_to_all.21.parts_ref = f32[8,1,512]{2,1,0:T(1,128)S(1)} all-to-all(f32[8,1,512]{2,1,0:T(1,128)S(1)} %get-tuple-element.30), channel_id=1, replica_groups=mesh['rows'=8,'cols'=16] {'rows'}, dimensions={0} | all-to-all | bytes 32768 | tf_op jit(solution)/shard_map/all_to_all | solution.py:446
  31.0 4.2 %broad_inner.1 = (bf16[10,128,512]{2,1,0:T(8,128)(2,1)S(1)}, f32[1,512]{1,0:T(1,128)S(1)}) custom-call(bf16[12,128,512]{2,1,0:T(8,128)(2,1)S(1)} %get-tuple-element.29.h_ref, bf16[4,128,512]{2,1,0:T(8,128)(2,1)S(1)} %bitcast.16, bf16[2,128,512]{2,1,0:T(8,128)(2,1)S(1)} %collective-permute-done.up_ref, ...), custom_call_target="tpu_custom_call" | custom-call | flops 4294967296 | tf_op jit(solution)/shard_map/broad_inner/pallas_call | solution.py:532
  35.2 0.4 collective-permute-start.2
  35.6 1.5 %arrange.1 = bf16[16,192,256]{2,1,0:T(8,128)(2,1)} custom-call(bf16[10,128,512]{2,1,0:T(8,128)(2,1)S(1)} %get-tuple-element.31.x_ref), custom_call_target="tpu_custom_call" | custom-call | flops 1073741824 | tf_op jit(solution)/shard_map/arrange/pallas_call | solution.py:549
  37.1 0.6 collective-permute-done.2
  37.7 11.0 %all-to-all-start.2 = ((bf16[16,192,256]{2,1,0:T(8,128)(2,1)}), bf16[16,192,256]{2,1,0:T(8,128)(2,1)}, u32[]{:S(2)}, u32[]{:S(2)}) async-start(bf16[16,192,256]{2,1,0:T(8,128)(2,1)} %arrange.1), calls=%async_computation.2 | async-start | bytes 3145728 | tf_op jit(solution)/shard_map/all_to_all | solution.py:565
  48.7 0.9 collective-permute-start.5
  49.6 1.2 %collective-permute-start.4 = (f32[2,512]{1,0:T(2,128)S(1)}, f32[2,512]{1,0:T(2,128)S(1)}, u32[]{:S(2)}, u32[]{:S(2)}) collective-permute-start(f32[2,512]{1,0:T(2,128)S(1)} %pad_maximum_fusion.a_ref), channel_id=1, source_target_pairs={{0,64},{16,80},{32,96},{48,112},{64,0},{80,16},{96,32},{112,48},{1... | collective-permute-start | bytes 12296 | tf_op jit(solution)/shard_map/ppermute | solution.py:454
  50.8 0.4 collective-permute-done.5.d_ref
  51.2 2.8 %collective-permute-done.4.c_ref = f32[2,512]{1,0:T(2,128)S(1)} collective-permute-done((f32[2,512]{1,0:T(2,128)S(1)}, f32[2,512]{1,0:T(2,128)S(1)}, u32[]{:S(2)}, u32[]{:S(2)}) %collective-permute-start.4) | collective-permute-done | bytes 4128 | tf_op jit(solution)/shard_map/ppermute | solution.py:454
  54.0 0.9 collective-permute-done.3.b_ref
  54.9 3.1 %detail_stats.1 = (f32[1,256]{1,0:T(1,128)S(1)}, f32[1,512]{1,0:T(1,128)S(1)}) custom-call(bf16[10,128,512]{2,1,0:T(8,128)(2,1)S(1)} %get-tuple-element.31.x_ref, f32[2,512]{1,0:T(2,128)S(1)} %pad_maximum_fusion.a_ref, f32[2,512]{1,0:T(2,128)S(1)} %collective-permute-done.3.b_ref, f32[2,512]{1,0:T(2,128)S(1)} %collective-permute-done.4.c_ref, ...), custom_call_target="tpu_custom_call" | custom-call | flops 4294967296 | tf_op jit(solution)/shard_map/detail_stats/pallas_call | solution.py:566
  58.0 0.6 collective-permute-start.8
  58.7 0.9 collective-permute-start.7
  59.6 1.3 %collective-permute-done.8 = f32[1,256]{1,0:T(1,128)S(1)} collective-permute-done((f32[1,256]{1,0:T(1,128)S(1)}, f32[1,256]{1,0:T(1,128)S(1)}, u32[]{:S(2)}, u32[]{:S(2)}) %collective-permute-start.8) | collective-permute-done | bytes 1056 | tf_op jit(solution)/shard_map/ppermute | solution.py:454
  60.9 2.1 %collective-permute-done.7 = f32[1,256]{1,0:T(1,128)S(1)} collective-permute-done((f32[1,256]{1,0:T(1,128)S(1)}, f32[1,256]{1,0:T(1,128)S(1)}, u32[]{:S(2)}, u32[]{:S(2)}) %collective-permute-start.7) | collective-permute-done | bytes 1056 | tf_op jit(solution)/shard_map/ppermute | solution.py:454
  63.0 0.3 collective-permute-done.6
  63.2 0.1 collective-permute-start.9
  63.3 2.9 %collective-permute-done.9.there_ref = f32[4,256]{1,0:T(4,128)S(1)} collective-permute-done((f32[4,256]{1,0:T(4,128)S(1)}, f32[4,256]{1,0:T(4,128)S(1)}, u32[]{:S(2)}, u32[]{:S(2)}) %collective-permute-start.9) | collective-permute-done | bytes 4128 | tf_op jit(solution)/shard_map/ppermute | solution.py:450
  66.2 0.9 summary.1
  67.2 4.5 %all-to-all-done.2 = bf16[16,192,256]{2,1,0:T(8,128)(2,1)} async-done(((bf16[16,192,256]{2,1,0:T(8,128)(2,1)}), bf16[16,192,256]{2,1,0:T(8,128)(2,1)}, u32[]{:S(2)}, u32[]{:S(2)}) %all-to-all-start.2) | async-done | bytes 1572896 | tf_op jit(solution)/shard_map/all_to_all | solution.py:565
  71.7 6.1 %all-to-all-start.3 = ((f32[16,1,768]{2,1,0:T(1,128)}), f32[16,1,768]{2,1,0:T(1,128)S(1)}, u32[]{:S(2)}, u32[]{:S(2)}) async-start(f32[16,1,768]{2,1,0:T(1,128)} %summary.1), calls=%async_computation.3 | async-start | bytes 98304 | tf_op jit(solution)/shard_map/all_to_all | solution.py:577
  77.9 2.3 %copy.19 = bf16[16,192,256]{2,0,1:T(8,128)(2,1)S(1)} copy(bf16[16,192,256]{2,1,0:T(8,128)(2,1)} %all-to-all-done.2) | data formatting | bytes 3145728 | tf_op jit(solution)/shard_map/optimization_barrier | solution.py:576
  80.2 5.0 %all-to-all-done.3.norm_ref = f32[16,1,768]{2,1,0:T(1,128)S(1)} async-done(((f32[16,1,768]{2,1,0:T(1,128)}), f32[16,1,768]{2,1,0:T(1,128)S(1)}, u32[]{:S(2)}, u32[]{:S(2)}) %all-to-all-start.3) | async-done | bytes 49184 | tf_op jit(solution)/shard_map/all_to_all | solution.py:577
  85.2 9.0 %detail.1 = bf16[16,16,32,128]{3,2,1,0:T(8,128)(2,1)} custom-call(bf16[192,16,256]{2,1,0:T(8,128)(2,1)S(1)} %bitcast.13, f32[16,1,768]{2,1,0:T(1,128)S(1)} %all-to-all-done.3.norm_ref, f32[1,256]{1,0:T(1,128)S(1)} %bitcast.21, f32[1,256]{1,0:T(1,128)S(1)} %bitcast.23, f32[1,128]{1,0:T(1,128)S(1)} %bitcast.24, f32[1,128]{1,0:T(1,128)S(1)} %bitcast.25, ...), custom_call_target="tpu_custom_call" | custom-call | flops 8589934592 | tf_op jit(solution)/shard_map/detail/pallas_call | solution.py:470
  (31 shorter events, 0.1 us)
Async XLA Ops:
  0.0 1.0 %copy-start = (bf16[1,4,128,512]{3,2,1,0:T(8,128)(2,1)S(1)}, bf16[1,4,128,512]{3,2,1,0:T(8,128)(2,1)}, u32[]{:S(2)}) copy-start(bf16[1,4,128,512]{3,2,1,0:T(8,128)(2,1)} %param.15) | copy-start | bytes 1572868
  1.3 15.5 %collective-permute-start = (bf16[2,128,512]{2,1,0:T(8,128)(2,1)S(1)}, bf16[2,128,512]{2,1,0:T(8,128)(2,1)S(1)}, u32[]{:S(2)}, u32[]{:S(2)}) collective-permute-start(bf16[2,128,512]{2,1,0:T(8,128)(2,1)S(1)} %get-tuple-element.22), channel_id=1, source_target_pairs={{0,16},{16,32},{32,48},{48,64},{64,80},{80,96},{96,112},{112,0},{1... | collective-permute-start | bytes 786440 | tf_op jit(solution)/shard_map/ppermute | solution.py:513
  3.9 13.0 %collective-permute-start.1 = (bf16[2,128,512]{2,1,0:T(8,128)(2,1)S(1)}, bf16[2,128,512]{2,1,0:T(8,128)(2,1)S(1)}, u32[]{:S(2)}, u32[]{:S(2)}) collective-permute-start(bf16[2,128,512]{2,1,0:T(8,128)(2,1)S(1)} %get-tuple-element.23), channel_id=1, source_target_pairs={{16,0},{32,16},{48,32},{64,48},{80,64},{96,80},{112,96},{0,112},{1... | collective-permute-start | bytes 786440 | tf_op jit(solution)/shard_map/ppermute | solution.py:514
  6.4 10.4 %copy-start.1 = (bf16[1,4,128,512]{3,2,1,0:T(8,128)(2,1)S(1)}, bf16[1,4,128,512]{3,2,1,0:T(8,128)(2,1)}, u32[]{:S(2)}) copy-start(bf16[1,4,128,512]{3,2,1,0:T(8,128)(2,1)} %param.15) | copy-start | bytes 1572868
  16.9 14.1 %copy-start.2 = (bf16[3,3,256,256]{3,2,1,0:T(8,128)(2,1)S(1)}, bf16[3,3,256,256]{3,2,1,0:T(8,128)(2,1)}, u32[]{:S(2)}) copy-start(bf16[3,3,256,256]{3,2,1,0:T(8,128)(2,1)} %param.21) | copy-start | bytes 3538948
  16.9 14.1 %copy-start.5 = (bf16[512,256]{1,0:T(8,128)(2,1)S(1)}, bf16[512,256]{1,0:T(8,128)(2,1)}, u32[]{:S(2)}) copy-start(bf16[512,256]{1,0:T(8,128)(2,1)} %p_ref.2) | copy-start | bytes 786436
  16.9 14.1 %copy-start.7 = (f32[256]{0:T(256)S(1)}, f32[256]{0:T(256)}, u32[]{:S(2)}) copy-start(f32[256]{0:T(256)} %param.19) | copy-start | bytes 3076
  16.9 14.1 %copy-start.8 = (f32[256]{0:T(256)S(1)}, f32[256]{0:T(256)}, u32[]{:S(2)}) copy-start(f32[256]{0:T(256)} %param.20) | copy-start | bytes 3076
  35.2 2.5 %collective-permute-start.2 = (f32[1,512]{1,0:T(1,128)S(1)}, f32[1,512]{1,0:T(1,128)S(1)}, u32[]{:S(2)}, u32[]{:S(2)}) collective-permute-start(f32[1,512]{1,0:T(1,128)S(1)} %get-tuple-element.32), channel_id=1, source_target_pairs={{0,16},{16,0},{32,48},{48,32},{64,80},{80,64},{96,112},{112,96},{1... | collective-permute-start | bytes 6152 | tf_op jit(solution)/shard_map/ppermute | solution.py:450
  37.7 17.2 %copy-start.3 = (bf16[3,3,256,128]{3,2,1,0:T(8,128)(2,1)S(1)}, bf16[3,3,256,128]{3,2,1,0:T(8,128)(2,1)}, u32[]{:S(2)}) copy-start(bf16[3,3,256,128]{3,2,1,0:T(8,128)(2,1)} %k3_ref.1) | copy-start | bytes 1769476
  37.7 17.2 %copy-start.9 = (f32[256]{0:T(256)S(1)}, f32[256]{0:T(256)}, u32[]{:S(2)}) copy-start(f32[256]{0:T(256)} %param.23) | copy-start | bytes 3076
  37.7 17.2 %copy-start.10 = (f32[256]{0:T(256)S(1)}, f32[256]{0:T(256)}, u32[]{:S(2)}) copy-start(f32[256]{0:T(256)} %param.24) | copy-start | bytes 3076
  37.7 33.9 %all-to-all-start.2 = ((bf16[16,192,256]{2,1,0:T(8,128)(2,1)}), bf16[16,192,256]{2,1,0:T(8,128)(2,1)}, u32[]{:S(2)}, u32[]{:S(2)}) async-start(bf16[16,192,256]{2,1,0:T(8,128)(2,1)} %arrange.1), calls=%async_computation.2 | async-start | bytes 3145728 | tf_op jit(solution)/shard_map/all_to_all | solution.py:565
  48.7 2.5 %collective-permute-start.5 = (f32[2,512]{1,0:T(2,128)S(1)}, f32[2,512]{1,0:T(2,128)S(1)}, u32[]{:S(2)}, u32[]{:S(2)}) collective-permute-start(f32[2,512]{1,0:T(2,128)S(1)} %pad_maximum_fusion.a_ref), channel_id=1, source_target_pairs={{0,96},{16,112},{32,0},{48,16},{64,32},{80,48},{96,64},{112,80},{1... | collective-permute-start | bytes 12296 | tf_op jit(solution)/shard_map/ppermute | solution.py:454
  49.6 4.4 %collective-permute-start.4 = (f32[2,512]{1,0:T(2,128)S(1)}, f32[2,512]{1,0:T(2,128)S(1)}, u32[]{:S(2)}, u32[]{:S(2)}) collective-permute-start(f32[2,512]{1,0:T(2,128)S(1)} %pad_maximum_fusion.a_ref), channel_id=1, source_target_pairs={{0,64},{16,80},{32,96},{48,112},{64,0},{80,16},{96,32},{112,48},{1... | collective-permute-start | bytes 12296 | tf_op jit(solution)/shard_map/ppermute | solution.py:454
  50.8 4.1 %collective-permute-start.3 = (f32[2,512]{1,0:T(2,128)S(1)}, f32[2,512]{1,0:T(2,128)S(1)}, u32[]{:S(2)}, u32[]{:S(2)}) collective-permute-start(f32[2,512]{1,0:T(2,128)S(1)} %pad_maximum_fusion.a_ref), channel_id=1, source_target_pairs={{0,32},{16,48},{32,64},{48,80},{64,96},{80,112},{96,0},{112,16},{1... | collective-permute-start | bytes 12296 | tf_op jit(solution)/shard_map/ppermute | solution.py:454
  58.0 2.9 %collective-permute-start.8 = (f32[1,256]{1,0:T(1,128)S(1)}, f32[1,256]{1,0:T(1,128)S(1)}, u32[]{:S(2)}, u32[]{:S(2)}) collective-permute-start(f32[1,256]{1,0:T(1,128)S(1)} %get-tuple-element.35), channel_id=1, source_target_pairs={{0,96},{16,112},{32,0},{48,16},{64,32},{80,48},{96,64},{112,80},{1... | collective-permute-start | bytes 3080 | tf_op jit(solution)/shard_map/ppermute | solution.py:454
  58.7 4.3 %collective-permute-start.7 = (f32[1,256]{1,0:T(1,128)S(1)}, f32[1,256]{1,0:T(1,128)S(1)}, u32[]{:S(2)}, u32[]{:S(2)}) collective-permute-start(f32[1,256]{1,0:T(1,128)S(1)} %get-tuple-element.35), channel_id=1, source_target_pairs={{0,64},{16,80},{32,96},{48,112},{64,0},{80,16},{96,32},{112,48},{1... | collective-permute-start | bytes 3080 | tf_op jit(solution)/shard_map/ppermute | solution.py:454
  59.6 3.7 %collective-permute-start.6 = (f32[1,256]{1,0:T(1,128)S(1)}, f32[1,256]{1,0:T(1,128)S(1)}, u32[]{:S(2)}, u32[]{:S(2)}) collective-permute-start(f32[1,256]{1,0:T(1,128)S(1)} %get-tuple-element.35), channel_id=1, source_target_pairs={{0,32},{16,48},{32,64},{48,80},{64,96},{80,112},{96,0},{112,16},{1... | collective-permute-start | bytes 3080 | tf_op jit(solution)/shard_map/ppermute | solution.py:454
  63.2 3.0 %collective-permute-start.9 = (f32[4,256]{1,0:T(4,128)S(1)}, f32[4,256]{1,0:T(4,128)S(1)}, u32[]{:S(2)}, u32[]{:S(2)}) collective-permute-start(f32[4,256]{1,0:T(4,128)S(1)} %pad_maximum_fusion.1.here_ref), channel_id=1, source_target_pairs={{0,16},{16,0},{32,48},{48,32},{64,80},{80,64},{96,112},{112,96},{1... | collective-permute-start | bytes 12296 | tf_op jit(solution)/shard_map/ppermute | solution.py:450
  71.7 13.5 %all-to-all-start.3 = ((f32[16,1,768]{2,1,0:T(1,128)}), f32[16,1,768]{2,1,0:T(1,128)S(1)}, u32[]{:S(2)}, u32[]{:S(2)}) async-start(f32[16,1,768]{2,1,0:T(1,128)} %summary.1), calls=%async_computation.3 | async-start | bytes 98304 | tf_op jit(solution)/shard_map/all_to_all | solution.py:577
  77.8 7.4 %copy-start.4 = (bf16[3,3,128,128]{3,2,1,0:T(8,128)(2,1)S(1)}, bf16[3,3,128,128]{3,2,1,0:T(8,128)(2,1)}, u32[]{:S(2)}) copy-start(bf16[3,3,128,128]{3,2,1,0:T(8,128)(2,1)} %k4_ref.1) | copy-start | bytes 884740
  77.8 7.3 %copy-start.6 = (bf16[256,128]{1,0:T(8,128)(2,1)S(1)}, bf16[256,128]{1,0:T(8,128)(2,1)}, u32[]{:S(2)}) copy-start(bf16[256,128]{1,0:T(8,128)(2,1)} %p_ref.3) | copy-start | bytes 196612
  77.8 7.3 %copy-start.11 = (f32[128]{0:T(128)S(1)}, f32[128]{0:T(128)}, u32[]{:S(2)}) copy-start(f32[128]{0:T(128)} %param.26) | copy-start | bytes 1540
  77.8 7.3 %copy-start.12 = (f32[128]{0:T(128)S(1)}, f32[128]{0:T(128)}, u32[]{:S(2)}) copy-start(f32[128]{0:T(128)} %param.27) | copy-start | bytes 1540
